TPU v7x, 32 devices: a whole 2x2x4 slice. The times are simulated.
32 devices in a mesh: code: 2 (over core), aa: 8 (over z, y), ba: 2 (over x).
Axes of the slice: x: 2, y: 2, z: 4, core: 2. Of those that a mesh axis runs over, the one named last changes fastest.
Arguments:
- states: float32 [2, 64, 65536], P('code', 'ba', 'aa'), may hold values from -4 to 4, as said below
- coupled: float32 [2, 3, 64, 65536], P('code', None, 'ba', 'aa'), may hold values from -2 to 2, as said below
- facies: int32 [2, 64, 65536], P('code', 'ba', 'aa'), may hold values from 0 to 5, as said below
- injectors: int32 [2, 64, 65536], P('code', 'ba', 'aa'), may hold values from 0 to 1, as said below
- producers: int32 [2, 64, 65536], P('code', 'ba', 'aa'), may hold values from 0 to 1, as said below
- perm_table: float32 [6], replicated, may hold values from 0.1 to 10
- cond_table: float32 [6], replicated, may hold values from 0.1 to 1
Outputs:
- stepped_states: float32 [2, 64, 65536], P('code', 'ba', 'aa')
- new_coupled: float32 [2, 3, 64, 65536], P('code', None, 'ba', 'aa')
Inputs may be any that keep to these rules, and one draw needn't show every extreme that they name: Slice 1 of states lies in [0, 1]. Slice 0 of coupled lies in [0.2, 1]. `facies`: both slices hold the same class map of the grid, each in its group's layout. `injectors`: 0 or 1; both slices mark the same cells; no cell is both an injector and a producer. `producers`: 0 or 1; both slices mark the same cells; no cell is both an injector and a producer.
All inputs are finite; a program needn't handle non-finite values.
Results may differ from a plain program's by a relative error of at most 0.00002.
Values sent between devices are 32-bit elements; how exact they have to be, the bound alone decides.
No kernel may reach another device: no remote copies, remote signals or barrier semaphores. Data moves between devices by JAX's collectives and lax.ppermute only.
A program may use at most 128 MiB of HBM per device.

v0:
```python
import jax
import jax.numpy as jnp
from jax import lax
from jax.sharding import PartitionSpec as P

W = 64
NF = 6
ITERS = 4


STORAGE = 0.5
LOWER_BOUND = 0.05
INJECTION = 2.0
PRODUCT_INDEX = 1.0
WELL_PRESSURE = -1.0
FLOW_RATE = 1.0
CHILLED_INFLOW = 0.1
TIME_STEP = 0.05


def extended(block, sides, width):
    for axis, dim in sides:
        count = lax.axis_size(axis)
        forward = [(i, i + 1) for i in range(count - 1)]
        backward = [(target, source) for source, target in forward]
        low = lax.ppermute(
            lax.slice_in_dim(block, block.shape[dim] - width, None, axis=dim), axis, forward
        )
        high = lax.ppermute(lax.slice_in_dim(block, 0, width, axis=dim), axis, backward)
        block = jnp.concatenate([low, block, high], axis=dim)
    return block


def from_partner(value, axis, stride):
    mask = 2**stride
    pairs = [(source, source ^ mask) for source in range(lax.axis_size(axis))]
    return lax.ppermute(value, axis, pairs)


def brine_flowability(matrix_heat_level):
    return 0.2 + 0.8 * jax.nn.sigmoid(6.0 * (matrix_heat_level - 0.5))


def harmonic(left_val, eastern_neighbor_number, face_mask):
    return (
        face_mask
        * 2.0
        * left_val
        * eastern_neighbor_number
        / (left_val + eastern_neighbor_number + 1.0 - face_mask)
    )


def accumulate(terms):
    result = terms[0]
    for term in terms[1:]:
        result = result + term
    return result


def sweep_weights():
    centre_val = (2.0 + LOWER_BOUND) / 2.0
    half_width = (2.0 - LOWER_BOUND) / 2.0
    quotient_number = centre_val / half_width
    rho_old = 1.0 / quotient_number
    chebyshev = [(1.0 / centre_val, 0.0)]
    for index_k in range(1, ITERS):
        rho_new = 1.0 / (2.0 * quotient_number - rho_old)
        chebyshev.append((2.0 * rho_new / half_width, rho_new * rho_old))
        rho_old = rho_new
    explicit = []
    for index_k in range(ITERS):
        if index_k % 2 == 0:
            explicit.append((TIME_STEP, 0.0))
        else:
            explicit.append((0.5 * TIME_STEP, -0.5))
    return (chebyshev, explicit)


def pressure_terms(center, beside_all):
    masks = [center[2] * beside_all[direction][2] for direction in range(6)]
    perm_faces = [
        harmonic(center[1], beside_all[direction][1], masks[direction]) for direction in range(6)
    ]
    mobility = []
    for direction in range(6):
        field_component = 5 + direction // 2
        if direction % 2 == 0:
            mobility.append(center[field_component] * masks[direction])
        else:
            mobility.append(beside_all[direction][field_component] * masks[direction])
    coefficient = [perm_faces[direction] * mobility[direction] for direction in range(6)]
    diagonal_entries = accumulate(coefficient) + STORAGE + center[4]
    forcing = center[3] + STORAGE * center[0]
    scaling = 1.0 / diagonal_entries
    outgoing = [
        perm_faces[direction] * (center[0] - beside_all[direction][0]) for direction in (0, 2, 4)
    ]
    return (coefficient, diagonal_entries, forcing, scaling, outgoing)


def heat_terms(center, beside_all):
    masks = [center[2] * beside_all[direction][2] for direction in range(6)]
    conduct_faces = [
        harmonic(center[1], beside_all[direction][1], masks[direction]) for direction in range(6)
    ]
    own_fluid = brine_flowability(center[0])
    fluid_faces = [
        harmonic(own_fluid, brine_flowability(beside_all[direction][0]), masks[direction])
        for direction in range(6)
    ]
    velocity = []
    for direction in range(6):
        field_component = 5 + direction // 2
        if direction % 2 == 0:
            velocity.append(center[field_component] * fluid_faces[direction])
        else:
            velocity.append(-beside_all[direction][field_component] * fluid_faces[direction])
    coefficient = [
        conduct_faces[direction] - jnp.minimum(velocity[direction], 0.0) for direction in range(6)
    ]
    outflow = accumulate([jnp.maximum(velocity[direction], 0.0) for direction in range(6)])
    diagonal_entries = accumulate(conduct_faces) + outflow + center[4]
    forcing = center[3]
    scaling = jnp.ones_like(diagonal_entries)
    outgoing = [fluid_faces[direction] for direction in (0, 2, 4)]
    return (coefficient, diagonal_entries, forcing, scaling, outgoing)


def crop(values, margin):
    row_count = values.shape[-2]
    col_count = values.shape[-1]
    return values[..., margin : row_count - margin, margin * W : col_count - margin * W]


def beside(values):
    row_count = values.shape[-2]
    col_count = values.shape[-1]
    inner_cols = col_count - 2 * W
    column_pos = lax.broadcasted_iota(jnp.int32, (row_count - 2, inner_cols), 1) % W
    lower_mask = (column_pos > 0).astype(values.dtype)
    upper_mask = (column_pos < W - 1).astype(values.dtype)
    center = values[..., 1 : row_count - 1, W : col_count - W]
    beside_all = [
        values[..., 2:, W : col_count - W],
        values[..., : row_count - 2, W : col_count - W],
        values[..., 1 : row_count - 1, 2 * W :],
        values[..., 1 : row_count - 1, : col_count - 2 * W],
        values[..., 1 : row_count - 1, W + 1 : col_count - W + 1] * upper_mask,
        values[..., 1 : row_count - 1, W - 1 : col_count - W - 1] * lower_mask,
    ]
    return (beside_all, center)


def extend(values, margin):
    row_ext = extended(values, (("ba", 1),), margin)
    return extended(row_ext, (("aa", 2),), margin * W)


def regroup_layout(received_block):
    components = received_block.shape[0]
    turned = jnp.transpose(received_block, (0, 3, 2, 1))
    return turned.reshape(
        components, received_block.shape[3], received_block.shape[2] * received_block.shape[1]
    )


def body(states, coupled, facies, injectors, producers, perm_table, cond_table):
    is_press = lax.axis_index("code") == 0
    own_field = states[0]
    row_count = own_field.shape[0]
    col_count = own_field.shape[1]
    lithology_lookup = jnp.where(is_press, perm_table, cond_table)
    other_table = jnp.where(is_press, cond_table, perm_table)
    own_classes = facies[0]
    property_field = accumulate(
        [jnp.where(own_classes == index_c, lithology_lookup[index_c], 0.0) for index_c in range(NF)]
    )
    other_property = accumulate(
        [jnp.where(own_classes == index_c, other_table[index_c], 0.0) for index_c in range(NF)]
    )
    inject_cells = injectors[0].astype(jnp.float32)
    produce_cells = producers[0].astype(jnp.float32)
    source = inject_cells * jnp.where(
        is_press, INJECTION, FLOW_RATE * CHILLED_INFLOW
    ) + produce_cells * jnp.where(is_press, PRODUCT_INDEX * WELL_PRESSURE, 0.0)
    well_sink = produce_cells * jnp.where(
        is_press, PRODUCT_INDEX, FLOW_RATE
    ) + inject_cells * jnp.where(is_press, 0.0, FLOW_RATE)
    inside = jnp.ones_like(own_field)
    stacked = jnp.concatenate(
        [
            jnp.stack([own_field, property_field, inside, source, well_sink]),
            coupled[0],
            other_property[None],
        ],
        axis=0,
    )
    halo_depth = 1
    widened_stack = extend(stacked, halo_depth)
    beside_all, center = beside(widened_stack)
    coefficient, diagonal_entries, forcing, scaling, outgoing_list = lax.cond(
        is_press, pressure_terms, heat_terms, center, beside_all
    )
    outgoing = jnp.stack([crop(face_item, halo_depth - 1) for face_item in outgoing_list])
    payload = outgoing[::-1].reshape(3, row_count, col_count // W, W)
    regrouped = regroup_layout(
        lax.all_to_all(payload, "ba", split_axis=3, concat_axis=1, tiled=True)
    )
    received = from_partner(regrouped, "code", 0)
    chebyshev, explicit = sweep_weights()
    present_iterate = own_field
    previous = None
    prev_depth = 0
    counter = 0
    for sweep_block in range(ITERS // halo_depth):
        widened = extend(present_iterate[None], halo_depth)[0]
        if previous is None:
            previous = widened
            prev_depth = halo_depth
        region = halo_depth
        region = region - 1
        around_v, center_v = beside(widened)
        index_shift = halo_depth - 1 - region
        applied = crop(diagonal_entries, index_shift) * center_v - accumulate(
            [
                crop(coefficient[direction], index_shift) * around_v[direction]
                for direction in range(6)
            ]
        )
        residual = crop(scaling, index_shift) * (crop(forcing, index_shift) - applied)
        weight_new = jnp.where(is_press, chebyshev[counter][0], explicit[counter][0])
        weight_old = jnp.where(is_press, chebyshev[counter][1], explicit[counter][1])
        updated = (
            center_v
            + weight_new * residual
            + weight_old * (center_v - crop(previous, prev_depth - region))
        )
        previous = widened
        prev_depth = region + 1
        widened = updated
        counter = counter + 1
        present_iterate = widened
    return (present_iterate[None], received[None])


def solution(mesh):
    return jax.shard_map(
        body,
        mesh=mesh,
        in_specs=(
            P("code", "ba", "aa"),
            P("code", None, "ba", "aa"),
            P("code", "ba", "aa"),
            P("code", "ba", "aa"),
            P("code", "ba", "aa"),
            P(),
            P(),
        ),
        out_specs=(P("code", "ba", "aa"), P("code", None, "ba", "aa")),
        check_vma=False,
    )
```

profile of v0, /device:TPU:9, one launch (start us, length us, event | category | flops | bytes accessed | tf_op | source)
XLA Modules:
  0.0 276.1 jit_solution(8384227951068717032)
XLA Ops:
  0.7 2.4 constant_dynamic-update-slice_fusion.1
  4.4 7.0 %fusion.146 = (f32[32,8192]{1,0:T(8,128)}, pred[1,32,8192]{2,1,0:T(8,128)(4,1)S(1)}, pred[1,32,8192]{2,1,0:T(8,128)(4,1)S(1)}, pred[1,32,8192]{2,1,0:T(8,128)(4,...) fusion(f32[]{:T(128)} %bitcast.56, f32[]{:T(128)} %bitcast.55, ...), kind=kLoop, calls=%fused_computation.269 | loop fusion | flops 4456448 | bytes 3670040 | tf_op jit(solution)/shard_map/add | solution.py:57
  11.5 5.4 %fusion.147 = f32[9,32,8192]{2,1,0:T(8,128)} fusion(f32[9,32,8192]{2,1,0:T(8,128)} %constant_dynamic-update-slice_fusion.1, pred[1,32,8192]{2,1,0:T(8,128)(4,1)S(1)} %get-tuple-element.116, f32[]{:T(128)} %bitcast.56, pred[1,32,8192]{2,1,0:T(8,128)(4,1)S(1)} %get-tuple-element.115, f32[]{:T(128)} %bitcast.55, ...), kind=kLoop, calls=%fused_computation.270 | loop fusion | flops 2883584 | bytes 2624512
  19.2 3.4 %fusion.144 = (f32[32,8192]{1,0:T(8,128)S(1)}, f32[32,8192]{1,0:T(8,128)}, f32[9,32,8192]{2,1,0:T(8,128)}) fusion(f32[]{:T(128)S(6)} %select_n.156, s32[1,32,8192]{2,1,0:T(8,128)S(1)} %copy-done.25, f32[]{:T(128)S(6)} %select_n.155, s32[1,32,8192]{2,1,0:T(8,128)} %param.12, f32[]{:T(128)S(6)} %select_n.157, f32[9,32,8192]{2,1,0:T(8,128)} %fusion.145), kind=kLoop, calls=%fused_computation.264 | loop fusion | flops 1835008 | bytes 5242892 | tf_op jit(solution)/shard_map/add | solution.py:184
  22.6 1.9 constant_dynamic-update-slice_fusion
  24.5 5.6 %add_dynamic-update-slice_fusion = f32[9,32,8192]{2,1,0:T(8,128)} fusion(f32[9,32,8192]{2,1,0:T(8,128)} %constant_dynamic-update-slice_fusion, pred[1,32,8192]{2,1,0:T(8,128)(4,1)S(1)} %copy-done.36, pred[1,32,8192]{2,1,0:T(8,128)(4,1)S(1)} %copy-done.34, pred[1,32,8192]{2,1,0:T(8,128)(4,1)S(1)} %copy-done.32, pred[1,32,8192]{2,1,0:T(8,128)(4,1)S(1)} %copy-done.30, ...), kind=kLoop, calls=%fused_computation.251 | loop fusion | flops 2883584 | bytes 2624512 | tf_op jit(solution)/shard_map/concatenate | solution.py:191
  30.1 3.7 %fusion.164 = (f32[9,1,8192]{2,1,0:T(1,128)}, f32[9,1,8192]{2,1,0:T(1,128)}) fusion(f32[9,32,8192]{2,1,0:T(8,128)} %add_dynamic-update-slice_fusion), kind=kLoop, calls=%fused_computation.280 | loop fusion | bytes 1179648 | tf_op jit(solution)/shard_map/slice | solution.py:27
  35.0 4.7 %collective-permute-start.5 = (f32[9,1,8192]{2,1,0:T(1,128)}, f32[9,1,8192]{2,1,0:T(1,128)}, u32[]{:S(2)}, u32[]{:S(2)}) collective-permute-start(f32[9,1,8192]{2,1,0:T(1,128)} %get-tuple-element.139), channel_id=1, source_target_pairs={{0,1},{2,3},{4,5},{6,7},{8,9},{10,11},{12,13},{14,15},{16,17},{18,... | collective-permute-start | bytes 884744 | tf_op jit(solution)/shard_map/ppermute | solution.py:26
  42.4 2.8 %collective-permute-done = f32[1,1,8192]{2,1,0:T(1,128)S(1)} collective-permute-done((f32[1,1,8192]{2,1,0:T(1,128)S(1)}, f32[1,1,8192]{2,1,0:T(1,128)S(1)}, u32[]{:S(2)}, u32[]{:S(2)}) %collective-permute-start) | collective-permute-done | bytes 32800 | tf_op jit(solution)/shard_map/ppermute | solution.py:26
  47.1 3.1 %collective-permute-start.2 = (f32[1,34,64]{2,1,0:T(8,128)S(1)}, f32[1,34,64]{2,1,0:T(8,128)S(1)}, u32[]{:S(2)}, u32[]{:S(2)}) collective-permute-start(f32[1,34,64]{2,1,0:T(8,128)S(1)} %get-tuple-element.151), channel_id=1, source_target_pairs={{0,2},{2,4},{4,6},{6,8},{8,10},{10,12},{12,14},{1,3},{3,5},{5,7},{... | collective-permute-start | bytes 26120 | tf_op jit(solution)/shard_map/ppermute | solution.py:26
  50.2 3.0 %collective-permute-start.3 = (f32[1,34,64]{2,1,0:T(8,128)S(1)}, f32[1,34,64]{2,1,0:T(8,128)S(1)}, u32[]{:S(2)}, u32[]{:S(2)}) collective-permute-start(f32[1,34,64]{2,1,0:T(8,128)S(1)} %get-tuple-element.150), channel_id=1, source_target_pairs={{2,0},{4,2},{6,4},{8,6},{10,8},{12,10},{14,12},{3,1},{5,3},{7,5},{... | collective-permute-start | bytes 26120 | tf_op jit(solution)/shard_map/ppermute | solution.py:29
  54.8 1.9 concatenate.46
  58.0 4.1 %collective-permute-start.6 = (f32[9,34,64]{2,1,0:T(8,128)S(1)}, f32[9,34,64]{2,1,0:T(8,128)S(1)}, u32[]{:S(2)}, u32[]{:S(2)}) collective-permute-start(f32[9,34,64]{2,1,0:T(8,128)S(1)} %get-tuple-element.136), channel_id=1, source_target_pairs={{2,0},{4,2},{6,4},{8,6},{10,8},{12,10},{14,12},{3,1},{5,3},{7,5},{... | collective-permute-start | bytes 235016 | tf_op jit(solution)/shard_map/ppermute | solution.py:29
  62.1 2.3 collective-permute-start.7
  64.5 8.6 %pad_maximum_fusion.1 = (f32[9,32,8192]{2,1,0:T(8,128)}, f32[9,32,8192]{2,1,0:T(8,128)}) fusion(f32[9,32,8192]{2,1,0:T(8,128)S(1)} %copy-done, f32[9,1,8192]{2,1,0:T(1,128)} %collective-permute-done.5, f32[9,1,8192]{2,1,0:T(1,128)S(1)} %collective-permute-done.4), kind=kLoop, calls=%fused_computation.160 | loop fusion | flops 4718592 | bytes 28901376 | tf_op jit(solution)/shard_map/concatenate | solution.py:30
  73.7 10.1 %maximum_maximum_fusion = (f32[9,34,8256]{2,1,0:T(8,128)}, f32[9,34,8256]{2,1,0:T(8,128)S(1)}) fusion(f32[9,1,8192]{2,1,0:T(1,128)S(1)} %collective-permute-done.4, f32[9,32,8192]{2,1,0:T(8,128)S(1)} %copy-done, f32[9,1,8192]{2,1,0:T(1,128)} %collective-permute-done.5, f32[9,34,64]{2,1,0:T(8,128)} %collective-permute-done.7, f32[9,34,64]{2,1,0:T(8,128)} %copy-done.37), kind=kLoop, calls=%fused_computation.157 | loop fusion | flops 15158016 | bytes 30394368 | tf_op jit(solution)/shard_map/concatenate | solution.py:30
  83.8 17.1 %slice_multiply_fusion = (f32[9,32,8192]{2,1,0:T(8,128)}, f32[9,32,8192]{2,1,0:T(8,128)}) fusion(f32[9,34,8256]{2,1,0:T(8,128)} %get-tuple-element.133, f32[32,8192]{1,0:T(8,128)} %get-tuple-element.160), kind=kLoop, calls=%fused_computation.158 | loop fusion | flops 2359296 | bytes 38797312 | tf_op jit(solution)/shard_map/mul | solution.py:150
  101.0 10.1 %slice_multiply_fusion.1 = (f32[9,32,8192]{2,1,0:T(8,128)}, f32[9,32,8192]{2,1,0:T(8,128)}) fusion(f32[9,34,8256]{2,1,0:T(8,128)S(1)} %get-tuple-element.134, f32[32,8192]{1,0:T(8,128)} %get-tuple-element.161), kind=kLoop, calls=%fused_computation.159 | loop fusion | flops 2359296 | bytes 38797312 | tf_op jit(solution)/shard_map/mul | solution.py:149
  111.1 19.9 %conditional.1 = (f32[32,8192]{1,0:T(8,128)S(1)}, f32[32,8192]{1,0:T(8,128)S(1)}, f32[32,8192]{1,0:T(8,128)S(1)}, f32[32,8192]{1,0:T(8,128)S(1)}, f32[32,8192]{1...) conditional(s32[]{:T(128)} %convert_element_type.37, ...), branch_computations={%region_0.1_spmd, %region_1.2_spmd} | conditional | flops 67371008 | bytes 78643328 | solution.py:202
  111.1 10.7 %add_add_fusion = (f32[32,8192]{1,0:T(8,128)S(1)}, f32[32,8192]{1,0:T(8,128)S(1)}, f32[32,8192]{1,0:T(8,128)S(1)}, f32[32,8192]{1,0:T(8,128)S(1)}, f32[32,8192]{...) fusion(f32[32,8192]{1,0:T(8,128)} %get-tuple-element.56, f32[32,8192]{1,0:T(8,128)S(1)} %get-tuple-element.48, ...), kind=kLoop, calls=%fused_computation.86 | loop fusion | flops 40370176 | bytes 35651584 | tf_op jit(solution)/shard_map/cond/branch_0_fun/add | solution.py:123
  121.8 5.0 %minimum_subtract_fusion = (f32[32,8192]{1,0:T(8,128)S(1)}, f32[32,8192]{1,0:T(8,128)S(1)}, f32[32,8192]{1,0:T(8,128)S(1)}, f32[32,8192]{1,0:T(8,128)S(1)}, f32[32,8192]{1,0:T(8,128)S(1)}) fusion(f32[32,8192]{1,0:T(8,128)S(1)} %get-tuple-element.96, f32[32,8192]{1,0:T(8,128)S(1)} %get-tuple-element.48, f32[9,32,8192]{2,1,0:T(8,128)} %get-tuple-element.55, ...), kind=kLoop, calls=%fused_computation.87 | loop fusion | flops 11796480 | bytes 22020096 | tf_op jit(solution)/shard_map/cond/branch_0_fun/sub | solution.py:120
  127.2 3.5 %subtract_divide_fusion = (f32[1,32,8192]{2,1,0:T(8,128)S(1)}, f32[1,32,8192]{2,1,0:T(8,128)S(1)}, f32[1,32,8192]{2,1,0:T(8,128)S(1)}) fusion(f32[9,32,8192]{2,1,0:T(8,128)} %get-tuple-element.54, f32[1,32,8192]{2,1,0:T(8,128)S(1)} %copy-done.5, f32[9,32,8192]{2,1,0:T(8,128)} %get-tuple-element.52, f32[9,32,8192]{2,1,0:T(8,128)S(1)} %get-tuple-element.47), kind=kLoop, calls=%fused_computation.83 | loop fusion | flops 12845056 | bytes 10485760 | tf_op jit(solution)/shard_map/cond/branch_0_fun/div | solution.py:46
  133.9 3.7 %collective-permute-start.8 = (f32[1,1,8192]{2,1,0:T(1,128)S(1)}, f32[1,1,8192]{2,1,0:T(1,128)S(1)}, u32[]{:S(2)}, u32[]{:S(2)}) collective-permute-start(f32[1,1,8192]{2,1,0:T(1,128)S(1)} %get-tuple-element.156), channel_id=1, source_target_pairs={{0,1},{2,3},{4,5},{6,7},{8,9},{10,11},{12,13},{14,15},{16,17},{18,... | collective-permute-start | bytes 98312 | tf_op jit(solution)/shard_map/ppermute | solution.py:26
  138.9 3.3 %collective-permute-done.9 = f32[1,1,8192]{2,1,0:T(1,128)S(1)} collective-permute-done((f32[1,1,8192]{2,1,0:T(1,128)S(1)}, f32[1,1,8192]{2,1,0:T(1,128)S(1)}, u32[]{:S(2)}, u32[]{:S(2)}) %collective-permute-start.9) | collective-permute-done | bytes 32800 | tf_op jit(solution)/shard_map/ppermute | solution.py:29
  143.6 4.1 %collective-permute-start.10 = (f32[1,34,64]{2,1,0:T(8,128)S(1)}, f32[1,34,64]{2,1,0:T(8,128)S(1)}, u32[]{:S(2)}, u32[]{:S(2)}) collective-permute-start(f32[1,34,64]{2,1,0:T(8,128)S(1)} %get-tuple-element.149), channel_id=1, source_target_pairs={{0,2},{2,4},{4,6},{6,8},{8,10},{10,12},{12,14},{1,3},{3,5},{5,7},{... | collective-permute-start | bytes 26120 | tf_op jit(solution)/shard_map/ppermute | solution.py:26
  147.7 2.1 collective-permute-start.11
  149.8 2.4 collective-permute-done.11
  152.2 1.8 concatenate.54
  154.1 5.5 %fusion.103 = f32[1,32,8192]{2,1,0:T(8,128)S(1)} fusion(f32[32,8192]{1,0:T(8,128)} %copy-done.9, f32[32,8192]{1,0:T(8,128)} %copy-done.1, f32[32,8192]{1,0:T(8,128)} %copy-done.10, f32[32,8192]{1,0:T(8,128)} %copy-done.13, f32[34,8320]{1,0:T(8,128)S(1)} %bitcast.551, f32[32,8192]{1,0:T(8,128)} %copy-done.12, f32[32,8192]{1,0:T(8,128)} %copy-done.14, ...), kind=kLoop, calls=%fused_computation.196 | loop fusion | flops 6553600 | bytes 18948104 | tf_op jit(solution)/shard_map/broadcast_in_dim | solution.py:217
  163.6 3.3 %collective-permute-done.13 = f32[1,1,8192]{2,1,0:T(1,128)S(1)} collective-permute-done((f32[1,1,8192]{2,1,0:T(1,128)S(1)}, f32[1,1,8192]{2,1,0:T(1,128)S(1)}, u32[]{:S(2)}, u32[]{:S(2)}) %collective-permute-start.13) | collective-permute-done | bytes 32800 | tf_op jit(solution)/shard_map/ppermute | solution.py:29
  169.4 3.1 %collective-permute-start.14 = (f32[1,34,64]{2,1,0:T(8,128)S(1)}, f32[1,34,64]{2,1,0:T(8,128)S(1)}, u32[]{:S(2)}, u32[]{:S(2)}) collective-permute-start(f32[1,34,64]{2,1,0:T(8,128)S(1)} %get-tuple-element.147), channel_id=1, source_target_pairs={{0,2},{2,4},{4,6},{6,8},{8,10},{10,12},{12,14},{1,3},{3,5},{5,7},{... | collective-permute-start | bytes 26120 | tf_op jit(solution)/shard_map/ppermute | solution.py:26
  172.5 3.1 %collective-permute-start.15 = (f32[1,34,64]{2,1,0:T(8,128)S(1)}, f32[1,34,64]{2,1,0:T(8,128)S(1)}, u32[]{:S(2)}, u32[]{:S(2)}) collective-permute-start(f32[1,34,64]{2,1,0:T(8,128)S(1)} %get-tuple-element.146), channel_id=1, source_target_pairs={{2,0},{4,2},{6,4},{8,6},{10,8},{12,10},{14,12},{3,1},{5,3},{7,5},{... | collective-permute-start | bytes 26120 | tf_op jit(solution)/shard_map/ppermute | solution.py:29
  175.6 3.7 %pad_maximum_fusion.3 = f32[3,32,8192]{2,1,0:T(8,128)} fusion(f32[1,32,8192]{2,1,0:T(8,128)} %copy-done.22, f32[1,32,8192]{2,1,0:T(8,128)} %copy-done.23, f32[1,32,8192]{2,1,0:T(8,128)} %copy-done.24), kind=kLoop, calls=%fused_computation.162 | loop fusion | flops 1572864 | bytes 6291456 | tf_op jit(solution)/shard_map/stack | solution.py:205
  179.4 3.8 %rev.3 = f32[3,32,8192]{2,1,0:T(8,128)} reverse(f32[3,32,8192]{2,1,0:T(8,128)} %pad_maximum_fusion.3), dimensions={0} | reverse | bytes 6291456 | tf_op jit(solution)/shard_map/rev | solution.py:206
  183.1 6.1 %reshape.195 = f32[3,32,128,64]{3,2,1,0:T(8,128)} reshape(f32[3,32,8192]{2,1,0:T(8,128)} %rev.3) | data formatting | bytes 6291456 | tf_op jit(solution)/shard_map/reshape | solution.py:206
  189.2 6.5 %copy.13 = f32[3,32,128,64]{2,1,0,3:T(8,128)} copy(f32[3,32,128,64]{3,2,1,0:T(8,128)} %reshape.195) | data formatting | bytes 6291456 | tf_op jit(solution)/shard_map/reshape | solution.py:206
  195.7 5.2 %all-to-all-start = ((f32[3,32,128,64]{2,1,0,3:T(8,128)}), f32[3,32,128,64]{2,1,0,3:T(8,128)}, u32[]{:S(2)}, u32[]{:S(2)}) async-start(f32[3,32,128,64]{2,1,0,3:T(8,128)} %copy.13), calls=%async_computation | async-start | bytes 6291456 | tf_op jit(solution)/shard_map/all_to_all | solution.py:208
  201.0 1.9 concatenate.56
  202.8 5.5 %fusion.112 = f32[1,32,8192]{2,1,0:T(8,128)S(1)} fusion(f32[32,8192]{1,0:T(8,128)} %copy-done.9, f32[32,8192]{1,0:T(8,128)} %copy-done.1, f32[32,8192]{1,0:T(8,128)} %copy-done.10, f32[32,8192]{1,0:T(8,128)} %copy-done.13, f32[34,8320]{1,0:T(8,128)S(1)} %bitcast.549, f32[32,8192]{1,0:T(8,128)} %copy-done.12, f32[32,8192]{1,0:T(8,128)} %copy-done.14, ...), kind=kLoop, calls=%fused_computation.205 | loop fusion | flops 6553600 | bytes 18948104 | tf_op jit(solution)/shard_map/broadcast_in_dim | solution.py:217
  209.4 3.3 %collective-permute-start.16 = (f32[1,1,8192]{2,1,0:T(1,128)S(1)}, f32[1,1,8192]{2,1,0:T(1,128)S(1)}, u32[]{:S(2)}, u32[]{:S(2)}) collective-permute-start(f32[1,1,8192]{2,1,0:T(1,128)S(1)} %get-tuple-element.152), channel_id=1, source_target_pairs={{0,1},{2,3},{4,5},{6,7},{8,9},{10,11},{12,13},{14,15},{16,17},{18,... | collective-permute-start | bytes 98312 | tf_op jit(solution)/shard_map/ppermute | solution.py:26
  214.3 23.3 %all-to-all-done = f32[3,32,128,64]{2,1,0,3:T(8,128)} async-done(((f32[3,32,128,64]{2,1,0,3:T(8,128)}), f32[3,32,128,64]{2,1,0,3:T(8,128)}, u32[]{:S(2)}, u32[]{:S(2)}) %all-to-all-start) | async-done | bytes 3145760 | tf_op jit(solution)/shard_map/all_to_all | solution.py:208
  237.5 5.3 %copy.15 = f32[3,2,32,128,32]{3,4,2,1,0:T(8,128)} copy(f32[3,2,32,128,32]{3,2,0,4,1:T(8,128)} %bitcast.76) | data formatting | bytes 6291456 | tf_op jit(solution)/shard_map/all_to_all | solution.py:208
  242.9 5.9 %copy.16 = f32[3,32,128,64]{3,2,1,0:T(8,128)} copy(f32[3,32,128,64]{2,1,3,0:T(8,128)} %bitcast.558) | data formatting | bytes 6291456 | tf_op jit(solution)/shard_map/transpose | solution.py:162
  248.7 5.8 %reshape.196 = f32[3,32,8192]{2,1,0:T(8,128)} reshape(f32[3,32,128,64]{3,2,1,0:T(8,128)} %copy.16) | data formatting | bytes 6291456 | tf_op jit(solution)/shard_map/reshape | solution.py:163
  256.5 1.9 collective-permute-start.18
  258.4 4.3 %collective-permute-start.19 = (f32[1,34,64]{2,1,0:T(8,128)S(1)}, f32[1,34,64]{2,1,0:T(8,128)S(1)}, u32[]{:S(2)}, u32[]{:S(2)}) collective-permute-start(f32[1,34,64]{2,1,0:T(8,128)S(1)} %get-tuple-element.144), channel_id=1, source_target_pairs={{2,0},{4,2},{6,4},{8,6},{10,8},{12,10},{14,12},{3,1},{5,3},{7,5},{... | collective-permute-start | bytes 26120 | tf_op jit(solution)/shard_map/ppermute | solution.py:29
  265.8 6.5 %fusion.121 = f32[1,32,8192]{2,1,0:T(8,128)} fusion(f32[32,8192]{1,0:T(8,128)} %copy-done.9, f32[32,8192]{1,0:T(8,128)} %copy-done.1, f32[32,8192]{1,0:T(8,128)} %copy-done.10, f32[32,8192]{1,0:T(8,128)} %copy-done.13, f32[34,8320]{1,0:T(8,128)S(1)} %bitcast.553, f32[32,8192]{1,0:T(8,128)} %copy-done.12, f32[32,8192]{1,0:T(8,128)} %copy-done.14, ...), kind=kLoop, calls=%fused_computation.214 | loop fusion | flops 6553600 | bytes 18948104 | tf_op jit(solution)/shard_map/broadcast_in_dim | solution.py:244
  272.3 3.8 %copy.49 = f32[1,3,32,8192]{3,2,1,0:T(8,128)} copy(f32[1,3,32,8192]{3,2,1,0:T(8,128)} %bitcast.79) | data formatting | bytes 6291456
  (130 shorter events, 32.7 us)
Async XLA Ops:
  0.6 17.3 %copy-start.26 = (s32[1,32,8192]{2,1,0:T(8,128)S(1)}, s32[1,32,8192]{2,1,0:T(8,128)}, u32[]{:S(2)}) copy-start(s32[1,32,8192]{2,1,0:T(8,128)} %param.12) | copy-start | bytes 3145732
  0.6 17.3 %copy-start.25 = (s32[1,32,8192]{2,1,0:T(8,128)S(1)}, s32[1,32,8192]{2,1,0:T(8,128)}, u32[]{:S(2)}) copy-start(s32[1,32,8192]{2,1,0:T(8,128)} %param.13) | copy-start | bytes 3145732
  11.5 5.4 %copy-start.33 = (pred[1,32,8192]{2,1,0:T(8,128)(4,1)}, pred[1,32,8192]{2,1,0:T(8,128)(4,1)S(1)}, u32[]{:S(2)}) copy-start(pred[1,32,8192]{2,1,0:T(8,128)(4,1)S(1)} %get-tuple-element.115) | copy-start | bytes 786436
  11.5 5.4 %copy-start.35 = (pred[1,32,8192]{2,1,0:T(8,128)(4,1)}, pred[1,32,8192]{2,1,0:T(8,128)(4,1)S(1)}, u32[]{:S(2)}) copy-start(pred[1,32,8192]{2,1,0:T(8,128)(4,1)S(1)} %get-tuple-element.116) | copy-start | bytes 786436
  17.9 21.8 %copy-start.4 = (f32[1,32,8192]{2,1,0:T(8,128)S(1)}, f32[1,32,8192]{2,1,0:T(8,128)}, u32[]{:S(2)}) copy-start(f32[1,32,8192]{2,1,0:T(8,128)} %param.9) | copy-start | bytes 3145732
  18.0 6.6 %copy-start.28 = (pred[1,32,8192]{2,1,0:T(8,128)(4,1)S(1)}, pred[1,32,8192]{2,1,0:T(8,128)(4,1)}, u32[]{:S(2)}) copy-start(pred[1,32,8192]{2,1,0:T(8,128)(4,1)} %copy-done.27) | copy-start | bytes 786436
  18.0 6.6 %copy-start.30 = (pred[1,32,8192]{2,1,0:T(8,128)(4,1)S(1)}, pred[1,32,8192]{2,1,0:T(8,128)(4,1)}, u32[]{:S(2)}) copy-start(pred[1,32,8192]{2,1,0:T(8,128)(4,1)} %copy-done.29) | copy-start | bytes 786436
  18.0 6.5 %copy-start.32 = (pred[1,32,8192]{2,1,0:T(8,128)(4,1)S(1)}, pred[1,32,8192]{2,1,0:T(8,128)(4,1)}, u32[]{:S(2)}) copy-start(pred[1,32,8192]{2,1,0:T(8,128)(4,1)} %copy-done.31) | copy-start | bytes 786436
  18.0 6.5 %copy-start.34 = (pred[1,32,8192]{2,1,0:T(8,128)(4,1)S(1)}, pred[1,32,8192]{2,1,0:T(8,128)(4,1)}, u32[]{:S(2)}) copy-start(pred[1,32,8192]{2,1,0:T(8,128)(4,1)} %copy-done.33) | copy-start | bytes 786436
  18.0 6.5 %copy-start.36 = (pred[1,32,8192]{2,1,0:T(8,128)(4,1)S(1)}, pred[1,32,8192]{2,1,0:T(8,128)(4,1)}, u32[]{:S(2)}) copy-start(pred[1,32,8192]{2,1,0:T(8,128)(4,1)} %copy-done.35) | copy-start | bytes 786436
  33.7 22.9 %collective-permute-start.4 = (f32[9,1,8192]{2,1,0:T(1,128)}, f32[9,1,8192]{2,1,0:T(1,128)S(1)}, u32[]{:S(2)}, u32[]{:S(2)}) collective-permute-start(f32[9,1,8192]{2,1,0:T(1,128)} %get-tuple-element.140), channel_id=1, source_target_pairs={{1,0},{3,2},{5,4},{7,6},{9,8},{11,10},{13,12},{15,14},{17,16},{19,... | collective-permute-start | bytes 884744 | tf_op jit(solution)/shard_map/ppermute | solution.py:29
  35.0 21.6 %collective-permute-start.5 = (f32[9,1,8192]{2,1,0:T(1,128)}, f32[9,1,8192]{2,1,0:T(1,128)}, u32[]{:S(2)}, u32[]{:S(2)}) collective-permute-start(f32[9,1,8192]{2,1,0:T(1,128)} %get-tuple-element.139), channel_id=1, source_target_pairs={{0,1},{2,3},{4,5},{6,7},{8,9},{10,11},{12,13},{14,15},{16,17},{18,... | collective-permute-start | bytes 884744 | tf_op jit(solution)/shard_map/ppermute | solution.py:26
  39.8 5.5 %collective-permute-start = (f32[1,1,8192]{2,1,0:T(1,128)S(1)}, f32[1,1,8192]{2,1,0:T(1,128)S(1)}, u32[]{:S(2)}, u32[]{:S(2)}) collective-permute-start(f32[1,1,8192]{2,1,0:T(1,128)S(1)} %get-tuple-element.158), channel_id=1, source_target_pairs={{0,1},{2,3},{4,5},{6,7},{8,9},{10,11},{12,13},{14,15},{16,17},{18,... | collective-permute-start | bytes 98312 | tf_op jit(solution)/shard_map/ppermute | solution.py:26
  41.1 4.7 %collective-permute-start.1 = (f32[1,1,8192]{2,1,0:T(1,128)S(1)}, f32[1,1,8192]{2,1,0:T(1,128)S(1)}, u32[]{:S(2)}, u32[]{:S(2)}) collective-permute-start(f32[1,1,8192]{2,1,0:T(1,128)S(1)} %get-tuple-element.159), channel_id=1, source_target_pairs={{1,0},{3,2},{5,4},{7,6},{9,8},{11,10},{13,12},{15,14},{17,16},{19,... | collective-permute-start | bytes 98312 | tf_op jit(solution)/shard_map/ppermute | solution.py:29
  47.1 7.7 %collective-permute-start.2 = (f32[1,34,64]{2,1,0:T(8,128)S(1)}, f32[1,34,64]{2,1,0:T(8,128)S(1)}, u32[]{:S(2)}, u32[]{:S(2)}) collective-permute-start(f32[1,34,64]{2,1,0:T(8,128)S(1)} %get-tuple-element.151), channel_id=1, source_target_pairs={{0,2},{2,4},{4,6},{6,8},{8,10},{10,12},{12,14},{1,3},{3,5},{5,7},{... | collective-permute-start | bytes 26120 | tf_op jit(solution)/shard_map/ppermute | solution.py:26
  50.2 4.6 %collective-permute-start.3 = (f32[1,34,64]{2,1,0:T(8,128)S(1)}, f32[1,34,64]{2,1,0:T(8,128)S(1)}, u32[]{:S(2)}, u32[]{:S(2)}) collective-permute-start(f32[1,34,64]{2,1,0:T(8,128)S(1)} %get-tuple-element.150), channel_id=1, source_target_pairs={{2,0},{4,2},{6,4},{8,6},{10,8},{12,10},{14,12},{3,1},{5,3},{7,5},{... | collective-permute-start | bytes 26120 | tf_op jit(solution)/shard_map/ppermute | solution.py:29
  56.6 7.8 %copy-start = (f32[9,32,8192]{2,1,0:T(8,128)S(1)}, f32[9,32,8192]{2,1,0:T(8,128)}, u32[]{:S(2)}) copy-start(f32[9,32,8192]{2,1,0:T(8,128)} %add_dynamic-update-slice_fusion) | copy-start | bytes 28311556
  58.0 15.1 %collective-permute-start.6 = (f32[9,34,64]{2,1,0:T(8,128)S(1)}, f32[9,34,64]{2,1,0:T(8,128)S(1)}, u32[]{:S(2)}, u32[]{:S(2)}) collective-permute-start(f32[9,34,64]{2,1,0:T(8,128)S(1)} %get-tuple-element.136), channel_id=1, source_target_pairs={{2,0},{4,2},{6,4},{8,6},{10,8},{12,10},{14,12},{3,1},{5,3},{7,5},{... | collective-permute-start | bytes 235016 | tf_op jit(solution)/shard_map/ppermute | solution.py:29
  62.1 11.6 %collective-permute-start.7 = (f32[9,34,64]{2,1,0:T(8,128)S(1)}, f32[9,34,64]{2,1,0:T(8,128)}, u32[]{:S(2)}, u32[]{:S(2)}) collective-permute-start(f32[9,34,64]{2,1,0:T(8,128)S(1)} %get-tuple-element.135), channel_id=1, source_target_pairs={{0,2},{2,4},{4,6},{6,8},{8,10},{10,12},{12,14},{1,3},{3,5},{5,7},{... | collective-permute-start | bytes 235016 | tf_op jit(solution)/shard_map/ppermute | solution.py:26
  83.8 27.2 %slice-start = ((s8[9437184]{0:T(1024)(128)(4,1)}), s8[4194304]{0:T(1024)(128)(4,1)S(1)}, s32[]{:S(2)}) async-start(s8[9437184]{0:T(1024)(128)(4,1)} %bitcast.554), calls=%async_computation.1 | async-start | bytes 8388608
  83.8 27.2 %slice-start.1 = ((s8[9437184]{0:T(1024)(128)(4,1)}), s8[4194304]{0:T(1024)(128)(4,1)S(1)}, s32[]{:S(2)}) async-start(s8[9437184]{0:T(1024)(128)(4,1)} %bitcast.554), calls=%async_computation.2 | async-start | bytes 8388608
  101.0 10.1 %slice-start.2 = ((s8[9437184]{0:T(1024)(128)(4,1)}), s8[1048576]{0:T(1024)(128)(4,1)S(1)}, s32[]{:S(2)}) async-start(s8[9437184]{0:T(1024)(128)(4,1)} %bitcast.554), calls=%async_computation.3 | async-start | bytes 2097152
  101.0 10.1 %copy-start.2 = (f32[32,8192]{1,0:T(8,128)S(1)}, f32[32,8192]{1,0:T(8,128)}, u32[]{:S(2)}) copy-start(f32[32,8192]{1,0:T(8,128)} %get-tuple-element.110) | copy-start | bytes 3145732
  131.0 7.9 %copy-start.22 = (f32[1,32,8192]{2,1,0:T(8,128)}, f32[1,32,8192]{2,1,0:T(8,128)S(1)}, u32[]{:S(2)}) copy-start(f32[1,32,8192]{2,1,0:T(8,128)S(1)} %get-tuple-element.94) | copy-start | bytes 3145732
  131.0 11.4 %copy-start.1 = (f32[32,8192]{1,0:T(8,128)}, f32[32,8192]{1,0:T(8,128)S(1)}, u32[]{:S(2)}) copy-start(f32[32,8192]{1,0:T(8,128)S(1)} %get-tuple-element.84) | copy-start | bytes 3145732
  131.0 11.4 %copy-start.7 = (f32[32,8192]{1,0:T(8,128)}, f32[32,8192]{1,0:T(8,128)S(1)}, u32[]{:S(2)}) copy-start(f32[32,8192]{1,0:T(8,128)S(1)} %get-tuple-element.85) | copy-start | bytes 3145732
  131.0 11.4 %copy-start.8 = (f32[32,8192]{1,0:T(8,128)}, f32[32,8192]{1,0:T(8,128)S(1)}, u32[]{:S(2)}) copy-start(f32[32,8192]{1,0:T(8,128)S(1)} %get-tuple-element.86) | copy-start | bytes 3145732
  131.0 11.4 %copy-start.9 = (f32[32,8192]{1,0:T(8,128)}, f32[32,8192]{1,0:T(8,128)S(1)}, u32[]{:S(2)}) copy-start(f32[32,8192]{1,0:T(8,128)S(1)} %get-tuple-element.83) | copy-start | bytes 3145732
  131.0 11.4 %copy-start.10 = (f32[32,8192]{1,0:T(8,128)}, f32[32,8192]{1,0:T(8,128)S(1)}, u32[]{:S(2)}) copy-start(f32[32,8192]{1,0:T(8,128)S(1)} %get-tuple-element.91) | copy-start | bytes 3145732
  131.1 11.4 %copy-start.11 = (f32[32,8192]{1,0:T(8,128)}, f32[32,8192]{1,0:T(8,128)S(1)}, u32[]{:S(2)}) copy-start(f32[32,8192]{1,0:T(8,128)S(1)} %get-tuple-element.87) | copy-start | bytes 3145732
  131.1 11.4 %copy-start.12 = (f32[32,8192]{1,0:T(8,128)}, f32[32,8192]{1,0:T(8,128)S(1)}, u32[]{:S(2)}) copy-start(f32[32,8192]{1,0:T(8,128)S(1)} %get-tuple-element.89) | copy-start | bytes 3145732
  131.1 11.4 %copy-start.13 = (f32[32,8192]{1,0:T(8,128)}, f32[32,8192]{1,0:T(8,128)S(1)}, u32[]{:S(2)}) copy-start(f32[32,8192]{1,0:T(8,128)S(1)} %get-tuple-element.90) | copy-start | bytes 3145732
  131.1 11.4 %copy-start.14 = (f32[32,8192]{1,0:T(8,128)}, f32[32,8192]{1,0:T(8,128)S(1)}, u32[]{:S(2)}) copy-start(f32[32,8192]{1,0:T(8,128)S(1)} %get-tuple-element.88) | copy-start | bytes 3145732
  133.9 5.0 %collective-permute-start.8 = (f32[1,1,8192]{2,1,0:T(1,128)S(1)}, f32[1,1,8192]{2,1,0:T(1,128)S(1)}, u32[]{:S(2)}, u32[]{:S(2)}) collective-permute-start(f32[1,1,8192]{2,1,0:T(1,128)S(1)} %get-tuple-element.156), channel_id=1, source_target_pairs={{0,1},{2,3},{4,5},{6,7},{8,9},{10,11},{12,13},{14,15},{16,17},{18,... | collective-permute-start | bytes 98312 | tf_op jit(solution)/shard_map/ppermute | solution.py:26
  137.6 4.7 %collective-permute-start.9 = (f32[1,1,8192]{2,1,0:T(1,128)S(1)}, f32[1,1,8192]{2,1,0:T(1,128)S(1)}, u32[]{:S(2)}, u32[]{:S(2)}) collective-permute-start(f32[1,1,8192]{2,1,0:T(1,128)S(1)} %get-tuple-element.157), channel_id=1, source_target_pairs={{1,0},{3,2},{5,4},{7,6},{9,8},{11,10},{13,12},{15,14},{17,16},{19,... | collective-permute-start | bytes 98312 | tf_op jit(solution)/shard_map/ppermute | solution.py:29
  143.6 6.2 %collective-permute-start.10 = (f32[1,34,64]{2,1,0:T(8,128)S(1)}, f32[1,34,64]{2,1,0:T(8,128)S(1)}, u32[]{:S(2)}, u32[]{:S(2)}) collective-permute-start(f32[1,34,64]{2,1,0:T(8,128)S(1)} %get-tuple-element.149), channel_id=1, source_target_pairs={{0,2},{2,4},{4,6},{6,8},{8,10},{10,12},{12,14},{1,3},{3,5},{5,7},{... | collective-permute-start | bytes 26120 | tf_op jit(solution)/shard_map/ppermute | solution.py:26
  147.7 4.5 %collective-permute-start.11 = (f32[1,34,64]{2,1,0:T(8,128)S(1)}, f32[1,34,64]{2,1,0:T(8,128)S(1)}, u32[]{:S(2)}, u32[]{:S(2)}) collective-permute-start(f32[1,34,64]{2,1,0:T(8,128)S(1)} %get-tuple-element.148), channel_id=1, source_target_pairs={{2,0},{4,2},{6,4},{8,6},{10,8},{12,10},{14,12},{3,1},{5,3},{7,5},{... | collective-permute-start | bytes 26120 | tf_op jit(solution)/shard_map/ppermute | solution.py:29
  160.6 2.9 %collective-permute-start.12 = (f32[1,1,8192]{2,1,0:T(1,128)S(1)}, f32[1,1,8192]{2,1,0:T(1,128)S(1)}, u32[]{:S(2)}, u32[]{:S(2)}) collective-permute-start(f32[1,1,8192]{2,1,0:T(1,128)S(1)} %get-tuple-element.154), channel_id=1, source_target_pairs={{0,1},{2,3},{4,5},{6,7},{8,9},{10,11},{12,13},{14,15},{16,17},{18,... | collective-permute-start | bytes 98312 | tf_op jit(solution)/shard_map/ppermute | solution.py:26
  162.3 4.7 %collective-permute-start.13 = (f32[1,1,8192]{2,1,0:T(1,128)S(1)}, f32[1,1,8192]{2,1,0:T(1,128)S(1)}, u32[]{:S(2)}, u32[]{:S(2)}) collective-permute-start(f32[1,1,8192]{2,1,0:T(1,128)S(1)} %get-tuple-element.155), channel_id=1, source_target_pairs={{1,0},{3,2},{5,4},{7,6},{9,8},{11,10},{13,12},{15,14},{17,16},{19,... | collective-permute-start | bytes 98312 | tf_op jit(solution)/shard_map/ppermute | solution.py:29
  169.4 31.5 %collective-permute-start.14 = (f32[1,34,64]{2,1,0:T(8,128)S(1)}, f32[1,34,64]{2,1,0:T(8,128)S(1)}, u32[]{:S(2)}, u32[]{:S(2)}) collective-permute-start(f32[1,34,64]{2,1,0:T(8,128)S(1)} %get-tuple-element.147), channel_id=1, source_target_pairs={{0,2},{2,4},{4,6},{6,8},{8,10},{10,12},{12,14},{1,3},{3,5},{5,7},{... | collective-permute-start | bytes 26120 | tf_op jit(solution)/shard_map/ppermute | solution.py:26
  172.5 28.4 %collective-permute-start.15 = (f32[1,34,64]{2,1,0:T(8,128)S(1)}, f32[1,34,64]{2,1,0:T(8,128)S(1)}, u32[]{:S(2)}, u32[]{:S(2)}) collective-permute-start(f32[1,34,64]{2,1,0:T(8,128)S(1)} %get-tuple-element.146), channel_id=1, source_target_pairs={{2,0},{4,2},{6,4},{8,6},{10,8},{12,10},{14,12},{3,1},{5,3},{7,5},{... | collective-permute-start | bytes 26120 | tf_op jit(solution)/shard_map/ppermute | solution.py:29
  195.7 41.8 %all-to-all-start = ((f32[3,32,128,64]{2,1,0,3:T(8,128)}), f32[3,32,128,64]{2,1,0,3:T(8,128)}, u32[]{:S(2)}, u32[]{:S(2)}) async-start(f32[3,32,128,64]{2,1,0,3:T(8,128)} %copy.13), calls=%async_computation | async-start | bytes 6291456 | tf_op jit(solution)/shard_map/all_to_all | solution.py:208
  209.4 45.8 %collective-permute-start.16 = (f32[1,1,8192]{2,1,0:T(1,128)S(1)}, f32[1,1,8192]{2,1,0:T(1,128)S(1)}, u32[]{:S(2)}, u32[]{:S(2)}) collective-permute-start(f32[1,1,8192]{2,1,0:T(1,128)S(1)} %get-tuple-element.152), channel_id=1, source_target_pairs={{0,1},{2,3},{4,5},{6,7},{8,9},{10,11},{12,13},{14,15},{16,17},{18,... | collective-permute-start | bytes 98312 | tf_op jit(solution)/shard_map/ppermute | solution.py:26
  212.7 42.5 %collective-permute-start.17 = (f32[1,1,8192]{2,1,0:T(1,128)S(1)}, f32[1,1,8192]{2,1,0:T(1,128)S(1)}, u32[]{:S(2)}, u32[]{:S(2)}) collective-permute-start(f32[1,1,8192]{2,1,0:T(1,128)S(1)} %get-tuple-element.153), channel_id=1, source_target_pairs={{1,0},{3,2},{5,4},{7,6},{9,8},{11,10},{13,12},{15,14},{17,16},{19,... | collective-permute-start | bytes 98312 | tf_op jit(solution)/shard_map/ppermute | solution.py:29
  242.9 12.3 %copy-start.20 = (f32[1,32,8192]{2,1,0:T(8,128)S(1)}, f32[1,32,8192]{2,1,0:T(8,128)}, u32[]{:S(2)}) copy-start(f32[1,32,8192]{2,1,0:T(8,128)} %copy-done.19) | copy-start | bytes 3145732
  254.6 17.7 %collective-permute-start.20 = (f32[3,32,8192]{2,1,0:T(8,128)}, f32[3,32,8192]{2,1,0:T(8,128)}, u32[]{:S(2)}, u32[]{:S(2)}) collective-permute-start(f32[3,32,8192]{2,1,0:T(8,128)} %reshape.196), channel_id=1, source_target_pairs={{0,16},{16,0},{1,17},{17,1},{2,18},{18,2},{3,19},{19,3},{4,20},{20... | collective-permute-start | bytes 9437192 | tf_op jit(solution)/shard_map/ppermute | solution.py:37
  256.5 6.2 %collective-permute-start.18 = (f32[1,34,64]{2,1,0:T(8,128)S(1)}, f32[1,34,64]{2,1,0:T(8,128)S(1)}, u32[]{:S(2)}, u32[]{:S(2)}) collective-permute-start(f32[1,34,64]{2,1,0:T(8,128)S(1)} %get-tuple-element.145), channel_id=1, source_target_pairs={{0,2},{2,4},{4,6},{6,8},{8,10},{10,12},{12,14},{1,3},{3,5},{5,7},{... | collective-permute-start | bytes 26120 | tf_op jit(solution)/shard_map/ppermute | solution.py:26
  258.4 5.5 %collective-permute-start.19 = (f32[1,34,64]{2,1,0:T(8,128)S(1)}, f32[1,34,64]{2,1,0:T(8,128)S(1)}, u32[]{:S(2)}, u32[]{:S(2)}) collective-permute-start(f32[1,34,64]{2,1,0:T(8,128)S(1)} %get-tuple-element.144), channel_id=1, source_target_pairs={{2,0},{4,2},{6,4},{8,6},{10,8},{12,10},{14,12},{3,1},{5,3},{7,5},{... | collective-permute-start | bytes 26120 | tf_op jit(solution)/shard_map/ppermute | solution.py:29
  (14 other events, 35.6 us)
where the time goes:
time: 279 us; the launch traced here: 276 us
  other arithmetic  116 us (42%)
  local copies, waits for them, and re-layouts  63 us (23%)
  starting transfers between devices  58.4 us (21%)
  waiting for transfers between devices  37 us (13%)
    ppermute x10, starting transfers between devices, extended(): lax.ppermute(lax.slice_in_dim(block, block.shape[dim] - width, None, axis...  29.3 us
    ppermute x10, starting transfers between devices, extended(): lax.ppermute(lax.slice_in_dim(block, 0, width, axis=dim), axis, backward)  23.3 us
    all_to_all x1, waiting for transfers between devices, body(): lax.all_to_all(payload, 'ba', split_axis=3, concat_axis=1, tiled=True)  23.3 us
    concatenate x7, other arithmetic, extended(): block = jnp.concatenate([low, block, high], axis=dim)  21.8 us
    unnamed x82, local copies, waits for them, and re-layouts  17.3 us
    mul x1, other arithmetic, beside(): values[..., 1:row_count - 1, W - 1:col_count - W - 1] * lower_mask  17.1 us
    reshape x2, local copies, waits for them, and re-layouts, body(): payload = outgoing[::-1].reshape(3, row_count, col_count // W, W)  12.6 us
    broadcast_in_dim x3, other arithmetic, body(): widened = extend(present_iterate[None], halo_depth)[0]  12.5 us
  transfers between devices with their start and end apart: 22, of which 7 were waited for; matrix products, arithmetic and copies ran while one was open for 24% of the time, Pallas kernels for 0%

commit v1 on v0

--- a/solution.py
+++ b/solution.py
@@ -1,6 +1,8 @@
 import jax
 import jax.numpy as jnp
 from jax import lax
+from jax.experimental import pallas as pl
+from jax.experimental.pallas import tpu as pltpu
 from jax.sharding import PartitionSpec as P
 
 W = 64
@@ -244,9 +246,688 @@
     return (present_iterate[None], received[None])
 
 
+TINY = 1e-30
+LANES = 128
+HALF = 64
+XH = 4
+VM = pl.BlockSpec(memory_space=pltpu.VMEM)
+SM = pl.BlockSpec(memory_space=pltpu.SMEM)
+HB = pl.BlockSpec(memory_space=pltpu.HBM)
+UNROLL = 4
+LEAN = pltpu.CompilerParams(vmem_limit_bytes=6 * 2**20)
+
+
+def params(megabytes):
+    return pltpu.CompilerParams(vmem_limit_bytes=megabytes * 2**20)
+
+
+def cost(micros):
+    return pl.CostEstimate(flops=0, bytes_accessed=int(micros * 3.2e6), transcendentals=0)
+
+
+def in_vmem(shape):
+    return pltpu.VMEM(shape, jnp.float32)
+
+
+def held(value):
+    return pltpu.with_memory_space_constraint(value, pltpu.VMEM)
+
+
+def lanes_at(tile, base=0):
+    return pl.ds(pl.multiple_of(base + tile * LANES, LANES), LANES)
+
+
+def lane_index(shape):
+    return lax.broadcasted_iota(jnp.int32, shape, len(shape) - 1)
+
+
+def inverse(value):
+    return pl.reciprocal(value, approx=False)
+
+
+def face_mean(left, right):
+    return 2.0 * left * right * inverse(jnp.maximum(left + right, TINY))
+
+
+def flowability(level):
+    return 0.2 + 0.8 * inverse(1.0 + jnp.exp(-6.0 * (level - 0.5)))
+
+
+def half_turn(value):
+    return pltpu.roll(value, HALF, 1)
+
+
+def next_lane(value):
+    return pltpu.roll(value, LANES - 1, 1)
+
+
+def prev_lane(value):
+    return pltpu.roll(value, 1, 1)
+
+
+def next_row(value):
+    return pltpu.roll(value, value.shape[0] - 1, 0)
+
+
+def prev_row(value):
+    return pltpu.roll(value, 1, 0)
+
+
+def class_table(table_ref, shape):
+    lane = lane_index(shape)
+    table = jnp.zeros(shape, jnp.float32)
+    for index_c in range(NF):
+        table = jnp.where(lane == index_c + 1, table_ref[index_c], table)
+    return table
+
+
+def look_up(table, codes):
+    return jnp.take_along_axis(table, codes, axis=1)
+
+
+def placed_pair(pair, is_low):
+    blank = jnp.zeros((6, pair.shape[1]), pair.dtype)
+    return jnp.where(
+        is_low, jnp.concatenate([pair, blank], 0), jnp.concatenate([blank, pair], 0)
+    )
+
+
+def placed_row(row, is_low):
+    blank = jnp.zeros((7, row.shape[1]), row.dtype)
+    return jnp.where(is_low, jnp.concatenate([row, blank], 0), jnp.concatenate([blank, row], 0))
+
+
+def edges_kernel(
+    where_ref, st, cp, fa, ij, pr, to_right, to_left, across, across_right, across_left,
+    left_f, right_f, row_f, left_i, right_i, row_i, sems,
+):
+    is_low = where_ref[1] == 0
+    rows, cols = st.shape[1], st.shape[2]
+    wide = XH * W
+    first = pl.multiple_of(jnp.where(is_low, rows - 8, 0), 8)
+    floats = [st.at[0]] + [cp.at[0, c] for c in range(3)]
+    ints = [fa.at[0], ij.at[0], pr.at[0]]
+    copies = []
+    for group, (left, right, row) in (
+        (floats, (left_f, right_f, row_f)),
+        (ints, (left_i, right_i, row_i)),
+    ):
+        for index, field in enumerate(group):
+            for source, target in (
+                (field.at[pl.ds(first, 8), :], row.at[index]),
+                (field.at[:, pl.ds(0, wide)], left.at[index]),
+                (field.at[:, pl.ds(cols - wide, wide)], right.at[index]),
+            ):
+                copy = pltpu.make_async_copy(source, target, sems.at[len(copies)])
+                copy.start()
+                copies.append(copy)
+    for copy in copies:
+        copy.wait()
+    for target, floats_ref, ints_ref in ((to_right, right_f, right_i), (to_left, left_f, left_i)):
+        parts = [
+            floats_ref[0],
+            (ints_ref[0] + 1).astype(jnp.float32),
+            floats_ref[1],
+            floats_ref[2],
+            floats_ref[3],
+            ints_ref[1].astype(jnp.float32),
+            ints_ref[2].astype(jnp.float32),
+        ]
+        for index, part in enumerate(parts):
+            target[:, index * wide : (index + 1) * wide] = part
+
+    def pair(value):
+        return jnp.where(is_low, value[6:8], value[0:2])
+
+    def near(value):
+        return jnp.where(is_low, value[7:8], value[0:1])
+
+    slots = [
+        pair(row_f[0]),
+        pair((row_i[0] + 1).astype(jnp.float32)),
+        pair(row_f[1]),
+        jnp.concatenate([near(row_f[2]), near(row_f[3])], 0),
+        jnp.concatenate(
+            [near(row_i[1].astype(jnp.float32)), near(row_i[2].astype(jnp.float32))], 0
+        ),
+    ]
+    for index, slot in enumerate(slots):
+        across[:, index * cols : (index + 1) * cols] = slot
+        across_right[:, index * wide : (index + 1) * wide] = slot[:, cols - wide :]
+        across_left[:, index * wide : (index + 1) * wide] = slot[:, :wide]
+
+
+def turn_kernel(
+    where_ref, st_in, cp_in, fa_in, ij_in, pr_in, st, cp, fa, ij, pr, own, other_a, other_b, sems
+):
+    copies = [
+        pltpu.make_async_copy(source, target, sems.at[index])
+        for index, (source, target) in enumerate(
+            ((st_in, st), (cp_in, cp), (fa_in, fa), (ij_in, ij), (pr_in, pr))
+        )
+    ]
+    for copy in copies:
+        copy.start()
+    copies[0].wait()
+    is_heat = where_ref[0] == 1
+    is_low = where_ref[1] == 0
+    groups = st.shape[2] // (4 * LANES)
+    half = groups // 2
+    extra = groups * 2 * LANES
+    row = lax.broadcasted_iota(jnp.int32, (32, LANES), 0)
+
+    def step(group, rims):
+        tall = jnp.concatenate(
+            [st[0, :, lanes_at(4 * group + q)] for q in range(4)], axis=0
+        )
+        tall = jnp.where(is_heat, flowability(tall), tall)
+        turned = tall.T
+        for par in range(2):
+            low = turned[par * HALF : par * HALF + 32]
+            high = turned[par * HALF + 32 : par * HALF + 64]
+            own[:, lanes_at(group, par * groups * LANES)] = jnp.where(is_low, low, high)
+            away = jnp.where(is_low, high, low)
+            rim = high[0:1]
+
+            @pl.when(group < half)
+            def _(away=away, par=par):
+                other_a[:, lanes_at(group, par * half * LANES)] = away
+
+            @pl.when(group >= half)
+            def _(away=away, par=par):
+                other_b[:, lanes_at(group - half, par * half * LANES)] = away
+
+            rims = jnp.where(row == par * groups + group, rim, rims)
+        return rims
+
+    rims = lax.fori_loop(0, groups, step, jnp.zeros((32, LANES), jnp.float32), unroll=UNROLL)
+    own[:, extra : extra + LANES] = jnp.where(is_low, rims, 0.0)
+    other_b[:, half * 2 * LANES : half * 2 * LANES + LANES] = jnp.where(is_low, 0.0, rims)
+    for copy in copies[1:]:
+        copy.wait()
+
+
+def plane_kernel(where_ref, from_right, own_in, other_in, *rest):
+    own, other = rest[-2:]
+    is_heat = where_ref[0] == 1
+    is_low = where_ref[1] == 0
+    wide = XH * W
+    value = from_right[:, 0:LANES]
+    inside = from_right[:, wide : wide + LANES] > 0.5
+    value = jnp.where(is_heat, jnp.where(inside, flowability(value), 0.0), value)
+    tall = jnp.concatenate([value, jnp.zeros((96, LANES), jnp.float32)], 0).T
+    low, high = tall[0:32], tall[32:64]
+    own[...] = own_in[...]
+    other[...] = other_in[...]
+    own[:, own.shape[1] - LANES :] = jnp.where(is_low, low, high)
+    other[:, other.shape[1] - LANES :] = jnp.where(is_low, high, low)
+
+
+def sweep(tiles, coeffs, force, diag, now, last, target, weight, pull):
+    first, stop = tiles
+    low_lanes = lane_index((now.shape[1], LANES)) < HALF
+
+    def step(e, carry):
+        before, here = carry
+        value = now[e + 1]
+        after = half_turn(now[e + 2])
+        total = force[e + 1]
+        total += coeffs[0, e + 1] * next_row(value)
+        total += coeffs[1, e + 1] * prev_row(value)
+        total += coeffs[2, e + 1] * jnp.where(low_lanes, here, after)
+        total += coeffs[3, e + 1] * jnp.where(low_lanes, before, here)
+        total += coeffs[4, e + 1] * next_lane(value)
+        total += coeffs[5, e + 1] * prev_lane(value)
+        if diag is None:
+            result = (1.0 + pull - weight) * value + weight * total
+        else:
+            result = (1.0 + pull) * value + weight * (total - diag[e + 1] * value)
+        if pull != 0.0:
+            result -= pull * last[e + 1]
+        target(e, result)
+        return here, after
+
+    lax.fori_loop(
+        first, stop, step, (half_turn(now[first]), half_turn(now[first + 1])),
+        unroll=UNROLL,
+    )
+
+
+def store_in(ref):
+    def put(e, value):
+        ref[e + 1] = value
+
+    return put
+
+
+def main_kernel(
+    where_ref, perm_ref, cond_ref, st, cp, fa, ij, pr,
+    from_left, from_right, across, corner_left, corner_right,
+    v1, v2, coeffs, force, diag, faces, boundary,
+    v0, prop, rock, c0, c1, c2, src, snk, fluid,
+):
+    is_press = where_ref[0] == 0
+    is_low = where_ref[1] == 0
+    cols = st.shape[2]
+    tiles = cols // LANES
+    ext = v0.shape[0] - 2
+    height = v0.shape[1]
+    wide = XH * W
+    side = XH // 2
+    own_at = pl.multiple_of(jnp.where(is_low, 0, 8), 8)
+    rim_at = pl.multiple_of(jnp.where(is_low, 32, 0), 8)
+    own_rows, rim_rows = pl.ds(own_at, 32), pl.ds(rim_at, 8)
+    perm = class_table(perm_ref, (32, LANES))
+    cond = class_table(cond_ref, (32, LANES))
+    own_table = jnp.where(is_press, perm, cond)
+
+    def put_cells(e, rows, state, codes, f0, f1, f2, inject, produce):
+        count = state.shape[0]
+        v0[e + 1, rows, :] = state
+        prop[e + 1, rows, :] = look_up(own_table[:count], codes)
+        rock[e + 1, rows, :] = look_up(perm[:count], codes)
+        c0[e + 1, rows, :] = f0
+        c1[e + 1, rows, :] = f1
+        c2[e + 1, rows, :] = f2
+        src[e + 1, rows, :] = jnp.where(is_press, 2.0 * inject - produce, 0.1 * inject)
+        snk[e + 1, rows, :] = jnp.where(is_press, produce, produce + inject)
+
+    def put_rim(e, message, slots, at):
+        def pair(index):
+            return placed_pair(message[:, lanes_at(at, index * slots)], is_low)
+
+        def near(index, row):
+            return placed_row(message[row : row + 1, lanes_at(at, index * slots)], is_low)
+
+        put_cells(
+            e, rim_rows, pair(0), pair(1).astype(jnp.int32), pair(2),
+            near(3, 0), near(3, 1), near(4, 0), near(4, 1),
+        )
+
+    def put_side(e, message, at):
+        parts = [message[:, lanes_at(at, index * wide)] for index in range(7)]
+        put_cells(e, own_rows, parts[0], parts[1].astype(jnp.int32), *parts[2:])
+
+    for ref in (v0, prop, rock):
+        for e in (0, ext + 1):
+            ref[e] = jnp.zeros((height, LANES), jnp.float32)
+    for ref in (v1, v2):
+        for e in (0, ext + 1):
+            ref[e] = jnp.zeros((height, LANES), jnp.float32)
+
+    def fill(t, carry):
+        at = lanes_at(t)
+        put_cells(
+            t + side, own_rows, st[0, :, at], fa[0, :, at] + 1,
+            cp[0, 0, :, at], cp[0, 1, :, at], cp[0, 2, :, at],
+            ij[0, :, at].astype(jnp.float32), pr[0, :, at].astype(jnp.float32),
+        )
+        put_rim(t + side, across, cols, t)
+        return carry
+
+    lax.fori_loop(0, tiles, fill, 0, unroll=UNROLL)
+    for at in range(side):
+        put_side(at, from_left, at)
+        put_rim(at, corner_left, wide, at)
+        put_side(tiles + side + at, from_right, at)
+        put_rim(tiles + side + at, corner_right, wide, at)
+
+    lane = lane_index((height, LANES))
+    low_lanes = lane < HALF
+    not_last = lane % W != W - 1
+
+    def next_cells(value, after):
+        return (
+            next_row(value),
+            jnp.where(low_lanes, half_turn(value), half_turn(after)),
+            jnp.where(not_last, next_lane(value), 0.0),
+        )
+
+    blank = jnp.zeros((height, LANES), jnp.float32)
+    chebyshev, explicit = sweep_weights()
+
+    @pl.when(is_press)
+    def _():
+        def step(e, before):
+            value = prop[e + 1]
+            means = [face_mean(value, other) for other in next_cells(value, prop[e + 2])]
+            plus = [mean * ref[e + 1] for mean, ref in zip(means, (c0, c1, c2))]
+            turned = half_turn(plus[1])
+            minus = [
+                prev_row(plus[0]),
+                jnp.where(low_lanes, before, turned),
+                prev_lane(plus[2]),
+            ]
+            total = accumulate(plus + minus) + STORAGE + snk[e + 1]
+            scale = inverse(total)
+            for dim in range(3):
+                coeffs[2 * dim, e + 1] = scale * plus[dim]
+                coeffs[2 * dim + 1, e + 1] = scale * minus[dim]
+            force[e + 1] = scale * (src[e + 1] + STORAGE * v0[e + 1])
+            return turned
+
+        lax.fori_loop(0, ext, step, blank, unroll=UNROLL)
+        (w0, u0), (w1, u1) = chebyshev[:2]
+        sweep((0, ext), coeffs, force, None, v0, v0, store_in(v1), w0, u0)
+        sweep((0, ext), coeffs, force, None, v1, v0, store_in(v2), w1, u1)
+
+    @pl.when(jnp.logical_not(is_press))
+    def _():
+        fluid[0] = blank
+        fluid[ext + 1] = blank
+
+        def levels(e, carry):
+            fluid[e + 1] = jnp.where(prop[e + 1] > 0.0, flowability(v0[e + 1]), 0.0)
+            return carry
+
+        lax.fori_loop(0, ext, levels, 0, unroll=UNROLL)
+
+        def step(e, before):
+            value = prop[e + 1]
+            means = [face_mean(value, other) for other in next_cells(value, prop[e + 2])]
+            value = fluid[e + 1]
+            flows = [face_mean(value, other) for other in next_cells(value, fluid[e + 2])]
+            value = rock[e + 1]
+            for dim, other in enumerate(next_cells(value, rock[e + 2])):
+                faces[dim, e + 1] = face_mean(value, other)
+            speed = [flow * ref[e + 1] for flow, ref in zip(flows, (c0, c1, c2))]
+            gain = [mean + jnp.maximum(rate, 0.0) for mean, rate in zip(means, speed)]
+            loss = [up - rate for up, rate in zip(gain, speed)]
+            turned = half_turn(gain[1]), half_turn(loss[1])
+            minus = [
+                prev_row(gain[0]),
+                jnp.where(low_lanes, before[0], turned[0]),
+                prev_lane(gain[2]),
+            ]
+            behind = [
+                prev_row(loss[0]),
+                jnp.where(low_lanes, before[1], turned[1]),
+                prev_lane(loss[2]),
+            ]
+            diag[e + 1] = accumulate(gain + behind) + snk[e + 1]
+            for dim in range(3):
+                coeffs[2 * dim, e + 1] = loss[dim]
+                coeffs[2 * dim + 1, e + 1] = minus[dim]
+            force[e + 1] = src[e + 1]
+            return turned
+
+        lax.fori_loop(0, ext, step, (blank, blank), unroll=UNROLL)
+        (w0, u0), (w1, u1) = explicit[:2]
+        sweep((0, ext), coeffs, force, diag, v0, v0, store_in(v1), w0, u0)
+        sweep((0, ext), coeffs, force, diag, v1, v0, store_in(v2), w1, u1)
+
+    def send(e, carry):
+        value = v2[e + 1]
+        boundary[:, lanes_at(e)] = jnp.where(is_low, value[30:32], value[8:10])
+        return carry
+
+    lax.fori_loop(0, ext, send, 0, unroll=UNROLL)
+
+
+def finish_kernel(where_ref, v1, v2, coeffs, force, diag, boundary, out, now, later):
+    is_press = where_ref[0] == 0
+    is_low = where_ref[1] == 0
+    ext = v2.shape[0] - 2
+    side = XH // 2
+    rim_at = pl.multiple_of(jnp.where(is_low, 32, 0), 8)
+    blank = jnp.zeros(v2.shape[1:], jnp.float32)
+    for ref in (now, later):
+        ref[0] = blank
+        ref[ext + 1] = blank
+
+    def fill(e, carry):
+        now[e + 1] = v2[e + 1]
+        now[e + 1, pl.ds(rim_at, 8), :] = placed_pair(boundary[:, lanes_at(e)], is_low)
+        return carry
+
+    lax.fori_loop(0, ext, fill, 0, unroll=UNROLL)
+    chebyshev, explicit = sweep_weights()
+
+    def put_out(e, value):
+        out[0, :, lanes_at(e - side)] = jnp.where(is_low, value[0:32], value[8:40])
+
+    for chosen, weights, centre in (
+        (is_press, chebyshev, None),
+        (jnp.logical_not(is_press), explicit, diag),
+    ):
+
+        @pl.when(chosen)
+        def _(weights=weights, centre=centre):
+            (w2, u2), (w3, u3) = weights[2:]
+            sweep((0, ext), coeffs, force, centre, now, v1, store_in(later), w2, u2)
+            sweep((side, ext - side), coeffs, force, centre, later, now, put_out, w3, u3)
+
+
+def regrouped(pieces):
+    lane = lane_index(pieces[0].shape)
+    result = []
+    for q in range(4):
+        value = None
+        for place in range(4):
+            piece = pieces[place]
+            if place != q:
+                piece = pltpu.roll(piece, ((place - q) * 32) % LANES, 1)
+            value = piece if value is None else jnp.where(lane >= place * 32, piece, value)
+        result.append(value)
+    return result
+
+
+def faces_kernel(where_ref, own, other_a, other_b, faces, out, field, rim):
+    is_press = where_ref[0] == 0
+    is_low = where_ref[1] == 0
+    tiles = out.shape[3] // LANES
+    groups = tiles // 4
+    half = groups // 2
+    side = XH // 2
+    extra = groups * 2 * LANES
+    extra_other = half * 2 * LANES
+    own_at = pl.multiple_of(jnp.where(is_low, 0, 8), 8)
+
+    def ordered(mine, theirs):
+        return [jnp.where(is_low, mine, theirs), jnp.where(is_low, theirs, mine)]
+
+    pieces = []
+    for par in range(2):
+        pieces += ordered(
+            own[par * groups : (par + 1) * groups, extra : extra + LANES],
+            other_b[par * groups : (par + 1) * groups, extra_other : extra_other + LANES],
+        )
+    for q, value in enumerate(regrouped(pieces)):
+        rim[q] = value
+    plane = ordered(own[:, extra + LANES :], other_b[:, extra_other + LANES :])
+    lane = lane_index((32, LANES))
+    field[tiles, 0:32, :] = jnp.where(lane < 32, plane[0], pltpu.roll(plane[1], 32, 1))
+
+    def gather(other, first):
+        def step(group, carry):
+            pieces = []
+            for par in range(2):
+                pieces += ordered(
+                    own[:, lanes_at(group + first, par * groups * LANES)],
+                    other[:, lanes_at(group, par * half * LANES)],
+                )
+            for q, value in enumerate(regrouped(pieces)):
+                field[4 * (group + first) + q, 0:32, :] = value
+                field[4 * (group + first) + q, 32:33, :] = rim[q, pl.ds(group + first, 1), :]
+            return carry
+
+        lax.fori_loop(0, half, step, 0, unroll=UNROLL)
+
+    gather(other_a, 0)
+    gather(other_b, half)
+    low_lanes = lane < HALF
+    not_last = lane % W != W - 1
+
+    def around(t):
+        value = field[t]
+        here = value[0:32]
+        after = field[t + 1, 0:32, :]
+        return here, (
+            next_row(value)[0:32],
+            jnp.where(low_lanes, half_turn(here), half_turn(after)),
+            next_lane(here),
+        )
+
+    @pl.when(is_press)
+    def _():
+        def step(t, carry):
+            here, others = around(t)
+            others = (others[0], others[1], jnp.where(not_last, others[2], 0.0))
+            for dim in range(3):
+                out[0, dim, :, lanes_at(t)] = face_mean(here, others[dim])
+            return carry
+
+        lax.fori_loop(0, tiles, step, 0, unroll=UNROLL)
+
+    @pl.when(jnp.logical_not(is_press))
+    def _():
+        def step(t, carry):
+            here, others = around(t)
+            for dim in range(3):
+                mean = faces[dim, t + side + 1, pl.ds(own_at, 32), :]
+                out[0, dim, :, lanes_at(t)] = mean * (here - others[dim])
+            return carry
+
+        lax.fori_loop(0, tiles, step, 0, unroll=UNROLL)
+
+
+def paired_body(states, coupled, facies, injectors, producers, perm_table, cond_table):
+    rows, cols = states.shape[1], states.shape[2]
+    tiles = cols // LANES
+    ext = tiles + XH
+    wide = XH * W
+    groups = tiles // 4
+    place = jnp.stack([lax.axis_index("code"), lax.axis_index("ba")]).astype(jnp.int32)
+    count = lax.axis_size("aa")
+    up = [(i, i + 1) for i in range(count - 1)]
+    down = [(b, a) for a, b in up]
+    swap = [(0, 1), (1, 0)]
+    up_across = [(2 * a + c, 2 * b + 1 - c) for a, b in up for c in range(2)]
+    down_across = [(b, a) for a, b in up_across]
+    opposite = [(0, 3), (1, 2), (2, 1), (3, 0)]
+    f32, i32 = jnp.float32, jnp.int32
+    states, coupled, facies, injectors, producers = [
+        pltpu.with_memory_space_constraint(value, pltpu.HBM)
+        for value in (states, coupled, facies, injectors, producers)
+    ]
+
+    to_right, to_left, across, across_right, across_left = pl.pallas_call(
+        edges_kernel,
+        out_shape=[
+            in_vmem((rows, 7 * wide)),
+            in_vmem((rows, 7 * wide)),
+            in_vmem((2, 5 * cols)),
+            in_vmem((2, 5 * wide)),
+            in_vmem((2, 5 * wide)),
+        ],
+        in_specs=[SM] + [HB] * 5,
+        out_specs=[VM] * 5,
+        scratch_shapes=[
+            pltpu.VMEM((4, rows, wide), f32),
+            pltpu.VMEM((4, rows, wide), f32),
+            pltpu.VMEM((4, 8, cols), f32),
+            pltpu.VMEM((3, rows, wide), i32),
+            pltpu.VMEM((3, rows, wide), i32),
+            pltpu.VMEM((3, 8, cols), i32),
+            pltpu.SemaphoreType.DMA((21,)),
+        ],
+        compiler_params=LEAN,
+        cost_estimate=cost(1),
+        name="edges",
+    )(place, states, coupled, facies, injectors, producers)
+    from_left = held(lax.ppermute(to_right, "aa", up))
+    from_right = held(lax.ppermute(to_left, "aa", down))
+    from_across = held(lax.ppermute(across, "ba", swap))
+    corner_left = held(lax.ppermute(across_right, ("aa", "ba"), up_across))
+    corner_right = held(lax.ppermute(across_left, ("aa", "ba"), down_across))
+
+    st, cp, fa, ij, pr, turned_own, turned_a, turned_b = pl.pallas_call(
+        turn_kernel,
+        out_shape=[
+            in_vmem(states.shape),
+            in_vmem(coupled.shape),
+            pltpu.VMEM(facies.shape, i32),
+            pltpu.VMEM(facies.shape, i32),
+            pltpu.VMEM(facies.shape, i32),
+            in_vmem((32, (2 * groups + 2) * LANES)),
+            in_vmem((32, groups * LANES)),
+            in_vmem((32, (groups + 2) * LANES)),
+        ],
+        in_specs=[SM] + [HB] * 5,
+        out_specs=[VM] * 8,
+        scratch_shapes=[pltpu.SemaphoreType.DMA((5,))],
+        compiler_params=LEAN,
+        cost_estimate=cost(3),
+        name="turn",
+    )(place, states, coupled, facies, injectors, producers)
+    other_a = held(lax.ppermute(turned_a, ("code", "ba"), opposite))
+    turned_own, turned_b = pl.pallas_call(
+        plane_kernel,
+        out_shape=[in_vmem(turned_own.shape), in_vmem(turned_b.shape)],
+        in_specs=[SM] + [VM] * 7,
+        out_specs=[VM] * 2,
+        compiler_params=LEAN,
+        cost_estimate=cost(1),
+        name="plane",
+    )(
+        place, from_right, turned_own, turned_b, from_left, from_across, corner_left, corner_right
+    )
+    other_b = held(lax.ppermute(turned_b, ("code", "ba"), opposite))
+    own = held(lax.ppermute(turned_own, "code", swap))
+
+    field = (ext + 2, rows + 8, LANES)
+    v1, v2, coeffs, force, diag, faces, boundary = pl.pallas_call(
+        main_kernel,
+        out_shape=[
+            in_vmem(field),
+            in_vmem(field),
+            in_vmem((6,) + field),
+            in_vmem(field),
+            in_vmem(field),
+            in_vmem((3,) + field),
+            in_vmem((2, ext * LANES)),
+        ],
+        in_specs=[SM, SM, SM] + [VM] * 10,
+        out_specs=[VM] * 7,
+        scratch_shapes=[pltpu.VMEM(field, f32)] * 9,
+        compiler_params=params(18),
+        cost_estimate=cost(12),
+        name="main",
+    )(
+        place, perm_table, cond_table, st, cp, fa, ij, pr,
+        from_left, from_right, from_across, corner_left, corner_right,
+    )
+    boundary = held(lax.ppermute(boundary, "ba", swap))
+    stepped = pl.pallas_call(
+        finish_kernel,
+        out_shape=jax.ShapeDtypeStruct(states.shape, f32),
+        in_specs=[SM] + [VM] * 6,
+        out_specs=VM,
+        scratch_shapes=[pltpu.VMEM(field, f32)] * 2,
+        compiler_params=params(8),
+        cost_estimate=cost(6),
+        name="finish",
+    )(place, v1, v2, coeffs, force, diag, boundary)
+    received = pl.pallas_call(
+        faces_kernel,
+        out_shape=jax.ShapeDtypeStruct(coupled.shape, f32),
+        in_specs=[SM] + [VM] * 4,
+        out_specs=VM,
+        scratch_shapes=[
+            pltpu.VMEM((tiles + 1, rows + 8, LANES), f32),
+            pltpu.VMEM((4, groups, LANES), f32),
+        ],
+        compiler_params=params(8),
+        cost_estimate=cost(5),
+        name="faces",
+    )(place, own, other_a, other_b, faces)
+    return (stepped, received)
+
+
 def solution(mesh):
+    paired = mesh.shape["ba"] == 2 and mesh.shape["code"] == 2
     return jax.shard_map(
-        body,
+        paired_body if paired else body,
         mesh=mesh,
         in_specs=(
             P("code", "ba", "aa"),

time: 279 us -> 60.8 us (0.22)
  other arithmetic: 116 us -> 0.08 us
  local copies, waits for them, and re-layouts: 63 us -> 0.01 us
  starting transfers between devices: 58.4 us -> 18.7 us
  Pallas kernels: 0 us -> 38.1 us
  waiting for transfers between devices: 37 us -> 2.93 us
    pallas_call x0 -> x6, Pallas kernels: none -> 38.1 us  [the longest x1 19 us: paired_body(): pl.pallas_call(main_kernel, out_shape=[in_vmem(field), in_vmem(field), in...]
    ppermute x21 -> x9, starting transfers between devices: 53.2 us -> 18.7 us  [the longest x1 4.86 us: paired_body(): corner_right = held(lax.ppermute(across_left, ('aa', 'ba'), down_across))]
    concatenate x8 -> x0, other arithmetic: 27.3 us -> none  [the longest x7 21.8 us: extended(): block = jnp.concatenate([low, block, high], axis=dim)]
    mul x2 -> x0, other arithmetic: 27.2 us -> none  [the longest x1 17.1 us: beside(): values[..., 1:row_count - 1, W - 1:col_count - W - 1] * lower_mask]
    all_to_all x1 -> x0, waiting for transfers between devices: 23.3 us -> none  [body(): lax.all_to_all(payload, 'ba', split_axis=3, concat_axis=1, tiled=True)]
    add x3 -> x0, other arithmetic: 21.1 us -> none  [the longest x1 10.7 us: heat_terms(): diagonal_entries = accumulate(conduct_faces) + outflow + center[4]]
    broadcast_in_dim x4 -> x0, other arithmetic: 19 us -> none  [the longest x3 12.5 us: body(): widened = extend(present_iterate[None], halo_depth)[0]]
    reshape x3 -> x0, local copies, waits for them, and re-layouts: 18.4 us -> none  [the longest x2 12.6 us: body(): payload = outgoing[::-1].reshape(3, row_count, col_count // W, W)]
  transfers between devices with their start and end apart: 22 -> 9, of which waited for: 7 -> 1; matrix products, arithmetic and copies ran while one was open for 24% -> 0% of each run, Pallas kernels for 0% -> 49%
where the time goes in v1:
time: 60.8 us; the launch traced here: 60.6 us
  Pallas kernels  38.1 us (63%)
  starting transfers between devices  18.7 us (31%)
  waiting for transfers between devices  2.93 us (5%)
  between operations  0.75 us (1%)
    pallas_call x1, Pallas kernels, paired_body(): pl.pallas_call(main_kernel, out_shape=[in_vmem(field), in_vmem(field), in...  19 us
    pallas_call x1, Pallas kernels, paired_body(): pl.pallas_call(finish_kernel, out_shape=jax.ShapeDtypeStruct(states.shape...  6.66 us
    pallas_call x1, Pallas kernels, paired_body(): pl.pallas_call(faces_kernel, out_shape=jax.ShapeDtypeStruct(coupled.shape...  5.33 us
    ppermute x1, starting transfers between devices, paired_body(): corner_right = held(lax.ppermute(across_left, ('aa', 'ba'), down_across))  4.86 us
    pallas_call x1, Pallas kernels, paired_body(): pl.pallas_call(turn_kernel, out_shape=[in_vmem(states.shape), in_vmem(cou...  3.82 us
    ppermute x1, starting transfers between devices, paired_body(): from_left = held(lax.ppermute(to_right, 'aa', up))  3.14 us
    ppermute x1, starting transfers between devices, paired_body(): from_right = held(lax.ppermute(to_left, 'aa', down))  3.03 us
    ppermute x1, waiting for transfers between devices, paired_body(): boundary = held(lax.ppermute(boundary, 'ba', swap))  2.9 us
  transfers between devices with their start and end apart: 9, of which 1 were waited for; matrix products, arithmetic and copies ran while one was open for 0% of the time, Pallas kernels for 49%

profile of v1, /device:TPU:9, one launch (start us, length us, event | category | flops | bytes accessed | tf_op | source)
XLA Modules:
  0.0 60.6 jit_solution(5985544450611433435)
XLA Ops:
  0.6 0.1 pad_add_fusion.where_ref
  0.7 2.6 %edges.1 = (f32[32,1792]{1,0:T(8,128)S(1)}, f32[32,1792]{1,0:T(8,128)S(1)}, f32[2,40960]{1,0:T(2,128)S(1)}, f32[2,1280]{1,0:T(2,128)S(1)}, f32[2,1280]{1,0:T(2,128)S(1)}) custom-call(s32[2]{0:T(128)S(1)} %pad_add_fusion.where_ref, f32[1,32,8192]{2,1,0:T(8,128)} %st.1, f32[1,3,32,8192]{3,2,1,0:T(8,128)} %cp.1, s32[1,32,8192]{2,1,0:T(8,128)} %fa.1, ...), custom_call_target="tpu_custom_call" | custom-call | bytes 3200000 | tf_op jit(solution)/shard_map/edges/pallas_call | solution.py:814
  3.3 1.3 %collective-permute-start.2 = (f32[2,40960]{1,0:T(2,128)S(1)}, f32[2,40960]{1,0:T(2,128)S(1)}, u32[]{:S(2)}, u32[]{:S(2)}) collective-permute-start(f32[2,40960]{1,0:T(2,128)S(1)} %get-tuple-element.31), channel_id=1, source_target_pairs={{0,1},{1,0},{2,3},{3,2},{4,5},{5,4},{6,7},{7,6},{8,9},{9,8},{10,11... | collective-permute-start | bytes 983048 | tf_op jit(solution)/shard_map/ppermute | solution.py:840
  4.6 3.1 %collective-permute-start = (f32[32,1792]{1,0:T(8,128)S(1)}, f32[32,1792]{1,0:T(8,128)S(1)}, u32[]{:S(2)}, u32[]{:S(2)}) collective-permute-start(f32[32,1792]{1,0:T(8,128)S(1)} %get-tuple-element.29), channel_id=1, source_target_pairs={{0,2},{2,4},{4,6},{6,8},{8,10},{10,12},{12,14},{1,3},{3,5},{5,7},{... | collective-permute-start | bytes 688136 | tf_op jit(solution)/shard_map/ppermute | solution.py:838
  7.7 3.0 %collective-permute-start.1 = (f32[32,1792]{1,0:T(8,128)S(1)}, f32[32,1792]{1,0:T(8,128)S(1)}, u32[]{:S(2)}, u32[]{:S(2)}) collective-permute-start(f32[32,1792]{1,0:T(8,128)S(1)} %get-tuple-element.30), channel_id=1, source_target_pairs={{2,0},{4,2},{6,4},{8,6},{10,8},{12,10},{14,12},{3,1},{5,3},{7,5},{... | collective-permute-start | bytes 688136 | tf_op jit(solution)/shard_map/ppermute | solution.py:839
  10.8 2.2 %collective-permute-start.3 = (f32[2,1280]{1,0:T(2,128)S(1)}, f32[2,1280]{1,0:T(2,128)S(1)}, u32[]{:S(2)}, u32[]{:S(2)}) collective-permute-start(f32[2,1280]{1,0:T(2,128)S(1)} %get-tuple-element.32), channel_id=1, source_target_pairs={{0,3},{1,2},{2,5},{3,4},{4,7},{5,6},{6,9},{7,8},{8,11},{9,10},{10,... | collective-permute-start | bytes 30728 | tf_op jit(solution)/shard_map/ppermute | solution.py:841
  13.0 0.0 copy-start
  13.0 0.0 copy-start.1
  13.0 4.9 %collective-permute-start.4 = (f32[2,1280]{1,0:T(2,128)S(1)}, f32[2,1280]{1,0:T(2,128)S(1)}, u32[]{:S(2)}, u32[]{:S(2)}) collective-permute-start(f32[2,1280]{1,0:T(2,128)S(1)} %get-tuple-element.33), channel_id=1, source_target_pairs={{3,0},{2,1},{5,2},{4,3},{7,4},{6,5},{9,6},{8,7},{11,8},{10,9},{13,... | collective-permute-start | bytes 30728 | tf_op jit(solution)/shard_map/ppermute | solution.py:842
  17.9 3.8 %turn.1 = (f32[1,32,8192]{2,1,0:T(8,128)S(1)}, f32[1,3,32,8192]{3,2,1,0:T(8,128)S(1)}, s32[1,32,8192]{2,1,0:T(8,128)S(1)}, s32[1,32,8192]{2,1,0:T(8,128)S(1)}, s...) custom-call(s32[2]{0:T(128)S(1)} %pad_add_fusion.where_ref, ...), custom_call_target="tpu_custom_call" | custom-call | bytes 9600000 | tf_op jit(solution)/shard_map/turn/pallas_call | solution.py:844
  21.7 0.0 collective-permute-done.3.corner_left.rest_2_
  21.7 0.0 collective-permute-done.4.corner_right.rest_3_
  21.8 0.0 collective-permute-done.from_left.rest_0_
  21.8 0.0 collective-permute-done.1.from_right
  21.8 0.0 collective-permute-done.2.across.rest_1_
  21.8 0.6 %plane.1 = (f32[32,4352]{1,0:T(8,128)S(1)}, f32[32,2304]{1,0:T(8,128)S(1)}) custom-call(s32[2]{0:T(128)S(1)} %pad_add_fusion.where_ref, f32[32,1792]{1,0:T(8,128)S(1)} %collective-permute-done.1.from_right, f32[32,4352]{1,0:T(8,128)S(1)} %get-tuple-element.40.own_in, f32[32,2304]{1,0:T(8,128)S(1)} %get-tuple-element.41.other_in, ...), custom_call_target="tpu_custom_call" | custom-call | bytes 3200000 | tf_op jit(solution)/shard_map/plane/pallas_call | solution.py:864
  22.4 2.1 %collective-permute-start.6 = (f32[32,4352]{1,0:T(8,128)S(1)}, f32[32,4352]{1,0:T(8,128)S(1)}, u32[]{:S(2)}, u32[]{:S(2)}) collective-permute-start(f32[32,4352]{1,0:T(8,128)S(1)} %get-tuple-element.42), channel_id=1, source_target_pairs={{0,16},{16,0},{1,17},{17,1},{2,18},{18,2},{3,19},{19,3},{4,20},{20... | collective-permute-start | bytes 1671176 | tf_op jit(solution)/shard_map/ppermute | solution.py:876
  24.6 0.2 collective-permute-start.8
  24.8 1.5 %collective-permute-start.7 = (f32[32,2048]{1,0:T(8,128)S(1)}, f32[32,2048]{1,0:T(8,128)S(1)}, u32[]{:S(2)}, u32[]{:S(2)}) collective-permute-start(f32[32,2048]{1,0:T(8,128)S(1)} %get-tuple-element.43), channel_id=1, source_target_pairs={{0,17},{1,16},{16,1},{17,0},{2,19},{3,18},{18,3},{19,2},{4,21},{5,... | collective-permute-start | bytes 786440 | tf_op jit(solution)/shard_map/ppermute | solution.py:863
  26.3 0.0 copy-done
  26.3 0.0 copy-done.1
  26.3 19.0 %main.1 = (f32[70,40,128]{2,1,0:T(8,128)S(1)}, f32[70,40,128]{2,1,0:T(8,128)S(1)}, f32[6,70,40,128]{3,2,1,0:T(8,128)S(1)}, f32[70,40,128]{2,1,0:T(8,128)S(1)}, f...) custom-call(s32[2]{0:T(128)S(1)} %pad_add_fusion.where_ref, f32[6]{0:T(128)S(1)} %copy-done, ...), custom_call_target="tpu_custom_call" | custom-call | bytes 38400000 | tf_op jit(solution)/shard_map/main/pallas_call | solution.py:879
  45.3 0.3 collective-permute-start.5
  45.7 2.9 %collective-permute-done.5.boundary = f32[2,8704]{1,0:T(2,128)S(1)} collective-permute-done((f32[2,8704]{1,0:T(2,128)S(1)}, f32[2,8704]{1,0:T(2,128)S(1)}, u32[]{:S(2)}, u32[]{:S(2)}) %collective-permute-start.5) | collective-permute-done | bytes 69664 | tf_op jit(solution)/shard_map/ppermute | solution.py:900
  48.6 6.7 %finish.1 = f32[1,32,8192]{2,1,0:T(8,128)} custom-call(s32[2]{0:T(128)S(1)} %pad_add_fusion.where_ref, f32[70,40,128]{2,1,0:T(8,128)S(1)} %get-tuple-element.34.v1, f32[70,40,128]{2,1,0:T(8,128)S(1)} %get-tuple-element.35.v2, f32[6,70,40,128]{3,2,1,0:T(8,128)S(1)} %get-tuple-element.36.coeffs, f32[70,40,128]{2,1,0:T(8,128)S(1)} %get-tuple-element.37.force, ...), custom_call_target="tpu_custom_call" | custom-call | bytes 19200000 | tf_op jit(solution)/shard_map/finish/pallas_call | solution.py:901
  55.2 0.0 collective-permute-done.7.other_a
  55.2 0.0 collective-permute-done.8.other_b
  55.2 0.0 collective-permute-done.6.own
  55.2 5.3 %faces.1 = f32[1,3,32,8192]{3,2,1,0:T(8,128)} custom-call(s32[2]{0:T(128)S(1)} %pad_add_fusion.where_ref, f32[32,4352]{1,0:T(8,128)S(1)} %collective-permute-done.6.own, f32[32,2048]{1,0:T(8,128)S(1)} %collective-permute-done.7.other_a, f32[32,2304]{1,0:T(8,128)S(1)} %collective-permute-done.8.other_b, f32[3,70,40,128]{3,2,1,0:T(8,128)S(1)} %get-tuple-element.45.faces), custom_call_target="tpu_custom_call" | custom-call | bytes 16000000 | tf_op jit(solution)/shard_map/faces/pallas_call | solution.py:911
Async XLA Ops:
  3.3 18.5 %collective-permute-start.2 = (f32[2,40960]{1,0:T(2,128)S(1)}, f32[2,40960]{1,0:T(2,128)S(1)}, u32[]{:S(2)}, u32[]{:S(2)}) collective-permute-start(f32[2,40960]{1,0:T(2,128)S(1)} %get-tuple-element.31), channel_id=1, source_target_pairs={{0,1},{1,0},{2,3},{3,2},{4,5},{5,4},{6,7},{7,6},{8,9},{9,8},{10,11... | collective-permute-start | bytes 983048 | tf_op jit(solution)/shard_map/ppermute | solution.py:840
  4.6 17.2 %collective-permute-start = (f32[32,1792]{1,0:T(8,128)S(1)}, f32[32,1792]{1,0:T(8,128)S(1)}, u32[]{:S(2)}, u32[]{:S(2)}) collective-permute-start(f32[32,1792]{1,0:T(8,128)S(1)} %get-tuple-element.29), channel_id=1, source_target_pairs={{0,2},{2,4},{4,6},{6,8},{8,10},{10,12},{12,14},{1,3},{3,5},{5,7},{... | collective-permute-start | bytes 688136 | tf_op jit(solution)/shard_map/ppermute | solution.py:838
  7.7 14.0 %collective-permute-start.1 = (f32[32,1792]{1,0:T(8,128)S(1)}, f32[32,1792]{1,0:T(8,128)S(1)}, u32[]{:S(2)}, u32[]{:S(2)}) collective-permute-start(f32[32,1792]{1,0:T(8,128)S(1)} %get-tuple-element.30), channel_id=1, source_target_pairs={{2,0},{4,2},{6,4},{8,6},{10,8},{12,10},{14,12},{3,1},{5,3},{7,5},{... | collective-permute-start | bytes 688136 | tf_op jit(solution)/shard_map/ppermute | solution.py:839
  10.8 11.0 %collective-permute-start.3 = (f32[2,1280]{1,0:T(2,128)S(1)}, f32[2,1280]{1,0:T(2,128)S(1)}, u32[]{:S(2)}, u32[]{:S(2)}) collective-permute-start(f32[2,1280]{1,0:T(2,128)S(1)} %get-tuple-element.32), channel_id=1, source_target_pairs={{0,3},{1,2},{2,5},{3,4},{4,7},{5,6},{6,9},{7,8},{8,11},{9,10},{10,... | collective-permute-start | bytes 30728 | tf_op jit(solution)/shard_map/ppermute | solution.py:841
  13.0 13.3 %copy-start = (f32[6]{0:T(128)S(1)}, f32[6]{0:T(128)}, u32[]{:S(2)}) copy-start(f32[6]{0:T(128)} %perm_ref.1) | copy-start | bytes 76
  13.0 13.3 %copy-start.1 = (f32[6]{0:T(128)S(1)}, f32[6]{0:T(128)}, u32[]{:S(2)}) copy-start(f32[6]{0:T(128)} %cond_ref.1) | copy-start | bytes 76
  13.0 8.7 %collective-permute-start.4 = (f32[2,1280]{1,0:T(2,128)S(1)}, f32[2,1280]{1,0:T(2,128)S(1)}, u32[]{:S(2)}, u32[]{:S(2)}) collective-permute-start(f32[2,1280]{1,0:T(2,128)S(1)} %get-tuple-element.33), channel_id=1, source_target_pairs={{3,0},{2,1},{5,2},{4,3},{7,4},{6,5},{9,6},{8,7},{11,8},{10,9},{13,... | collective-permute-start | bytes 30728 | tf_op jit(solution)/shard_map/ppermute | solution.py:842
  22.4 32.8 %collective-permute-start.6 = (f32[32,4352]{1,0:T(8,128)S(1)}, f32[32,4352]{1,0:T(8,128)S(1)}, u32[]{:S(2)}, u32[]{:S(2)}) collective-permute-start(f32[32,4352]{1,0:T(8,128)S(1)} %get-tuple-element.42), channel_id=1, source_target_pairs={{0,16},{16,0},{1,17},{17,1},{2,18},{18,2},{3,19},{19,3},{4,20},{20... | collective-permute-start | bytes 1671176 | tf_op jit(solution)/shard_map/ppermute | solution.py:876
  24.6 30.7 %collective-permute-start.8 = (f32[32,2304]{1,0:T(8,128)S(1)}, f32[32,2304]{1,0:T(8,128)S(1)}, u32[]{:S(2)}, u32[]{:S(2)}) collective-permute-start(f32[32,2304]{1,0:T(8,128)S(1)} %get-tuple-element.44), channel_id=1, source_target_pairs={{0,17},{1,16},{16,1},{17,0},{2,19},{3,18},{18,3},{19,2},{4,21},{5,... | collective-permute-start | bytes 884744 | tf_op jit(solution)/shard_map/ppermute | solution.py:875
  24.8 30.4 %collective-permute-start.7 = (f32[32,2048]{1,0:T(8,128)S(1)}, f32[32,2048]{1,0:T(8,128)S(1)}, u32[]{:S(2)}, u32[]{:S(2)}) collective-permute-start(f32[32,2048]{1,0:T(8,128)S(1)} %get-tuple-element.43), channel_id=1, source_target_pairs={{0,17},{1,16},{16,1},{17,0},{2,19},{3,18},{18,3},{19,2},{4,21},{5,... | collective-permute-start | bytes 786440 | tf_op jit(solution)/shard_map/ppermute | solution.py:863
  45.3 3.2 %collective-permute-start.5 = (f32[2,8704]{1,0:T(2,128)S(1)}, f32[2,8704]{1,0:T(2,128)S(1)}, u32[]{:S(2)}, u32[]{:S(2)}) collective-permute-start(f32[2,8704]{1,0:T(2,128)S(1)} %get-tuple-element.39), channel_id=1, source_target_pairs={{0,1},{1,0},{2,3},{3,2},{4,5},{5,4},{6,7},{7,6},{8,9},{9,8},{10,11... | collective-permute-start | bytes 208904 | tf_op jit(solution)/shard_map/ppermute | solution.py:900

commit v2 on v1

--- a/solution.py
+++ b/solution.py
@@ -254,6 +254,7 @@
 SM = pl.BlockSpec(memory_space=pltpu.SMEM)
 HB = pl.BlockSpec(memory_space=pltpu.HBM)
 UNROLL = 4
+PARTS = 4
 LEAN = pltpu.CompilerParams(vmem_limit_bytes=6 * 2**20)
 
 
@@ -313,16 +314,11 @@
     return pltpu.roll(value, 1, 0)
 
 
-def class_table(table_ref, shape):
-    lane = lane_index(shape)
-    table = jnp.zeros(shape, jnp.float32)
+def look_up(table, codes):
+    value = jnp.zeros(codes.shape, jnp.float32)
     for index_c in range(NF):
-        table = jnp.where(lane == index_c + 1, table_ref[index_c], table)
-    return table
-
-
-def look_up(table, codes):
-    return jnp.take_along_axis(table, codes, axis=1)
+        value = jnp.where(codes == index_c + 1, table[index_c], value)
+    return value
 
 
 def placed_pair(pair, is_low):
@@ -338,7 +334,7 @@
 
 
 def edges_kernel(
-    where_ref, st, cp, fa, ij, pr, to_right, to_left, across, across_right, across_left,
+    where_ref, st, cp, fa, ij, pr, to_right, to_left, across, corners,
     left_f, right_f, row_f, left_i, right_i, row_i, sems,
 ):
     is_low = where_ref[1] == 0
@@ -393,13 +389,51 @@
     ]
     for index, slot in enumerate(slots):
         across[:, index * cols : (index + 1) * cols] = slot
-        across_right[:, index * wide : (index + 1) * wide] = slot[:, cols - wide :]
-        across_left[:, index * wide : (index + 1) * wide] = slot[:, :wide]
+        corners[:, 2 * index * wide : (2 * index + 1) * wide] = slot[:, :wide]
+        corners[:, (2 * index + 1) * wide : (2 * index + 2) * wide] = slot[:, cols - wide :]
+
+
+def pack_kernel(right_in, left_in, across_in, corners, to_right, to_left, across):
+    across[...] = across_in[...]
+    wide = XH * W
+    for side, (source, target) in enumerate(((left_in, to_left), (right_in, to_right))):
+        target[:, : 7 * wide] = source[...]
+        target[:, 7 * wide :] = jnp.zeros((32, LANES), jnp.float32)
+        for index in range(5):
+            for row in range(2):
+                for half in range(2):
+                    start = (2 * index + side) * wide + half * LANES
+                    place = index * 4 + row * 2 + half
+                    target[place : place + 1, 7 * wide :] = corners[
+                        row : row + 1, start : start + LANES
+                    ]
+
+
+def put_cells(refs, is_press, tables, e, rows, cells):
+    v0, prop, rock, c0, c1, c2, src, snk = refs
+    state, codes, f0, f1, f2, inject, produce = cells
+    v0[e + 1, rows, :] = state
+    prop[e + 1, rows, :] = look_up(tables[0], codes)
+    rock[e + 1, rows, :] = look_up(tables[1], codes)
+    c0[e + 1, rows, :] = f0
+    c1[e + 1, rows, :] = f1
+    c2[e + 1, rows, :] = f2
+    src[e + 1, rows, :] = jnp.where(is_press, 2.0 * inject - produce, 0.1 * inject)
+    snk[e + 1, rows, :] = jnp.where(is_press, produce, produce + inject)
+
+
+def class_tables(is_press, perm_ref, cond_ref):
+    perm = [perm_ref[index_c] for index_c in range(NF)]
+    own = [jnp.where(is_press, perm[index_c], cond_ref[index_c]) for index_c in range(NF)]
+    return own, perm
 
 
 def turn_kernel(
-    where_ref, st_in, cp_in, fa_in, ij_in, pr_in, st, cp, fa, ij, pr, own, other_a, other_b, sems
+    where_ref, perm_ref, cond_ref, st_in, cp_in, fa_in, ij_in, pr_in, corners,
+    own, other, fluid, v0, prop, rock, c0, c1, c2, src, snk,
+    st, cp, fa, ij, pr, sems,
 ):
+    del corners
     copies = [
         pltpu.make_async_copy(source, target, sems.at[index])
         for index, (source, target) in enumerate(
@@ -411,8 +445,8 @@
     copies[0].wait()
     is_heat = where_ref[0] == 1
     is_low = where_ref[1] == 0
+    own_rows = pl.ds(pl.multiple_of(jnp.where(is_low, 0, 8), 8), 32)
     groups = st.shape[2] // (4 * LANES)
-    half = groups // 2
     extra = groups * 2 * LANES
     row = lax.broadcasted_iota(jnp.int32, (32, LANES), 0)
 
@@ -421,6 +455,8 @@
             [st[0, :, lanes_at(4 * group + q)] for q in range(4)], axis=0
         )
         tall = jnp.where(is_heat, flowability(tall), tall)
+        for q in range(4):
+            fluid[4 * group + q + XH // 2 + 1, own_rows, :] = tall[32 * q : 32 * q + 32]
         turned = tall.T
         for par in range(2):
             low = turned[par * HALF : par * HALF + 32]
@@ -429,25 +465,33 @@
             away = jnp.where(is_low, high, low)
             rim = high[0:1]
 
-            @pl.when(group < half)
-            def _(away=away, par=par):
-                other_a[:, lanes_at(group, par * half * LANES)] = away
-
-            @pl.when(group >= half)
-            def _(away=away, par=par):
-                other_b[:, lanes_at(group - half, par * half * LANES)] = away
-
+            other[:, lanes_at(group, par * groups * LANES)] = away
             rims = jnp.where(row == par * groups + group, rim, rims)
         return rims
 
-    rims = lax.fori_loop(0, groups, step, jnp.zeros((32, LANES), jnp.float32), unroll=UNROLL)
+    rims = lax.fori_loop(0, groups, step, jnp.zeros((32, LANES), jnp.float32), unroll=8)
     own[:, extra : extra + LANES] = jnp.where(is_low, rims, 0.0)
-    other_b[:, half * 2 * LANES : half * 2 * LANES + LANES] = jnp.where(is_low, 0.0, rims)
+    other[:, extra : extra + LANES] = jnp.where(is_low, 0.0, rims)
     for copy in copies[1:]:
         copy.wait()
-
-
-def plane_kernel(where_ref, from_right, own_in, other_in, *rest):
+    refs = (v0, prop, rock, c0, c1, c2, src, snk)
+    is_press = where_ref[0] == 0
+    tables = class_tables(is_press, perm_ref, cond_ref)
+    tiles = st.shape[2] // LANES
+
+    def fill(t, carry):
+        at = lanes_at(t)
+        cells = (
+            st[0, :, at], fa[0, :, at] + 1, cp[0, 0, :, at], cp[0, 1, :, at], cp[0, 2, :, at],
+            ij[0, :, at].astype(jnp.float32), pr[0, :, at].astype(jnp.float32),
+        )
+        put_cells(refs, is_press, tables, t + XH // 2, own_rows, cells)
+        return carry
+
+    lax.fori_loop(0, tiles, fill, 0, unroll=8)
+
+
+def plane_kernel(where_ref, from_right, own_in, *rest):
     own, other = rest[-2:]
     is_heat = where_ref[0] == 1
     is_low = where_ref[1] == 0
@@ -458,9 +502,9 @@
     tall = jnp.concatenate([value, jnp.zeros((96, LANES), jnp.float32)], 0).T
     low, high = tall[0:32], tall[32:64]
     own[...] = own_in[...]
-    other[...] = other_in[...]
     own[:, own.shape[1] - LANES :] = jnp.where(is_low, low, high)
-    other[:, other.shape[1] - LANES :] = jnp.where(is_low, high, low)
+    other[...] = jnp.zeros(other.shape, jnp.float32)
+    other[:, :LANES] = jnp.where(is_low, high, low)
 
 
 def sweep(tiles, coeffs, force, diag, now, last, target, weight, pull):
@@ -489,7 +533,7 @@
 
     lax.fori_loop(
         first, stop, step, (half_turn(now[first]), half_turn(now[first + 1])),
-        unroll=UNROLL,
+        unroll=(stop - first) // 2,
     )
 
 
@@ -500,97 +544,74 @@
     return put
 
 
-def main_kernel(
-    where_ref, perm_ref, cond_ref, st, cp, fa, ij, pr,
-    from_left, from_right, across, corner_left, corner_right,
-    v1, v2, coeffs, force, diag, faces, boundary,
-    v0, prop, rock, c0, c1, c2, src, snk, fluid,
-):
-    is_press = where_ref[0] == 0
-    is_low = where_ref[1] == 0
-    cols = st.shape[2]
-    tiles = cols // LANES
-    ext = v0.shape[0] - 2
-    height = v0.shape[1]
-    wide = XH * W
-    side = XH // 2
-    own_at = pl.multiple_of(jnp.where(is_low, 0, 8), 8)
-    rim_at = pl.multiple_of(jnp.where(is_low, 32, 0), 8)
-    own_rows, rim_rows = pl.ds(own_at, 32), pl.ds(rim_at, 8)
-    perm = class_table(perm_ref, (32, LANES))
-    cond = class_table(cond_ref, (32, LANES))
-    own_table = jnp.where(is_press, perm, cond)
-
-    def put_cells(e, rows, state, codes, f0, f1, f2, inject, produce):
-        count = state.shape[0]
-        v0[e + 1, rows, :] = state
-        prop[e + 1, rows, :] = look_up(own_table[:count], codes)
-        rock[e + 1, rows, :] = look_up(perm[:count], codes)
-        c0[e + 1, rows, :] = f0
-        c1[e + 1, rows, :] = f1
-        c2[e + 1, rows, :] = f2
-        src[e + 1, rows, :] = jnp.where(is_press, 2.0 * inject - produce, 0.1 * inject)
-        snk[e + 1, rows, :] = jnp.where(is_press, produce, produce + inject)
-
-    def put_rim(e, message, slots, at):
-        def pair(index):
-            return placed_pair(message[:, lanes_at(at, index * slots)], is_low)
-
-        def near(index, row):
-            return placed_row(message[row : row + 1, lanes_at(at, index * slots)], is_low)
-
-        put_cells(
-            e, rim_rows, pair(0), pair(1).astype(jnp.int32), pair(2),
-            near(3, 0), near(3, 1), near(4, 0), near(4, 1),
-        )
-
-    def put_side(e, message, at):
-        parts = [message[:, lanes_at(at, index * wide)] for index in range(7)]
-        put_cells(e, own_rows, parts[0], parts[1].astype(jnp.int32), *parts[2:])
-
-    for ref in (v0, prop, rock):
-        for e in (0, ext + 1):
-            ref[e] = jnp.zeros((height, LANES), jnp.float32)
-    for ref in (v1, v2):
-        for e in (0, ext + 1):
-            ref[e] = jnp.zeros((height, LANES), jnp.float32)
-
-    def fill(t, carry):
-        at = lanes_at(t)
-        put_cells(
-            t + side, own_rows, st[0, :, at], fa[0, :, at] + 1,
-            cp[0, 0, :, at], cp[0, 1, :, at], cp[0, 2, :, at],
-            ij[0, :, at].astype(jnp.float32), pr[0, :, at].astype(jnp.float32),
-        )
-        put_rim(t + side, across, cols, t)
-        return carry
-
-    lax.fori_loop(0, tiles, fill, 0, unroll=UNROLL)
-    for at in range(side):
-        put_side(at, from_left, at)
-        put_rim(at, corner_left, wide, at)
-        put_side(tiles + side + at, from_right, at)
-        put_rim(tiles + side + at, corner_right, wide, at)
-
-    lane = lane_index((height, LANES))
+def rim_cells(is_low, read):
+    def pair(index):
+        return placed_pair(jnp.concatenate([read(index, 0), read(index, 1)], 0), is_low)
+
+    def near(index, row):
+        return placed_row(read(index, row), is_low)
+
+    return (
+        pair(0), pair(1).astype(jnp.int32), pair(2),
+        near(3, 0), near(3, 1), near(4, 0), near(4, 1),
+    )
+
+
+def rim_rows(is_low):
+    return pl.ds(pl.multiple_of(jnp.where(is_low, 32, 0), 8), 8)
+
+
+def put_level(fluid, cells, e, rows):
+    prop, state = cells[1][e + 1, rows, :], cells[0][e + 1, rows, :]
+    fluid[e + 1, rows, :] = jnp.where(prop > 0.0, flowability(state), 0.0)
+
+
+def clear(refs, places):
+    for ref in refs:
+        for e in places:
+            ref[e] = jnp.zeros(ref.shape[1:], jnp.float32)
+
+
+def face_terms(cells, made, is_press, ranges, long):
+    v0, prop, rock, c0, c1, c2, src, snk = cells
+    coeffs, force, diag, fluid = made
+    shape = v0.shape[1:]
+    lane = lane_index(shape)
     low_lanes = lane < HALF
     not_last = lane % W != W - 1
-
-    def next_cells(value, after):
+    blank = jnp.zeros(shape, jnp.float32)
+
+    def next_cells(value, here, after):
         return (
             next_row(value),
-            jnp.where(low_lanes, half_turn(value), half_turn(after)),
+            jnp.where(low_lanes, here, after),
             jnp.where(not_last, next_lane(value), 0.0),
         )
 
-    blank = jnp.zeros((height, LANES), jnp.float32)
-    chebyshev, explicit = sweep_weights()
+    def run(step, first, stop, start):
+        if stop - first > 8:
+            lax.fori_loop(first, stop, step, start(first), unroll=long)
+        else:
+            carry = start(first)
+            for e in range(first, stop):
+                carry = step(e, carry)
 
     @pl.when(is_press)
     def _():
-        def step(e, before):
+        def plus_along(e, here, after):
             value = prop[e + 1]
-            means = [face_mean(value, other) for other in next_cells(value, prop[e + 2])]
+            return face_mean(value, jnp.where(low_lanes, here, after)) * c1[e + 1]
+
+        def start(first):
+            here = half_turn(prop[first + 1])
+            if first == 0:
+                return blank, here
+            return half_turn(plus_along(first - 1, half_turn(prop[first]), here)), here
+
+        def step(e, carry):
+            before, here = carry
+            value, after = prop[e + 1], half_turn(prop[e + 2])
+            means = [face_mean(value, other) for other in next_cells(value, here, after)]
             plus = [mean * ref[e + 1] for mean, ref in zip(means, (c0, c1, c2))]
             turned = half_turn(plus[1])
             minus = [
@@ -604,57 +625,127 @@
                 coeffs[2 * dim, e + 1] = scale * plus[dim]
                 coeffs[2 * dim + 1, e + 1] = scale * minus[dim]
             force[e + 1] = scale * (src[e + 1] + STORAGE * v0[e + 1])
-            return turned
-
-        lax.fori_loop(0, ext, step, blank, unroll=UNROLL)
-        (w0, u0), (w1, u1) = chebyshev[:2]
-        sweep((0, ext), coeffs, force, None, v0, v0, store_in(v1), w0, u0)
-        sweep((0, ext), coeffs, force, None, v1, v0, store_in(v2), w1, u1)
+            return turned, after
+
+        for first, stop in ranges:
+            run(step, first, stop, start)
 
     @pl.when(jnp.logical_not(is_press))
     def _():
-        fluid[0] = blank
-        fluid[ext + 1] = blank
-
-        def levels(e, carry):
-            fluid[e + 1] = jnp.where(prop[e + 1] > 0.0, flowability(v0[e + 1]), 0.0)
-            return carry
-
-        lax.fori_loop(0, ext, levels, 0, unroll=UNROLL)
-
-        def step(e, before):
-            value = prop[e + 1]
-            means = [face_mean(value, other) for other in next_cells(value, prop[e + 2])]
-            value = fluid[e + 1]
-            flows = [face_mean(value, other) for other in next_cells(value, fluid[e + 2])]
-            value = rock[e + 1]
-            for dim, other in enumerate(next_cells(value, rock[e + 2])):
-                faces[dim, e + 1] = face_mean(value, other)
-            speed = [flow * ref[e + 1] for flow, ref in zip(flows, (c0, c1, c2))]
-            gain = [mean + jnp.maximum(rate, 0.0) for mean, rate in zip(means, speed)]
-            loss = [up - rate for up, rate in zip(gain, speed)]
-            turned = half_turn(gain[1]), half_turn(loss[1])
-            minus = [
-                prev_row(gain[0]),
-                jnp.where(low_lanes, before[0], turned[0]),
-                prev_lane(gain[2]),
+        def pair_of(mean, flow, field):
+            speed = flow * field
+            gain = mean + jnp.maximum(speed, 0.0)
+            return gain, gain - speed
+
+        def start(first):
+            here = [half_turn(ref[first + 1]) for ref in (prop, fluid)]
+            if first == 0:
+                return (blank, blank), here
+            means = [
+                face_mean(ref[first], jnp.where(low_lanes, half_turn(ref[first]), after))
+                for ref, after in zip((prop, fluid), here)
             ]
-            behind = [
-                prev_row(loss[0]),
-                jnp.where(low_lanes, before[1], turned[1]),
-                prev_lane(loss[2]),
-            ]
-            diag[e + 1] = accumulate(gain + behind) + snk[e + 1]
-            for dim in range(3):
-                coeffs[2 * dim, e + 1] = loss[dim]
-                coeffs[2 * dim + 1, e + 1] = minus[dim]
+            gain, loss = pair_of(means[0], means[1], c1[first])
+            return (half_turn(gain), half_turn(loss)), here
+
+        def step(e, carry):
+            before, here = carry
+            after = [half_turn(ref[e + 2]) for ref in (prop, fluid)]
+            value, level = prop[e + 1], fluid[e + 1]
+            total = snk[e + 1]
+            gain, loss = pair_of(
+                face_mean(value, next_row(value)), face_mean(level, next_row(level)), c0[e + 1]
+            )
+            coeffs[0, e + 1] = loss
+            coeffs[1, e + 1] = prev_row(gain)
+            total += gain + prev_row(loss)
+            gain, loss = pair_of(
+                face_mean(value, jnp.where(not_last, next_lane(value), 0.0)),
+                face_mean(level, jnp.where(not_last, next_lane(level), 0.0)),
+                c2[e + 1],
+            )
+            coeffs[4, e + 1] = loss
+            coeffs[5, e + 1] = prev_lane(gain)
+            total += gain + prev_lane(loss)
+            gain, loss = pair_of(
+                face_mean(value, jnp.where(low_lanes, here[0], after[0])),
+                face_mean(level, jnp.where(low_lanes, here[1], after[1])),
+                c1[e + 1],
+            )
+            turned = half_turn(gain), half_turn(loss)
+            coeffs[2, e + 1] = loss
+            coeffs[3, e + 1] = jnp.where(low_lanes, before[0], turned[0])
+            diag[e + 1] = total + gain + jnp.where(low_lanes, before[1], turned[1])
             force[e + 1] = src[e + 1]
-            return turned
-
-        lax.fori_loop(0, ext, step, (blank, blank), unroll=UNROLL)
-        (w0, u0), (w1, u1) = explicit[:2]
-        sweep((0, ext), coeffs, force, diag, v0, v0, store_in(v1), w0, u0)
-        sweep((0, ext), coeffs, force, diag, v1, v0, store_in(v2), w1, u1)
+            return turned, after
+
+        for first, stop in ranges:
+            run(step, first, stop, start)
+
+
+def inner_kernel(where_ref, perm_ref, cond_ref, across, *refs):
+    coeffs, force, diag, fluid = refs[-12:-8]
+    cells = refs[-8:]
+    is_press = where_ref[0] == 0
+    is_low = where_ref[1] == 0
+    ext = cells[0].shape[0] - 2
+    side = XH // 2
+    tiles = ext - XH
+    cols = tiles * LANES
+    rows = rim_rows(is_low)
+    tables = class_tables(is_press, perm_ref, cond_ref)
+    clear(tuple(cells[:3]) + (fluid,), (0, 1, 2, ext - 1, ext, ext + 1))
+
+    def fill(t, carry):
+        read = lambda index, row: across[row : row + 1, lanes_at(t, index * cols)]
+        put_cells(cells, is_press, tables, t + side, rows, rim_cells(is_low, read))
+        put_level(fluid, cells, t + side, rows)
+        return carry
+
+    lax.fori_loop(0, tiles, fill, 0, unroll=8)
+    made = (coeffs, force, diag, fluid)
+    face_terms(cells, made, is_press, [(side, ext - side)], UNROLL)
+
+
+def main_kernel(where_ref, perm_ref, cond_ref, from_left, from_right, *refs):
+    v1, v2, boundary = refs[12:15]
+    coeffs, force, diag, fluid = refs[15:19]
+    cells = refs[19:]
+    v0 = cells[0]
+    is_press = where_ref[0] == 0
+    is_low = where_ref[1] == 0
+    ext = v0.shape[0] - 2
+    wide = XH * W
+    side = XH // 2
+    own_rows = pl.ds(pl.multiple_of(jnp.where(is_low, 0, 8), 8), 32)
+    tables = class_tables(is_press, perm_ref, cond_ref)
+
+    for e, message, at in (
+        (0, from_left, 0), (1, from_left, 1), (ext - 2, from_right, 0), (ext - 1, from_right, 1)
+    ):
+        parts = [message[:, lanes_at(at, index * wide)] for index in range(7)]
+        parts[1] = parts[1].astype(jnp.int32)
+        put_cells(cells, is_press, tables, e, own_rows, parts)
+        corner = message[:, 7 * wide :]
+        read = lambda index, row, corner=corner, at=at: corner[
+            index * 4 + row * 2 + at : index * 4 + row * 2 + at + 1
+        ]
+        put_cells(cells, is_press, tables, e, rim_rows(is_low), rim_cells(is_low, read))
+        put_level(fluid, cells, e, slice(None))
+    clear((v1, v2), (0, ext + 1))
+    made = (coeffs, force, diag, fluid)
+    face_terms(cells, made, is_press, [(0, side + 1), (ext - side - 1, ext)], UNROLL)
+    chebyshev, explicit = sweep_weights()
+    for chosen, weights, centre in (
+        (is_press, chebyshev, None),
+        (jnp.logical_not(is_press), explicit, diag),
+    ):
+
+        @pl.when(chosen)
+        def _(weights=weights, centre=centre):
+            (w0, u0), (w1, u1) = weights[:2]
+            sweep((0, ext), coeffs, force, centre, v0, v0, store_in(v1), w0, u0)
+            sweep((0, ext), coeffs, force, centre, v1, v0, store_in(v2), w1, u1)
 
     def send(e, carry):
         value = v2[e + 1]
@@ -664,7 +755,8 @@
     lax.fori_loop(0, ext, send, 0, unroll=UNROLL)
 
 
-def finish_kernel(where_ref, v1, v2, coeffs, force, diag, boundary, out, now, later):
+def finish_kernel(where_ref, v1, v2, coeffs, force, diag, boundary, done, out, now, later):
+    del done
     is_press = where_ref[0] == 0
     is_low = where_ref[1] == 0
     ext = v2.shape[0] - 2
@@ -712,16 +804,14 @@
     return result
 
 
-def faces_kernel(where_ref, own, other_a, other_b, faces, out, field, rim):
+def faces_kernel(where_ref, own, other, plane_ref, rock, out_ref, token, field, rim, out, sems):
+    token[...] = jnp.zeros(token.shape, jnp.float32)
     is_press = where_ref[0] == 0
     is_low = where_ref[1] == 0
-    tiles = out.shape[3] // LANES
+    tiles = out.shape[2] // LANES
     groups = tiles // 4
-    half = groups // 2
     side = XH // 2
     extra = groups * 2 * LANES
-    extra_other = half * 2 * LANES
-    own_at = pl.multiple_of(jnp.where(is_low, 0, 8), 8)
 
     def ordered(mine, theirs):
         return [jnp.where(is_low, mine, theirs), jnp.where(is_low, theirs, mine)]
@@ -730,31 +820,25 @@
     for par in range(2):
         pieces += ordered(
             own[par * groups : (par + 1) * groups, extra : extra + LANES],
-            other_b[par * groups : (par + 1) * groups, extra_other : extra_other + LANES],
+            other[par * groups : (par + 1) * groups, extra : extra + LANES],
         )
     for q, value in enumerate(regrouped(pieces)):
         rim[q] = value
-    plane = ordered(own[:, extra + LANES :], other_b[:, extra_other + LANES :])
+    plane = ordered(own[:, extra + LANES :], plane_ref[:, :LANES])
     lane = lane_index((32, LANES))
     field[tiles, 0:32, :] = jnp.where(lane < 32, plane[0], pltpu.roll(plane[1], 32, 1))
 
-    def gather(other, first):
-        def step(group, carry):
-            pieces = []
-            for par in range(2):
-                pieces += ordered(
-                    own[:, lanes_at(group + first, par * groups * LANES)],
-                    other[:, lanes_at(group, par * half * LANES)],
-                )
-            for q, value in enumerate(regrouped(pieces)):
-                field[4 * (group + first) + q, 0:32, :] = value
-                field[4 * (group + first) + q, 32:33, :] = rim[q, pl.ds(group + first, 1), :]
-            return carry
-
-        lax.fori_loop(0, half, step, 0, unroll=UNROLL)
-
-    gather(other_a, 0)
-    gather(other_b, half)
+    def gather(group, carry):
+        pieces = []
+        for par in range(2):
+            at = lanes_at(group, par * groups * LANES)
+            pieces += ordered(own[:, at], other[:, at])
+        for q, value in enumerate(regrouped(pieces)):
+            field[4 * group + q, 0:32, :] = value
+            field[4 * group + q, 32:33, :] = rim[q, pl.ds(group, 1), :]
+        return carry
+
+    lax.fori_loop(0, groups, gather, 0, unroll=8)
     low_lanes = lane < HALF
     not_last = lane % W != W - 1
 
@@ -768,27 +852,50 @@
             next_lane(here),
         )
 
-    @pl.when(is_press)
-    def _():
-        def step(t, carry):
-            here, others = around(t)
-            others = (others[0], others[1], jnp.where(not_last, others[2], 0.0))
-            for dim in range(3):
-                out[0, dim, :, lanes_at(t)] = face_mean(here, others[dim])
-            return carry
-
-        lax.fori_loop(0, tiles, step, 0, unroll=UNROLL)
-
-    @pl.when(jnp.logical_not(is_press))
-    def _():
-        def step(t, carry):
-            here, others = around(t)
-            for dim in range(3):
-                mean = faces[dim, t + side + 1, pl.ds(own_at, 32), :]
-                out[0, dim, :, lanes_at(t)] = mean * (here - others[dim])
-            return carry
-
-        lax.fori_loop(0, tiles, step, 0, unroll=UNROLL)
+    def press(t, carry):
+        here, others = around(t)
+        others = (others[0], others[1], jnp.where(not_last, others[2], 0.0))
+        for dim in range(3):
+            out[dim, :, lanes_at(t)] = face_mean(here, others[dim])
+        return carry
+
+    def heat(t, carry):
+        here, others = around(t)
+        stone = rock[t + side + 1]
+        after = rock[t + side + 2]
+        near = (
+            next_row(stone),
+            jnp.where(tall_low, half_turn(stone), half_turn(after)),
+            jnp.where(tall_not_last, next_lane(stone), 0.0),
+        )
+        for dim in range(3):
+            mean = face_mean(stone, near[dim])
+            mean = jnp.where(is_low, mean[0:32], mean[8:40])
+            out[dim, :, lanes_at(t)] = mean * (here - others[dim])
+        return carry
+
+    tall_lane = lane_index(rock.shape[1:])
+    tall_low = tall_lane < HALF
+    tall_not_last = tall_lane % W != W - 1
+    part = tiles // PARTS
+    copies = []
+    for index in range(PARTS):
+        first = index * part
+
+        @pl.when(is_press)
+        def _(first=first):
+            lax.fori_loop(first, first + part, press, 0, unroll=8)
+
+        @pl.when(jnp.logical_not(is_press))
+        def _(first=first):
+            lax.fori_loop(first, first + part, heat, 0, unroll=8)
+
+        at = pl.ds(first * LANES, part * LANES)
+        copy = pltpu.make_async_copy(out.at[:, :, at], out_ref.at[0, :, :, at], sems.at[index])
+        copy.start()
+        copies.append(copy)
+    for copy in copies:
+        copy.wait()
 
 
 def paired_body(states, coupled, facies, injectors, producers, perm_table, cond_table):
@@ -802,8 +909,6 @@
     up = [(i, i + 1) for i in range(count - 1)]
     down = [(b, a) for a, b in up]
     swap = [(0, 1), (1, 0)]
-    up_across = [(2 * a + c, 2 * b + 1 - c) for a, b in up for c in range(2)]
-    down_across = [(b, a) for a, b in up_across]
     opposite = [(0, 3), (1, 2), (2, 1), (3, 0)]
     f32, i32 = jnp.float32, jnp.int32
     states, coupled, facies, injectors, producers = [
@@ -811,17 +916,16 @@
         for value in (states, coupled, facies, injectors, producers)
     ]
 
-    to_right, to_left, across, across_right, across_left = pl.pallas_call(
+    to_right, to_left, across, corners = pl.pallas_call(
         edges_kernel,
         out_shape=[
             in_vmem((rows, 7 * wide)),
             in_vmem((rows, 7 * wide)),
             in_vmem((2, 5 * cols)),
-            in_vmem((2, 5 * wide)),
-            in_vmem((2, 5 * wide)),
+            in_vmem((2, 10 * wide)),
         ],
         in_specs=[SM] + [HB] * 5,
-        out_specs=[VM] * 5,
+        out_specs=[VM] * 4,
         scratch_shapes=[
             pltpu.VMEM((4, rows, wide), f32),
             pltpu.VMEM((4, rows, wide), f32),
@@ -835,92 +939,112 @@
         cost_estimate=cost(1),
         name="edges",
     )(place, states, coupled, facies, injectors, producers)
+    corners = held(lax.ppermute(corners, "ba", swap))
+    to_right, to_left, across = pl.pallas_call(
+        pack_kernel,
+        out_shape=[
+            in_vmem((rows, 7 * wide + LANES)),
+            in_vmem((rows, 7 * wide + LANES)),
+            in_vmem(across.shape),
+        ],
+        in_specs=[VM] * 4,
+        out_specs=[VM] * 3,
+        compiler_params=LEAN,
+        cost_estimate=cost(1),
+        name="pack",
+    )(to_right, to_left, across, corners)
     from_left = held(lax.ppermute(to_right, "aa", up))
     from_right = held(lax.ppermute(to_left, "aa", down))
     from_across = held(lax.ppermute(across, "ba", swap))
-    corner_left = held(lax.ppermute(across_right, ("aa", "ba"), up_across))
-    corner_right = held(lax.ppermute(across_left, ("aa", "ba"), down_across))
-
-    st, cp, fa, ij, pr, turned_own, turned_a, turned_b = pl.pallas_call(
+
+    field = (ext + 2, rows + 8, LANES)
+    turned = in_vmem((32, (2 * groups + 2) * LANES))
+    turned_over = in_vmem((32, (2 * groups + 3) * LANES))
+    turned_own, turned_other, fluid, *cells = pl.pallas_call(
         turn_kernel,
-        out_shape=[
-            in_vmem(states.shape),
-            in_vmem(coupled.shape),
+        out_shape=[turned, turned_over]
+        + [in_vmem(field)] * 9,
+        in_specs=[SM] * 3 + [HB] * 5 + [VM],
+        out_specs=[VM] * 11,
+        scratch_shapes=[
+            pltpu.VMEM(states.shape, f32),
+            pltpu.VMEM(coupled.shape, f32),
             pltpu.VMEM(facies.shape, i32),
             pltpu.VMEM(facies.shape, i32),
             pltpu.VMEM(facies.shape, i32),
-            in_vmem((32, (2 * groups + 2) * LANES)),
-            in_vmem((32, groups * LANES)),
-            in_vmem((32, (groups + 2) * LANES)),
+            pltpu.SemaphoreType.DMA((5,)),
         ],
-        in_specs=[SM] + [HB] * 5,
-        out_specs=[VM] * 8,
-        scratch_shapes=[pltpu.SemaphoreType.DMA((5,))],
-        compiler_params=LEAN,
-        cost_estimate=cost(3),
+        compiler_params=params(10),
+        cost_estimate=cost(6),
         name="turn",
-    )(place, states, coupled, facies, injectors, producers)
-    other_a = held(lax.ppermute(turned_a, ("code", "ba"), opposite))
-    turned_own, turned_b = pl.pallas_call(
+    )(
+        place, perm_table, cond_table, states, coupled, facies, injectors, producers,
+        corners,
+    )
+    other = held(lax.ppermute(turned_other, ("code", "ba"), opposite))
+    coeffs, force, diag, fluid, *cells = pl.pallas_call(
+        inner_kernel,
+        out_shape=[in_vmem((6,) + field)] + [in_vmem(field)] * 11,
+        in_specs=[SM] * 3 + [VM] * 10,
+        out_specs=[VM] * 12,
+        input_output_aliases={4 + index: 3 + index for index in range(9)},
+        compiler_params=params(2),
+        cost_estimate=cost(6),
+        name="inner",
+    )(place, perm_table, cond_table, from_across, fluid, *cells)
+    turned_own, plane = pl.pallas_call(
         plane_kernel,
-        out_shape=[in_vmem(turned_own.shape), in_vmem(turned_b.shape)],
-        in_specs=[SM] + [VM] * 7,
+        out_shape=[turned, in_vmem((32, 5 * LANES))],
+        in_specs=[SM] + [VM] * 4,
         out_specs=[VM] * 2,
         compiler_params=LEAN,
         cost_estimate=cost(1),
         name="plane",
-    )(
-        place, from_right, turned_own, turned_b, from_left, from_across, corner_left, corner_right
-    )
-    other_b = held(lax.ppermute(turned_b, ("code", "ba"), opposite))
+    )(place, from_right, turned_own, from_left, force)
     own = held(lax.ppermute(turned_own, "code", swap))
-
-    field = (ext + 2, rows + 8, LANES)
-    v1, v2, coeffs, force, diag, faces, boundary = pl.pallas_call(
+    plane_over = held(lax.ppermute(plane, ("code", "ba"), opposite))
+    v1, v2, boundary, coeffs, force, diag, fluid, *cells = pl.pallas_call(
         main_kernel,
-        out_shape=[
-            in_vmem(field),
-            in_vmem(field),
-            in_vmem((6,) + field),
-            in_vmem(field),
-            in_vmem(field),
-            in_vmem((3,) + field),
-            in_vmem((2, ext * LANES)),
-        ],
-        in_specs=[SM, SM, SM] + [VM] * 10,
-        out_specs=[VM] * 7,
-        scratch_shapes=[pltpu.VMEM(field, f32)] * 9,
-        compiler_params=params(18),
-        cost_estimate=cost(12),
+        out_shape=[in_vmem(field), in_vmem(field), in_vmem((2, ext * LANES))]
+        + [in_vmem((6,) + field)]
+        + [in_vmem(field)] * 11,
+        in_specs=[SM] * 3 + [VM] * 14,
+        out_specs=[VM] * 15,
+        input_output_aliases={5 + index: 3 + index for index in range(12)},
+        compiler_params=params(2),
+        cost_estimate=cost(6),
         name="main",
     )(
-        place, perm_table, cond_table, st, cp, fa, ij, pr,
-        from_left, from_right, from_across, corner_left, corner_right,
-    )
+        place, perm_table, cond_table, from_left, from_right,
+        coeffs, force, diag, fluid, *cells,
+    )
+    rock = cells[2]
     boundary = held(lax.ppermute(boundary, "ba", swap))
+    received, token = pl.pallas_call(
+        faces_kernel,
+        out_shape=[jax.ShapeDtypeStruct(coupled.shape, f32), in_vmem((8, LANES))],
+        in_specs=[SM] + [VM] * 4,
+        out_specs=[HB, VM],
+        scratch_shapes=[
+            pltpu.VMEM((tiles + 1, rows + 8, LANES), f32),
+            pltpu.VMEM((4, groups, LANES), f32),
+            pltpu.VMEM(coupled.shape[1:], f32),
+            pltpu.SemaphoreType.DMA((PARTS,)),
+        ],
+        compiler_params=params(8),
+        cost_estimate=cost(5),
+        name="faces",
+    )(place, own, other, plane_over, rock)
     stepped = pl.pallas_call(
         finish_kernel,
         out_shape=jax.ShapeDtypeStruct(states.shape, f32),
-        in_specs=[SM] + [VM] * 6,
+        in_specs=[SM] + [VM] * 7,
         out_specs=VM,
         scratch_shapes=[pltpu.VMEM(field, f32)] * 2,
         compiler_params=params(8),
         cost_estimate=cost(6),
         name="finish",
-    )(place, v1, v2, coeffs, force, diag, boundary)
-    received = pl.pallas_call(
-        faces_kernel,
-        out_shape=jax.ShapeDtypeStruct(coupled.shape, f32),
-        in_specs=[SM] + [VM] * 4,
-        out_specs=VM,
-        scratch_shapes=[
-            pltpu.VMEM((tiles + 1, rows + 8, LANES), f32),
-            pltpu.VMEM((4, groups, LANES), f32),
-        ],
-        compiler_params=params(8),
-        cost_estimate=cost(5),
-        name="faces",
-    )(place, own, other_a, other_b, faces)
+    )(place, v1, v2, coeffs, force, diag, boundary, token)
     return (stepped, received)
 
 

time: 60.8 us -> 47 us (0.77)
  the two profiles are of different devices: /device:TPU:9 before, /device:TPU:11 now
where the time goes in v2:
time: 47 us; the launch traced here: 46.8 us
  Pallas kernels  30.2 us (64%)
  starting transfers between devices  12.6 us (27%)
  waiting for transfers between devices  3.21 us (7%)
  between operations  0.74 us (2%)
    pallas_call x1, Pallas kernels, paired_body(): pl.pallas_call(inner_kernel, out_shape=[in_vmem((6,) + field)] + [in_vmem...  7.39 us
    pallas_call x1, Pallas kernels, paired_body(): pl.pallas_call(turn_kernel, out_shape=[turned, turned_over] + [in_vmem(fi...  5.1 us
    pallas_call x1, Pallas kernels, paired_body(): pl.pallas_call(faces_kernel, out_shape=[jax.ShapeDtypeStruct(coupled.shap...  5.01 us
    pallas_call x1, Pallas kernels, paired_body(): pl.pallas_call(finish_kernel, out_shape=jax.ShapeDtypeStruct(states.shape...  4.73 us
    pallas_call x1, Pallas kernels, paired_body(): pl.pallas_call(main_kernel, out_shape=[in_vmem(field), in_vmem(field), in...  4.63 us
    ppermute x1, starting transfers between devices, paired_body(): other = held(lax.ppermute(turned_other, ('code', 'ba'), opposite))  3.83 us
    ppermute x1, starting transfers between devices, paired_body(): from_left = held(lax.ppermute(to_right, 'aa', up))  3.14 us
    ppermute x1, starting transfers between devices, paired_body(): from_right = held(lax.ppermute(to_left, 'aa', down))  3.03 us
  transfers between devices with their start and end apart: 8, of which 2 were waited for; matrix products, arithmetic and copies ran while one was open for 0% of the time, Pallas kernels for 49%

profile of v2, /device:TPU:11, one launch (start us, length us, event | category | flops | bytes accessed | tf_op | source)
XLA Modules:
  0.0 46.8 jit_solution(8596915819516484999)
XLA Ops:
  0.6 0.1 pad_add_fusion.where_ref
  0.7 0.0 copy-start
  0.7 0.0 copy-start.1
  0.7 2.6 %edges.1 = (f32[32,1792]{1,0:T(8,128)S(1)}, f32[32,1792]{1,0:T(8,128)S(1)}, f32[2,40960]{1,0:T(2,128)S(1)}, f32[2,2560]{1,0:T(2,128)S(1)}) custom-call(s32[2]{0:T(128)S(1)} %pad_add_fusion.where_ref, f32[1,32,8192]{2,1,0:T(8,128)} %st_in.1, f32[1,3,32,8192]{3,2,1,0:T(8,128)} %cp_in.1, s32[1,32,8192]{2,1,0:T(8,128)} %fa_in.1, s32[1,32,8192]{2,1,0:T(8,128)} %ij_in.1, ...), custom_call_target="tpu_custom_call" | custom-call | bytes 3200000 | tf_op jit(solution)/shard_map/edges/pallas_call | solution.py:919
  3.3 0.3 collective-permute-start
  3.6 2.4 %collective-permute-done.corners = f32[2,2560]{1,0:T(2,128)S(1)} collective-permute-done((f32[2,2560]{1,0:T(2,128)S(1)}, f32[2,2560]{1,0:T(2,128)S(1)}, u32[]{:S(2)}, u32[]{:S(2)}) %collective-permute-start) | collective-permute-done | bytes 20512 | tf_op jit(solution)/shard_map/ppermute | solution.py:942
  6.0 0.1 pack.1
  6.1 0.3 collective-permute-start.3
  6.4 3.1 %collective-permute-start.1 = (f32[32,1920]{1,0:T(8,128)S(1)}, f32[32,1920]{1,0:T(8,128)S(1)}, u32[]{:S(2)}, u32[]{:S(2)}) collective-permute-start(f32[32,1920]{1,0:T(8,128)S(1)} %get-tuple-element.47), channel_id=1, source_target_pairs={{0,2},{2,4},{4,6},{6,8},{8,10},{10,12},{12,14},{1,3},{3,5},{5,7},{... | collective-permute-start | bytes 737288 | tf_op jit(solution)/shard_map/ppermute | solution.py:956
  9.6 3.0 %collective-permute-start.2 = (f32[32,1920]{1,0:T(8,128)S(1)}, f32[32,1920]{1,0:T(8,128)S(1)}, u32[]{:S(2)}, u32[]{:S(2)}) collective-permute-start(f32[32,1920]{1,0:T(8,128)S(1)} %get-tuple-element.48), channel_id=1, source_target_pairs={{2,0},{4,2},{6,4},{8,6},{10,8},{12,10},{14,12},{3,1},{5,3},{7,5},{... | collective-permute-start | bytes 737288 | tf_op jit(solution)/shard_map/ppermute | solution.py:957
  12.6 0.0 copy-done
  12.6 0.0 copy-done.1
  12.6 5.1 %turn.1 = (f32[32,4352]{1,0:T(8,128)S(1)}, f32[32,4480]{1,0:T(8,128)S(1)}, f32[70,40,128]{2,1,0:T(8,128)S(1)}, f32[70,40,128]{2,1,0:T(8,128)S(1)}, f32[70,40,128...) custom-call(s32[2]{0:T(128)S(1)} %pad_add_fusion.where_ref, ...), custom_call_target="tpu_custom_call" | custom-call | bytes 19200000 | tf_op jit(solution)/shard_map/turn/pallas_call | solution.py:963
  17.7 3.8 %collective-permute-start.6 = (f32[32,4480]{1,0:T(8,128)S(1)}, f32[32,4480]{1,0:T(8,128)S(1)}, u32[]{:S(2)}, u32[]{:S(2)}) collective-permute-start(f32[32,4480]{1,0:T(8,128)S(1)} %get-tuple-element.79), channel_id=1, source_target_pairs={{0,17},{1,16},{16,1},{17,0},{2,19},{3,18},{18,3},{19,2},{4,21},{5,... | collective-permute-start | bytes 1720328 | tf_op jit(solution)/shard_map/ppermute | solution.py:984
  21.6 0.0 collective-permute-done.3.across
  21.6 7.4 %inner.1 = (f32[6,70,40,128]{3,2,1,0:T(8,128)S(1)}, f32[70,40,128]{2,1,0:T(8,128)S(1)}, f32[70,40,128]{2,1,0:T(8,128)S(1)}, f32[70,40,128]{2,1,0:T(8,128)S(1)}, ...) custom-call(s32[2]{0:T(128)S(1)} %pad_add_fusion.where_ref, ...), custom_call_target="tpu_custom_call", output_to_operand_aliasing={{3}: (4, {}), {4}: (5, {}), {5}: (6, {}), {6}: (7, {}), {7}... | custom-call | bytes 19200000 | tf_op jit(solution)/shard_map/inner/pallas_call | solution.py:985
  29.0 0.0 collective-permute-done.1.from_left.rest_0_
  29.0 0.0 collective-permute-done.2.from_right
  29.0 0.6 %plane.1 = (f32[32,4352]{1,0:T(8,128)S(1)}, f32[32,640]{1,0:T(8,128)S(1)}) custom-call(s32[2]{0:T(128)S(1)} %pad_add_fusion.where_ref, f32[32,1920]{1,0:T(8,128)S(1)} %collective-permute-done.2.from_right, f32[32,4352]{1,0:T(8,128)S(1)} %get-tuple-element.77.own_in, f32[32,1920]{1,0:T(8,128)S(1)} %collective-permute-done.1.from_left.rest_0_, ...), custom_call_target="tpu_custom_call" | custom-call | bytes 3200000 | tf_op jit(solution)/shard_map/plane/pallas_call | solution.py:995
  29.6 0.1 collective-permute-start.5
  29.7 0.6 %collective-permute-start.7 = (f32[32,640]{1,0:T(8,128)S(1)}, f32[32,640]{1,0:T(8,128)S(1)}, u32[]{:S(2)}, u32[]{:S(2)}) collective-permute-start(f32[32,640]{1,0:T(8,128)S(1)} %get-tuple-element.80), channel_id=1, source_target_pairs={{0,17},{1,16},{16,1},{17,0},{2,19},{3,18},{18,3},{19,2},{4,21},{5,... | collective-permute-start | bytes 245768 | tf_op jit(solution)/shard_map/ppermute | solution.py:1005
  30.3 4.6 %main.1 = (f32[70,40,128]{2,1,0:T(8,128)S(1)}, f32[70,40,128]{2,1,0:T(8,128)S(1)}, f32[2,8704]{1,0:T(2,128)S(1)}, f32[6,70,40,128]{3,2,1,0:T(8,128)S(1)}, f32[70...) custom-call(s32[2]{0:T(128)S(1)} %pad_add_fusion.where_ref, ...), custom_call_target="tpu_custom_call", output_to_operand_aliasing={{3}: (5, {}), {4}: (6, {}), {5}: (7, {}), {6}: (8, {}), {7}... | custom-call | bytes 19200000 | tf_op jit(solution)/shard_map/main/pallas_call | solution.py:1006
  35.0 1.3 %collective-permute-start.4 = (f32[2,8704]{1,0:T(2,128)S(1)}, f32[2,8704]{1,0:T(2,128)S(1)}, u32[]{:S(2)}, u32[]{:S(2)}) collective-permute-start(f32[2,8704]{1,0:T(2,128)S(1)} %get-tuple-element.76), channel_id=1, source_target_pairs={{0,1},{1,0},{2,3},{3,2},{4,5},{5,4},{6,7},{7,6},{8,9},{9,8},{10,11... | collective-permute-start | bytes 208904 | tf_op jit(solution)/shard_map/ppermute | solution.py:1022
  36.2 0.8 %collective-permute-done.7.plane_ref = f32[32,640]{1,0:T(8,128)S(1)} collective-permute-done((f32[32,640]{1,0:T(8,128)S(1)}, f32[32,640]{1,0:T(8,128)S(1)}, u32[]{:S(2)}, u32[]{:S(2)}) %collective-permute-start.7) | collective-permute-done | bytes 81952 | tf_op jit(solution)/shard_map/ppermute | solution.py:1005
  37.0 0.0 collective-permute-done.6.other
  37.1 0.0 collective-permute-done.5.own
  37.1 5.0 %faces.1 = (f32[1,3,32,8192]{3,2,1,0:T(8,128)}, f32[8,128]{1,0:T(8,128)S(1)}) custom-call(s32[2]{0:T(128)S(1)} %pad_add_fusion.where_ref, f32[32,4352]{1,0:T(8,128)S(1)} %collective-permute-done.5.own, f32[32,4480]{1,0:T(8,128)S(1)} %collective-permute-done.6.other, f32[32,640]{1,0:T(8,128)S(1)} %collective-permute-done.7.plane_ref, ...), custom_call_target="tpu_custom_call" | custom-call | bytes 16000000 | tf_op jit(solution)/shard_map/faces/pallas_call | solution.py:1023
  42.1 0.0 collective-permute-done.4.boundary
  42.1 4.7 %finish.1 = f32[1,32,8192]{2,1,0:T(8,128)} custom-call(s32[2]{0:T(128)S(1)} %pad_add_fusion.where_ref, f32[70,40,128]{2,1,0:T(8,128)S(1)} %get-tuple-element.71.v1, f32[70,40,128]{2,1,0:T(8,128)S(1)} %get-tuple-element.72.v2, f32[6,70,40,128]{3,2,1,0:T(8,128)S(1)} %get-tuple-element.73.coeffs, f32[70,40,128]{2,1,0:T(8,128)S(1)} %get-tuple-element.74.force, ...), custom_call_target="tpu_custom_call" | custom-call | bytes 19200000 | tf_op jit(solution)/shard_map/finish/pallas_call | solution.py:1038
Async XLA Ops:
  0.7 11.9 %copy-start = (f32[6]{0:T(128)S(1)}, f32[6]{0:T(128)}, u32[]{:S(2)}) copy-start(f32[6]{0:T(128)} %perm_ref.5) | copy-start | bytes 76
  0.7 11.9 %copy-start.1 = (f32[6]{0:T(128)S(1)}, f32[6]{0:T(128)}, u32[]{:S(2)}) copy-start(f32[6]{0:T(128)} %cond_ref.5) | copy-start | bytes 76
  3.3 2.7 %collective-permute-start = (f32[2,2560]{1,0:T(2,128)S(1)}, f32[2,2560]{1,0:T(2,128)S(1)}, u32[]{:S(2)}, u32[]{:S(2)}) collective-permute-start(f32[2,2560]{1,0:T(2,128)S(1)} %get-tuple-element.46), channel_id=1, source_target_pairs={{0,1},{1,0},{2,3},{3,2},{4,5},{5,4},{6,7},{7,6},{8,9},{9,8},{10,11... | collective-permute-start | bytes 61448 | tf_op jit(solution)/shard_map/ppermute | solution.py:942
  6.1 15.5 %collective-permute-start.3 = (f32[2,40960]{1,0:T(2,128)S(1)}, f32[2,40960]{1,0:T(2,128)S(1)}, u32[]{:S(2)}, u32[]{:S(2)}) collective-permute-start(f32[2,40960]{1,0:T(2,128)S(1)} %get-tuple-element.49), channel_id=1, source_target_pairs={{0,1},{1,0},{2,3},{3,2},{4,5},{5,4},{6,7},{7,6},{8,9},{9,8},{10,11... | collective-permute-start | bytes 983048 | tf_op jit(solution)/shard_map/ppermute | solution.py:958
  6.4 22.5 %collective-permute-start.1 = (f32[32,1920]{1,0:T(8,128)S(1)}, f32[32,1920]{1,0:T(8,128)S(1)}, u32[]{:S(2)}, u32[]{:S(2)}) collective-permute-start(f32[32,1920]{1,0:T(8,128)S(1)} %get-tuple-element.47), channel_id=1, source_target_pairs={{0,2},{2,4},{4,6},{6,8},{8,10},{10,12},{12,14},{1,3},{3,5},{5,7},{... | collective-permute-start | bytes 737288 | tf_op jit(solution)/shard_map/ppermute | solution.py:956
  9.6 19.4 %collective-permute-start.2 = (f32[32,1920]{1,0:T(8,128)S(1)}, f32[32,1920]{1,0:T(8,128)S(1)}, u32[]{:S(2)}, u32[]{:S(2)}) collective-permute-start(f32[32,1920]{1,0:T(8,128)S(1)} %get-tuple-element.48), channel_id=1, source_target_pairs={{2,0},{4,2},{6,4},{8,6},{10,8},{12,10},{14,12},{3,1},{5,3},{7,5},{... | collective-permute-start | bytes 737288 | tf_op jit(solution)/shard_map/ppermute | solution.py:957
  17.7 19.3 %collective-permute-start.6 = (f32[32,4480]{1,0:T(8,128)S(1)}, f32[32,4480]{1,0:T(8,128)S(1)}, u32[]{:S(2)}, u32[]{:S(2)}) collective-permute-start(f32[32,4480]{1,0:T(8,128)S(1)} %get-tuple-element.79), channel_id=1, source_target_pairs={{0,17},{1,16},{16,1},{17,0},{2,19},{3,18},{18,3},{19,2},{4,21},{5,... | collective-permute-start | bytes 1720328 | tf_op jit(solution)/shard_map/ppermute | solution.py:984
  29.6 7.4 %collective-permute-start.5 = (f32[32,4352]{1,0:T(8,128)S(1)}, f32[32,4352]{1,0:T(8,128)S(1)}, u32[]{:S(2)}, u32[]{:S(2)}) collective-permute-start(f32[32,4352]{1,0:T(8,128)S(1)} %get-tuple-element.78), channel_id=1, source_target_pairs={{0,16},{16,0},{1,17},{17,1},{2,18},{18,2},{3,19},{19,3},{4,20},{20... | collective-permute-start | bytes 1671176 | tf_op jit(solution)/shard_map/ppermute | solution.py:1004
  29.7 7.4 %collective-permute-start.7 = (f32[32,640]{1,0:T(8,128)S(1)}, f32[32,640]{1,0:T(8,128)S(1)}, u32[]{:S(2)}, u32[]{:S(2)}) collective-permute-start(f32[32,640]{1,0:T(8,128)S(1)} %get-tuple-element.80), channel_id=1, source_target_pairs={{0,17},{1,16},{16,1},{17,0},{2,19},{3,18},{18,3},{19,2},{4,21},{5,... | collective-permute-start | bytes 245768 | tf_op jit(solution)/shard_map/ppermute | solution.py:1005
  35.0 7.1 %collective-permute-start.4 = (f32[2,8704]{1,0:T(2,128)S(1)}, f32[2,8704]{1,0:T(2,128)S(1)}, u32[]{:S(2)}, u32[]{:S(2)}) collective-permute-start(f32[2,8704]{1,0:T(2,128)S(1)} %get-tuple-element.76), channel_id=1, source_target_pairs={{0,1},{1,0},{2,3},{3,2},{4,5},{5,4},{6,7},{7,6},{8,9},{9,8},{10,11... | collective-permute-start | bytes 208904 | tf_op jit(solution)/shard_map/ppermute | solution.py:1022

commit v3 on v2

--- a/solution.py
+++ b/solution.py
@@ -263,7 +263,9 @@
 
 
 def cost(micros):
-    return pl.CostEstimate(flops=0, bytes_accessed=int(micros * 3.2e6), transcendentals=0)
+    return pl.CostEstimate(
+        flops=int(micros * 1.15e9), bytes_accessed=int(micros * 3.6e6), transcendentals=0
+    )
 
 
 def in_vmem(shape):
@@ -333,64 +335,83 @@
     return jnp.where(is_low, jnp.concatenate([row, blank], 0), jnp.concatenate([blank, row], 0))
 
 
-def edges_kernel(
-    where_ref, st, cp, fa, ij, pr, to_right, to_left, across, corners,
-    left_f, right_f, row_f, left_i, right_i, row_i, sems,
-):
+def rim_slots(is_low, state, codes, f0, f1, f2, inject, produce):
+    def pair(value):
+        return jnp.where(is_low, value[6:8], value[0:2])
+
+    def near(one, two):
+        value = jnp.concatenate([one[0:8], two[0:8]], 0)
+        return jnp.concatenate(
+            [
+                jnp.where(is_low, value[7:8], value[0:1]),
+                jnp.where(is_low, value[15:16], value[8:9]),
+            ],
+            0,
+        )
+
+    return [
+        pair(state),
+        pair((codes + 1).astype(jnp.float32)),
+        pair(f0),
+        near(f1, f2),
+        near(inject.astype(jnp.float32), produce.astype(jnp.float32)),
+    ]
+
+
+def corner_kernel(where_ref, st, cp, fa, ij, pr, corners, state, field, codes, sems):
     is_low = where_ref[1] == 0
     rows, cols = st.shape[1], st.shape[2]
     wide = XH * W
-    first = pl.multiple_of(jnp.where(is_low, rows - 8, 0), 8)
-    floats = [st.at[0]] + [cp.at[0, c] for c in range(3)]
-    ints = [fa.at[0], ij.at[0], pr.at[0]]
+    at = pl.ds(pl.multiple_of(jnp.where(is_low, rows - 8, 0), 8), 8)
     copies = []
-    for group, (left, right, row) in (
-        (floats, (left_f, right_f, row_f)),
-        (ints, (left_i, right_i, row_i)),
-    ):
-        for index, field in enumerate(group):
-            for source, target in (
-                (field.at[pl.ds(first, 8), :], row.at[index]),
-                (field.at[:, pl.ds(0, wide)], left.at[index]),
-                (field.at[:, pl.ds(cols - wide, wide)], right.at[index]),
-            ):
-                copy = pltpu.make_async_copy(source, target, sems.at[len(copies)])
-                copy.start()
-                copies.append(copy)
+    for side, start in enumerate((0, cols - wide)):
+        lanes = pl.ds(start, wide)
+        for source, target in (
+            (st.at[0, at, lanes], state.at[side]),
+            (cp.at[0, :, at, lanes], field.at[side]),
+            (fa.at[0, at, lanes], codes.at[side, 0]),
+            (ij.at[0, at, lanes], codes.at[side, 1]),
+            (pr.at[0, at, lanes], codes.at[side, 2]),
+        ):
+            copy = pltpu.make_async_copy(source, target, sems.at[len(copies)])
+            copy.start()
+            copies.append(copy)
     for copy in copies:
         copy.wait()
-    for target, floats_ref, ints_ref in ((to_right, right_f, right_i), (to_left, left_f, left_i)):
+    for side in range(2):
+        slots = rim_slots(
+            is_low, state[side], codes[side, 0], field[side, 0], field[side, 1], field[side, 2],
+            codes[side, 1], codes[side, 2],
+        )
+        for index, slot in enumerate(slots):
+            start = (2 * index + side) * wide
+            corners[:, start : start + wide] = slot
+
+
+def edges_kernel(where_ref, st, cp, fa, ij, pr, to_right, to_left, across):
+    is_low = where_ref[1] == 0
+    rows, cols = st.shape[1], st.shape[2]
+    wide = XH * W
+    for target, start in ((to_right, cols - wide), (to_left, 0)):
+        at = slice(start, start + wide)
         parts = [
-            floats_ref[0],
-            (ints_ref[0] + 1).astype(jnp.float32),
-            floats_ref[1],
-            floats_ref[2],
-            floats_ref[3],
-            ints_ref[1].astype(jnp.float32),
-            ints_ref[2].astype(jnp.float32),
+            st[0, :, at],
+            (fa[0, :, at] + 1).astype(jnp.float32),
+            cp[0, 0, :, at],
+            cp[0, 1, :, at],
+            cp[0, 2, :, at],
+            ij[0, :, at].astype(jnp.float32),
+            pr[0, :, at].astype(jnp.float32),
         ]
         for index, part in enumerate(parts):
             target[:, index * wide : (index + 1) * wide] = part
-
-    def pair(value):
-        return jnp.where(is_low, value[6:8], value[0:2])
-
-    def near(value):
-        return jnp.where(is_low, value[7:8], value[0:1])
-
-    slots = [
-        pair(row_f[0]),
-        pair((row_i[0] + 1).astype(jnp.float32)),
-        pair(row_f[1]),
-        jnp.concatenate([near(row_f[2]), near(row_f[3])], 0),
-        jnp.concatenate(
-            [near(row_i[1].astype(jnp.float32)), near(row_i[2].astype(jnp.float32))], 0
-        ),
-    ]
+    rim = pl.ds(pl.multiple_of(jnp.where(is_low, rows - 8, 0), 8), 8)
+    slots = rim_slots(
+        is_low, st[0, rim, :], fa[0, rim, :], cp[0, 0, rim, :], cp[0, 1, rim, :],
+        cp[0, 2, rim, :], ij[0, rim, :], pr[0, rim, :],
+    )
     for index, slot in enumerate(slots):
         across[:, index * cols : (index + 1) * cols] = slot
-        corners[:, 2 * index * wide : (2 * index + 1) * wide] = slot[:, :wide]
-        corners[:, (2 * index + 1) * wide : (2 * index + 2) * wide] = slot[:, cols - wide :]
 
 
 def pack_kernel(right_in, left_in, across_in, corners, to_right, to_left, across):
@@ -429,20 +450,10 @@
 
 
 def turn_kernel(
-    where_ref, perm_ref, cond_ref, st_in, cp_in, fa_in, ij_in, pr_in, corners,
-    own, other, fluid, v0, prop, rock, c0, c1, c2, src, snk,
-    st, cp, fa, ij, pr, sems,
+    where_ref, perm_ref, cond_ref, st, cp, fa, ij, pr, corners,
+    own, other, rim, fluid, v0, prop, rock, c0, c1, c2, src, snk,
 ):
     del corners
-    copies = [
-        pltpu.make_async_copy(source, target, sems.at[index])
-        for index, (source, target) in enumerate(
-            ((st_in, st), (cp_in, cp), (fa_in, fa), (ij_in, ij), (pr_in, pr))
-        )
-    ]
-    for copy in copies:
-        copy.start()
-    copies[0].wait()
     is_heat = where_ref[0] == 1
     is_low = where_ref[1] == 0
     own_rows = pl.ds(pl.multiple_of(jnp.where(is_low, 0, 8), 8), 32)
@@ -470,10 +481,8 @@
         return rims
 
     rims = lax.fori_loop(0, groups, step, jnp.zeros((32, LANES), jnp.float32), unroll=8)
-    own[:, extra : extra + LANES] = jnp.where(is_low, rims, 0.0)
+    rim[:, :LANES] = jnp.where(is_low, rims, 0.0)
     other[:, extra : extra + LANES] = jnp.where(is_low, 0.0, rims)
-    for copy in copies[1:]:
-        copy.wait()
     refs = (v0, prop, rock, c0, c1, c2, src, snk)
     is_press = where_ref[0] == 0
     tables = class_tables(is_press, perm_ref, cond_ref)
@@ -492,19 +501,35 @@
 
 
 def plane_kernel(where_ref, from_right, own_in, *rest):
-    own, other = rest[-2:]
+    del own_in
+    own = rest[-1]
     is_heat = where_ref[0] == 1
     is_low = where_ref[1] == 0
     wide = XH * W
     value = from_right[:, 0:LANES]
     inside = from_right[:, wide : wide + LANES] > 0.5
     value = jnp.where(is_heat, jnp.where(inside, flowability(value), 0.0), value)
-    tall = jnp.concatenate([value, jnp.zeros((96, LANES), jnp.float32)], 0).T
+    tall = jnp.concatenate([value, value, jnp.zeros((64, LANES), jnp.float32)], 0).T
     low, high = tall[0:32], tall[32:64]
-    own[...] = own_in[...]
-    own[:, own.shape[1] - LANES :] = jnp.where(is_low, low, high)
-    other[...] = jnp.zeros(other.shape, jnp.float32)
-    other[:, :LANES] = jnp.where(is_low, high, low)
+    keep = lane_index((32, LANES)) < 32
+    own[:, own.shape[1] - LANES :] = jnp.where(keep == is_low, low, high)
+
+
+def send_kernel(where_ref, v2, own, boundary):
+    is_low = where_ref[1] == 0
+    ext = v2.shape[0] - 2
+
+    def send(e, carry):
+        value = v2[e + 1]
+        boundary[:, lanes_at(e)] = jnp.where(is_low, value[30:32], value[8:10])
+        return carry
+
+    lax.fori_loop(0, ext, send, 0, unroll=17)
+    for index in range(16):
+        start = (ext + index) * LANES
+        boundary[:, start : start + LANES] = own[
+            2 * index : 2 * index + 2, own.shape[1] - LANES :
+        ]
 
 
 def sweep(tiles, coeffs, force, diag, now, last, target, weight, pull):
@@ -533,7 +558,7 @@
 
     lax.fori_loop(
         first, stop, step, (half_turn(now[first]), half_turn(now[first + 1])),
-        unroll=(stop - first) // 2,
+        unroll=stop - first,
     )
 
 
@@ -572,7 +597,7 @@
             ref[e] = jnp.zeros(ref.shape[1:], jnp.float32)
 
 
-def face_terms(cells, made, is_press, ranges, long):
+def face_terms(cells, made, is_press, ranges):
     v0, prop, rock, c0, c1, c2, src, snk = cells
     coeffs, force, diag, fluid = made
     shape = v0.shape[1:]
@@ -581,106 +606,132 @@
     not_last = lane % W != W - 1
     blank = jnp.zeros(shape, jnp.float32)
 
-    def next_cells(value, here, after):
-        return (
-            next_row(value),
-            jnp.where(low_lanes, here, after),
-            jnp.where(not_last, next_lane(value), 0.0),
-        )
-
     def run(step, first, stop, start):
         if stop - first > 8:
-            lax.fori_loop(first, stop, step, start(first), unroll=long)
-        else:
-            carry = start(first)
-            for e in range(first, stop):
-                carry = step(e, carry)
-
-    @pl.when(is_press)
-    def _():
-        def plus_along(e, here, after):
+            unroll = max(n for n in range(1, 10) if (stop - first) % n == 0)
+            return lax.fori_loop(first, stop, step, start, unroll=unroll)
+        for e in range(first, stop):
+            start = step(e, start)
+        return start
+
+    def beside(value, turns, after):
+        return (
+            jnp.where(low_lanes, turns[0], after[0]),
+            jnp.where(not_last, turns[1], 0.0),
+        )
+
+    def press_range(first, stop):
+        def turns(e):
             value = prop[e + 1]
-            return face_mean(value, jnp.where(low_lanes, here, after)) * c1[e + 1]
-
-        def start(first):
-            here = half_turn(prop[first + 1])
-            if first == 0:
-                return blank, here
-            return half_turn(plus_along(first - 1, half_turn(prop[first]), here)), here
-
-        def step(e, carry):
-            before, here = carry
-            value, after = prop[e + 1], half_turn(prop[e + 2])
-            means = [face_mean(value, other) for other in next_cells(value, here, after)]
-            plus = [mean * ref[e + 1] for mean, ref in zip(means, (c0, c1, c2))]
-            turned = half_turn(plus[1])
-            minus = [
-                prev_row(plus[0]),
-                jnp.where(low_lanes, before, turned),
-                prev_lane(plus[2]),
-            ]
-            total = accumulate(plus + minus) + STORAGE + snk[e + 1]
-            scale = inverse(total)
+            return half_turn(value), next_lane(value)
+
+        def along(e, now, after):
+            value = prop[e + 1]
+            x_side, b_side = beside(value, now, after)
+            return face_mean(value, x_side) * c1[e + 1], face_mean(value, b_side) * c2[e + 1]
+
+        def close(e, before, plus, turned):
+            value = prop[e + 1]
+            plus = [face_mean(value, next_row(value)) * c0[e + 1], *plus]
+            minus = [prev_row(plus[0]), jnp.where(low_lanes, before, turned[0]), turned[1]]
+            scale = inverse(accumulate(plus + minus) + STORAGE + snk[e + 1])
             for dim in range(3):
                 coeffs[2 * dim, e + 1] = scale * plus[dim]
                 coeffs[2 * dim + 1, e + 1] = scale * minus[dim]
             force[e + 1] = scale * (src[e + 1] + STORAGE * v0[e + 1])
-            return turned, after
-
-        for first, stop in ranges:
-            run(step, first, stop, start)
-
-    @pl.when(jnp.logical_not(is_press))
-    def _():
+
+        def step(e, carry):
+            before, plus, turned, now, after = carry
+            close(e - 1, before, plus, turned)
+            later = turns(e + 2)
+            fresh = along(e, now, after)
+            return turned[0], fresh, (half_turn(fresh[0]), prev_lane(fresh[1])), after, later
+
+        now, after = turns(first), turns(first + 1)
+        before = blank
+        if first > 0:
+            before = half_turn(along(first - 1, turns(first - 1), now)[0])
+        fresh = along(first, now, after)
+        carry = (
+            before, fresh, (half_turn(fresh[0]), prev_lane(fresh[1])), after, turns(first + 2)
+        )
+        before, plus, turned, _, _ = run(step, first + 1, stop, carry)
+        close(stop - 1, before, plus, turned)
+
+    def heat_range(first, stop):
+        def turns(e):
+            value, level = prop[e + 1], fluid[e + 1]
+            return half_turn(value), next_lane(value), half_turn(level), next_lane(level)
+
         def pair_of(mean, flow, field):
             speed = flow * field
             gain = mean + jnp.maximum(speed, 0.0)
             return gain, gain - speed
 
-        def start(first):
-            here = [half_turn(ref[first + 1]) for ref in (prop, fluid)]
-            if first == 0:
-                return (blank, blank), here
-            means = [
-                face_mean(ref[first], jnp.where(low_lanes, half_turn(ref[first]), after))
-                for ref, after in zip((prop, fluid), here)
-            ]
-            gain, loss = pair_of(means[0], means[1], c1[first])
-            return (half_turn(gain), half_turn(loss)), here
+        def along(e, now, after):
+            value, level = prop[e + 1], fluid[e + 1]
+            x_value, b_value = beside(value, now[:2], after[:2])
+            x_level, b_level = beside(level, now[2:], after[2:])
+            return (
+                pair_of(face_mean(value, x_value), face_mean(level, x_level), c1[e + 1]),
+                pair_of(face_mean(value, b_value), face_mean(level, b_level), c2[e + 1]),
+            )
+
+        def turned_pairs(x_pair, b_pair):
+            return (
+                half_turn(x_pair[0]), half_turn(x_pair[1]),
+                prev_lane(b_pair[0]), prev_lane(b_pair[1]),
+            )
+
+        def open_cell(e, x_pair, b_pair):
+            coeffs[2, e + 1] = x_pair[1]
+            coeffs[4, e + 1] = b_pair[1]
+            return snk[e + 1] + x_pair[0] + b_pair[0]
+
+        def close(e, before, turned, total):
+            coeffs[3, e + 1] = jnp.where(low_lanes, before[0], turned[0])
+            coeffs[5, e + 1] = turned[2]
+            diag[e + 1] = total + turned[3] + jnp.where(low_lanes, before[1], turned[1])
 
         def step(e, carry):
-            before, here = carry
-            after = [half_turn(ref[e + 2]) for ref in (prop, fluid)]
+            before, turned, total, now, after = carry
+            close(e - 1, before, turned, total)
+            later = turns(e + 2)
+            x_pair, b_pair = along(e, now, after)
+            total = open_cell(e, x_pair, b_pair)
+            return turned[:2], turned_pairs(x_pair, b_pair), total, after, later
+
+        def row_step(e, carry):
             value, level = prop[e + 1], fluid[e + 1]
-            total = snk[e + 1]
             gain, loss = pair_of(
                 face_mean(value, next_row(value)), face_mean(level, next_row(level)), c0[e + 1]
             )
             coeffs[0, e + 1] = loss
             coeffs[1, e + 1] = prev_row(gain)
-            total += gain + prev_row(loss)
-            gain, loss = pair_of(
-                face_mean(value, jnp.where(not_last, next_lane(value), 0.0)),
-                face_mean(level, jnp.where(not_last, next_lane(level), 0.0)),
-                c2[e + 1],
-            )
-            coeffs[4, e + 1] = loss
-            coeffs[5, e + 1] = prev_lane(gain)
-            total += gain + prev_lane(loss)
-            gain, loss = pair_of(
-                face_mean(value, jnp.where(low_lanes, here[0], after[0])),
-                face_mean(level, jnp.where(low_lanes, here[1], after[1])),
-                c1[e + 1],
-            )
-            turned = half_turn(gain), half_turn(loss)
-            coeffs[2, e + 1] = loss
-            coeffs[3, e + 1] = jnp.where(low_lanes, before[0], turned[0])
-            diag[e + 1] = total + gain + jnp.where(low_lanes, before[1], turned[1])
-            force[e + 1] = src[e + 1]
-            return turned, after
-
+            diag[e + 1] += gain + prev_row(loss)
+            return carry
+
+        now, after = turns(first), turns(first + 1)
+        before = (blank, blank)
+        if first > 0:
+            gain, loss = along(first - 1, turns(first - 1), now)[0]
+            before = half_turn(gain), half_turn(loss)
+        x_pair, b_pair = along(first, now, after)
+        total = open_cell(first, x_pair, b_pair)
+        carry = (before, turned_pairs(x_pair, b_pair), total, after, turns(first + 2))
+        before, turned, total, _, _ = run(step, first + 1, stop, carry)
+        close(stop - 1, before, turned, total)
+        run(row_step, first, stop, 0)
+
+    @pl.when(is_press)
+    def _():
         for first, stop in ranges:
-            run(step, first, stop, start)
+            press_range(first, stop)
+
+    @pl.when(jnp.logical_not(is_press))
+    def _():
+        for first, stop in ranges:
+            heat_range(first, stop)
 
 
 def inner_kernel(where_ref, perm_ref, cond_ref, across, *refs):
@@ -704,13 +755,13 @@
 
     lax.fori_loop(0, tiles, fill, 0, unroll=8)
     made = (coeffs, force, diag, fluid)
-    face_terms(cells, made, is_press, [(side, ext - side)], UNROLL)
+    face_terms(cells, made, is_press, [(side, ext - side)])
 
 
 def main_kernel(where_ref, perm_ref, cond_ref, from_left, from_right, *refs):
-    v1, v2, boundary = refs[12:15]
-    coeffs, force, diag, fluid = refs[15:19]
-    cells = refs[19:]
+    v1, v2 = refs[12:14]
+    coeffs, force, diag, fluid = refs[14:18]
+    cells = refs[18:]
     v0 = cells[0]
     is_press = where_ref[0] == 0
     is_low = where_ref[1] == 0
@@ -734,60 +785,85 @@
         put_level(fluid, cells, e, slice(None))
     clear((v1, v2), (0, ext + 1))
     made = (coeffs, force, diag, fluid)
-    face_terms(cells, made, is_press, [(0, side + 1), (ext - side - 1, ext)], UNROLL)
+    face_terms(cells, made, is_press, [(0, side + 1), (ext - side - 1, ext)])
     chebyshev, explicit = sweep_weights()
-    for chosen, weights, centre in (
-        (is_press, chebyshev, None),
-        (jnp.logical_not(is_press), explicit, diag),
+    src = cells[6]
+    for chosen, weights, centre, drive in (
+        (is_press, chebyshev, None, force),
+        (jnp.logical_not(is_press), explicit, diag, src),
     ):
 
         @pl.when(chosen)
-        def _(weights=weights, centre=centre):
+        def _(weights=weights, centre=centre, force=drive):
             (w0, u0), (w1, u1) = weights[:2]
             sweep((0, ext), coeffs, force, centre, v0, v0, store_in(v1), w0, u0)
             sweep((0, ext), coeffs, force, centre, v1, v0, store_in(v2), w1, u1)
 
-    def send(e, carry):
-        value = v2[e + 1]
-        boundary[:, lanes_at(e)] = jnp.where(is_low, value[30:32], value[8:10])
-        return carry
-
-    lax.fori_loop(0, ext, send, 0, unroll=UNROLL)
-
-
-def finish_kernel(where_ref, v1, v2, coeffs, force, diag, boundary, done, out, now, later):
-    del done
+
+def finish_kernel(
+    where_ref, v1, v2_in, received_in, coeffs, force, src, diag, boundary, edge, rim,
+    out_ref, now, received, later, out, tile, sems,
+):
+    del v2_in, received_in
     is_press = where_ref[0] == 0
     is_low = where_ref[1] == 0
-    ext = v2.shape[0] - 2
+    ext = now.shape[0] - 2
     side = XH // 2
-    rim_at = pl.multiple_of(jnp.where(is_low, 32, 0), 8)
-    blank = jnp.zeros(v2.shape[1:], jnp.float32)
-    for ref in (now, later):
-        ref[0] = blank
-        ref[ext + 1] = blank
+    tiles = ext - XH
+    rows = rim_rows(is_low)
+    clear((later,), (0, ext + 1))
+    lane = lane_index((32, LANES))
+    mine = rim[:, LANES:]
+    start = boundary.shape[1] - 16 * LANES
+    theirs = jnp.concatenate(
+        [boundary[:, start + index * LANES : start + (index + 1) * LANES] for index in range(16)],
+        0,
+    )
+    plane = jnp.where(
+        is_low,
+        jnp.where(lane < 32, mine, theirs),
+        jnp.where(lane < 32, pltpu.roll(theirs, 96, 1), pltpu.roll(mine, 32, 1)),
+    )
+    here = edge[0]
+    beside = jnp.where(lane < HALF, half_turn(here), half_turn(plane))
+    tile[...] = jnp.where(is_press, face_mean(here, beside), edge[1] * (here - beside))
+    last_tile = pl.ds((tiles - 1) * LANES, LANES)
+    tile_copy = pltpu.make_async_copy(tile, received.at[0, 1, :, last_tile], sems.at[PARTS])
+    tile_copy.start()
 
     def fill(e, carry):
-        now[e + 1] = v2[e + 1]
-        now[e + 1, pl.ds(rim_at, 8), :] = placed_pair(boundary[:, lanes_at(e)], is_low)
+        now[e + 1, rows, :] = placed_pair(boundary[:, lanes_at(e)], is_low)
         return carry
 
-    lax.fori_loop(0, ext, fill, 0, unroll=UNROLL)
+    lax.fori_loop(0, ext, fill, 0, unroll=17)
     chebyshev, explicit = sweep_weights()
 
     def put_out(e, value):
-        out[0, :, lanes_at(e - side)] = jnp.where(is_low, value[0:32], value[8:40])
-
-    for chosen, weights, centre in (
-        (is_press, chebyshev, None),
-        (jnp.logical_not(is_press), explicit, diag),
+        out[:, lanes_at(e - side)] = jnp.where(is_low, value[0:32], value[8:40])
+
+    for chosen, weights, centre, drive in (
+        (is_press, chebyshev, None, force),
+        (jnp.logical_not(is_press), explicit, diag, src),
     ):
 
         @pl.when(chosen)
-        def _(weights=weights, centre=centre):
+        def _(weights=weights, centre=centre, force=drive):
             (w2, u2), (w3, u3) = weights[2:]
             sweep((0, ext), coeffs, force, centre, now, v1, store_in(later), w2, u2)
-            sweep((side, ext - side), coeffs, force, centre, later, now, put_out, w3, u3)
+            part = tiles // PARTS
+            copies = []
+            for index in range(PARTS):
+                first = side + index * part
+                sweep((first, first + part), coeffs, force, centre, later, now, put_out, w3, u3)
+                at = pl.ds(index * part * LANES, part * LANES)
+                copy = pltpu.make_async_copy(
+                    out.at[:, at], out_ref.at[0, :, at], sems.at[index]
+                )
+                copy.start()
+                copies.append(copy)
+            for copy in copies:
+                copy.wait()
+    tile_copy.wait()
 
 
 def regrouped(pieces):
@@ -804,8 +880,9 @@
     return result
 
 
-def faces_kernel(where_ref, own, other, plane_ref, rock, out_ref, token, field, rim, out, sems):
-    token[...] = jnp.zeros(token.shape, jnp.float32)
+def faces_kernel(
+    where_ref, own, other, own_rim, rock, out_ref, edge, field, rim, out, sems
+):
     is_press = where_ref[0] == 0
     is_low = where_ref[1] == 0
     tiles = out.shape[2] // LANES
@@ -819,14 +896,13 @@
     pieces = []
     for par in range(2):
         pieces += ordered(
-            own[par * groups : (par + 1) * groups, extra : extra + LANES],
+            own_rim[par * groups : (par + 1) * groups, :LANES],
             other[par * groups : (par + 1) * groups, extra : extra + LANES],
         )
     for q, value in enumerate(regrouped(pieces)):
         rim[q] = value
-    plane = ordered(own[:, extra + LANES :], plane_ref[:, :LANES])
     lane = lane_index((32, LANES))
-    field[tiles, 0:32, :] = jnp.where(lane < 32, plane[0], pltpu.roll(plane[1], 32, 1))
+    field[tiles] = jnp.zeros(field.shape[1:], jnp.float32)
 
     def gather(group, carry):
         pieces = []
@@ -842,53 +918,55 @@
     low_lanes = lane < HALF
     not_last = lane % W != W - 1
 
-    def around(t):
+    def around(t, turned):
         value = field[t]
         here = value[0:32]
-        after = field[t + 1, 0:32, :]
-        return here, (
-            next_row(value)[0:32],
-            jnp.where(low_lanes, half_turn(here), half_turn(after)),
-            next_lane(here),
-        )
+        after = half_turn(field[t + 1, 0:32, :])
+        others = next_row(value)[0:32], jnp.where(low_lanes, turned, after), next_lane(here)
+        return here, others, after
 
     def press(t, carry):
-        here, others = around(t)
+        here, others, after = around(t, carry)
         others = (others[0], others[1], jnp.where(not_last, others[2], 0.0))
         for dim in range(3):
             out[dim, :, lanes_at(t)] = face_mean(here, others[dim])
-        return carry
+        return after
 
     def heat(t, carry):
-        here, others = around(t)
-        stone = rock[t + side + 1]
-        after = rock[t + side + 2]
+        here, others, after = around(t, carry[0])
+        stone = rock[t + side + 1, own_rows, :]
+        stone_after = half_turn(rock[t + side + 2, own_rows, :])
+        rim_row = jnp.where(is_low, rock[t + side + 1, 32:33, :], 0.0)
         near = (
-            next_row(stone),
-            jnp.where(tall_low, half_turn(stone), half_turn(after)),
-            jnp.where(tall_not_last, next_lane(stone), 0.0),
+            jnp.where(last_row, rim_row, next_row(stone)),
+            jnp.where(low_lanes, carry[1], stone_after),
+            jnp.where(not_last, next_lane(stone), 0.0),
         )
         for dim in range(3):
             mean = face_mean(stone, near[dim])
-            mean = jnp.where(is_low, mean[0:32], mean[8:40])
             out[dim, :, lanes_at(t)] = mean * (here - others[dim])
-        return carry
-
-    tall_lane = lane_index(rock.shape[1:])
-    tall_low = tall_lane < HALF
-    tall_not_last = tall_lane % W != W - 1
+        return after, stone_after
+
+    own_rows = pl.ds(pl.multiple_of(jnp.where(is_low, 0, 8), 8), 32)
+    last_row = lax.broadcasted_iota(jnp.int32, (32, LANES), 0) == 31
     part = tiles // PARTS
     copies = []
+    edge[0] = field[tiles - 1, 0:32, :]
+    stone = rock[tiles - 1 + side + 1, own_rows, :]
+    stone_after = half_turn(rock[tiles + side + 1, own_rows, :])
+    edge[1] = face_mean(stone, jnp.where(low_lanes, half_turn(stone), stone_after))
     for index in range(PARTS):
         first = index * part
 
         @pl.when(is_press)
         def _(first=first):
-            lax.fori_loop(first, first + part, press, 0, unroll=8)
+            start = half_turn(field[first, 0:32, :])
+            lax.fori_loop(first, first + part, press, start, unroll=16)
 
         @pl.when(jnp.logical_not(is_press))
         def _(first=first):
-            lax.fori_loop(first, first + part, heat, 0, unroll=8)
+            start = half_turn(field[first, 0:32, :]), half_turn(rock[first + side + 1, own_rows, :])
+            lax.fori_loop(first, first + part, heat, start, unroll=16)
 
         at = pl.ds(first * LANES, part * LANES)
         copy = pltpu.make_async_copy(out.at[:, :, at], out_ref.at[0, :, :, at], sems.at[index])
@@ -904,6 +982,7 @@
     ext = tiles + XH
     wide = XH * W
     groups = tiles // 4
+    loaded = [held(value) for value in (states, coupled, facies, injectors, producers)]
     place = jnp.stack([lax.axis_index("code"), lax.axis_index("ba")]).astype(jnp.int32)
     count = lax.axis_size("aa")
     up = [(i, i + 1) for i in range(count - 1)]
@@ -916,30 +995,35 @@
         for value in (states, coupled, facies, injectors, producers)
     ]
 
-    to_right, to_left, across, corners = pl.pallas_call(
+    corners = pl.pallas_call(
+        corner_kernel,
+        out_shape=in_vmem((2, 10 * wide)),
+        in_specs=[SM] + [HB] * 5,
+        out_specs=VM,
+        scratch_shapes=[
+            pltpu.VMEM((2, 8, wide), f32),
+            pltpu.VMEM((2, 3, 8, wide), f32),
+            pltpu.VMEM((2, 3, 8, wide), i32),
+            pltpu.SemaphoreType.DMA((10,)),
+        ],
+        compiler_params=LEAN,
+        cost_estimate=cost(1),
+        name="corner",
+    )(place, states, coupled, facies, injectors, producers)
+    corners = held(lax.ppermute(corners, "ba", swap))
+    to_right, to_left, across = pl.pallas_call(
         edges_kernel,
         out_shape=[
             in_vmem((rows, 7 * wide)),
             in_vmem((rows, 7 * wide)),
             in_vmem((2, 5 * cols)),
-            in_vmem((2, 10 * wide)),
         ],
-        in_specs=[SM] + [HB] * 5,
-        out_specs=[VM] * 4,
-        scratch_shapes=[
-            pltpu.VMEM((4, rows, wide), f32),
-            pltpu.VMEM((4, rows, wide), f32),
-            pltpu.VMEM((4, 8, cols), f32),
-            pltpu.VMEM((3, rows, wide), i32),
-            pltpu.VMEM((3, rows, wide), i32),
-            pltpu.VMEM((3, 8, cols), i32),
-            pltpu.SemaphoreType.DMA((21,)),
-        ],
+        in_specs=[SM] + [VM] * 5,
+        out_specs=[VM] * 3,
         compiler_params=LEAN,
-        cost_estimate=cost(1),
+        cost_estimate=cost(2),
         name="edges",
-    )(place, states, coupled, facies, injectors, producers)
-    corners = held(lax.ppermute(corners, "ba", swap))
+    )(place, *loaded)
     to_right, to_left, across = pl.pallas_call(
         pack_kernel,
         out_shape=[
@@ -958,30 +1042,24 @@
     from_across = held(lax.ppermute(across, "ba", swap))
 
     field = (ext + 2, rows + 8, LANES)
-    turned = in_vmem((32, (2 * groups + 2) * LANES))
-    turned_over = in_vmem((32, (2 * groups + 3) * LANES))
-    turned_own, turned_other, fluid, *cells = pl.pallas_call(
+    turned_own, turned_other, rim, fluid, *cells = pl.pallas_call(
         turn_kernel,
-        out_shape=[turned, turned_over]
+        out_shape=[
+            in_vmem((32, 2 * groups * LANES)),
+            in_vmem((32, (2 * groups + 1) * LANES)),
+            in_vmem((32, 2 * LANES)),
+        ]
         + [in_vmem(field)] * 9,
-        in_specs=[SM] * 3 + [HB] * 5 + [VM],
-        out_specs=[VM] * 11,
-        scratch_shapes=[
-            pltpu.VMEM(states.shape, f32),
-            pltpu.VMEM(coupled.shape, f32),
-            pltpu.VMEM(facies.shape, i32),
-            pltpu.VMEM(facies.shape, i32),
-            pltpu.VMEM(facies.shape, i32),
-            pltpu.SemaphoreType.DMA((5,)),
-        ],
-        compiler_params=params(10),
-        cost_estimate=cost(6),
+        in_specs=[SM] * 3 + [VM] * 6,
+        out_specs=[VM] * 12,
+        compiler_params=params(2),
+        cost_estimate=cost(1),
         name="turn",
     )(
-        place, perm_table, cond_table, states, coupled, facies, injectors, producers,
-        corners,
+        place, perm_table, cond_table, *loaded, across,
     )
     other = held(lax.ppermute(turned_other, ("code", "ba"), opposite))
+    own = held(lax.ppermute(turned_own, "code", swap))
     coeffs, force, diag, fluid, *cells = pl.pallas_call(
         inner_kernel,
         out_shape=[in_vmem((6,) + field)] + [in_vmem(field)] * 11,
@@ -989,40 +1067,49 @@
         out_specs=[VM] * 12,
         input_output_aliases={4 + index: 3 + index for index in range(9)},
         compiler_params=params(2),
-        cost_estimate=cost(6),
+        cost_estimate=cost(10),
         name="inner",
     )(place, perm_table, cond_table, from_across, fluid, *cells)
-    turned_own, plane = pl.pallas_call(
+    rim = pl.pallas_call(
         plane_kernel,
-        out_shape=[turned, in_vmem((32, 5 * LANES))],
+        out_shape=in_vmem(rim.shape),
         in_specs=[SM] + [VM] * 4,
-        out_specs=[VM] * 2,
+        out_specs=VM,
+        input_output_aliases={2: 0},
         compiler_params=LEAN,
         cost_estimate=cost(1),
         name="plane",
-    )(place, from_right, turned_own, from_left, force)
-    own = held(lax.ppermute(turned_own, "code", swap))
-    plane_over = held(lax.ppermute(plane, ("code", "ba"), opposite))
-    v1, v2, boundary, coeffs, force, diag, fluid, *cells = pl.pallas_call(
+    )(place, from_right, rim, from_left, force)
+    rim = held(lax.ppermute(rim, "code", swap))
+
+    v1, v2, coeffs, force, diag, fluid, *cells = pl.pallas_call(
         main_kernel,
-        out_shape=[in_vmem(field), in_vmem(field), in_vmem((2, ext * LANES))]
+        out_shape=[in_vmem(field), in_vmem(field)]
         + [in_vmem((6,) + field)]
         + [in_vmem(field)] * 11,
         in_specs=[SM] * 3 + [VM] * 14,
-        out_specs=[VM] * 15,
-        input_output_aliases={5 + index: 3 + index for index in range(12)},
+        out_specs=[VM] * 14,
+        input_output_aliases={5 + index: 2 + index for index in range(12)},
         compiler_params=params(2),
-        cost_estimate=cost(6),
+        cost_estimate=cost(10),
         name="main",
     )(
         place, perm_table, cond_table, from_left, from_right,
         coeffs, force, diag, fluid, *cells,
     )
-    rock = cells[2]
+    boundary = pl.pallas_call(
+        send_kernel,
+        out_shape=in_vmem((2, (ext + 16) * LANES)),
+        in_specs=[SM] + [VM] * 2,
+        out_specs=VM,
+        compiler_params=LEAN,
+        cost_estimate=cost(1),
+        name="send",
+    )(place, v2, rim)
     boundary = held(lax.ppermute(boundary, "ba", swap))
-    received, token = pl.pallas_call(
+    received, edge = pl.pallas_call(
         faces_kernel,
-        out_shape=[jax.ShapeDtypeStruct(coupled.shape, f32), in_vmem((8, LANES))],
+        out_shape=[jax.ShapeDtypeStruct(coupled.shape, f32), in_vmem((2, 32, LANES))],
         in_specs=[SM] + [VM] * 4,
         out_specs=[HB, VM],
         scratch_shapes=[
@@ -1032,19 +1119,30 @@
             pltpu.SemaphoreType.DMA((PARTS,)),
         ],
         compiler_params=params(8),
-        cost_estimate=cost(5),
+        cost_estimate=cost(6),
         name="faces",
-    )(place, own, other, plane_over, rock)
-    stepped = pl.pallas_call(
+    )(place, own, other, rim, cells[2])
+    received = pltpu.with_memory_space_constraint(received, pltpu.HBM)
+    stepped, _, received = pl.pallas_call(
         finish_kernel,
-        out_shape=jax.ShapeDtypeStruct(states.shape, f32),
-        in_specs=[SM] + [VM] * 7,
-        out_specs=VM,
-        scratch_shapes=[pltpu.VMEM(field, f32)] * 2,
-        compiler_params=params(8),
+        out_shape=[
+            jax.ShapeDtypeStruct(states.shape, f32),
+            in_vmem(field),
+            jax.ShapeDtypeStruct(coupled.shape, f32),
+        ],
+        in_specs=[SM] + [VM] * 2 + [HB] + [VM] * 7,
+        out_specs=[HB, VM, HB],
+        scratch_shapes=[
+            pltpu.VMEM(field, f32),
+            pltpu.VMEM(states.shape[1:], f32),
+            pltpu.VMEM((32, LANES), f32),
+            pltpu.SemaphoreType.DMA((PARTS + 1,)),
+        ],
+        input_output_aliases={2: 1, 3: 2},
+        compiler_params=params(5),
         cost_estimate=cost(6),
         name="finish",
-    )(place, v1, v2, coeffs, force, diag, boundary, token)
+    )(place, v1, v2, received, coeffs, force, cells[6], diag, boundary, edge, rim)
     return (stepped, received)
 
 

time: 47 us -> 40.7 us (0.87)
  the two profiles are of different devices: /device:TPU:11 before, /device:TPU:9 now
where the time goes in v3:
time: 40.7 us; the launch traced here: 40.5 us
  Pallas kernels  25.6 us (63%)
  starting transfers between devices  13 us (32%)
  between operations  0.94 us (2%)
  waiting for transfers between devices  0.75 us (2%)
    pallas_call x1, Pallas kernels, paired_body(): pl.pallas_call(inner_kernel, out_shape=[in_vmem((6,) + field)] + [in_vmem...  6.85 us
    pallas_call x1, Pallas kernels, paired_body(): pl.pallas_call(finish_kernel, out_shape=[jax.ShapeDtypeStruct(states.shap...  4.24 us
    pallas_call x1, Pallas kernels, paired_body(): pl.pallas_call(faces_kernel, out_shape=[jax.ShapeDtypeStruct(coupled.shap...  4.08 us
    pallas_call x1, Pallas kernels, paired_body(): pl.pallas_call(main_kernel, out_shape=[in_vmem(field), in_vmem(field)] +...  3.93 us
    ppermute x1, starting transfers between devices, paired_body(): from_left = held(lax.ppermute(to_right, 'aa', up))  3.14 us
    ppermute x1, starting transfers between devices, paired_body(): from_right = held(lax.ppermute(to_left, 'aa', down))  3.03 us
    ppermute x1, starting transfers between devices, paired_body(): own = held(lax.ppermute(turned_own, 'code', swap))  2.73 us
    pallas_call x1, Pallas kernels, paired_body(): pl.pallas_call(turn_kernel, out_shape=[in_vmem((32, 2 * groups * LANES)),...  2.56 us
  transfers between devices with their start and end apart: 8, of which 2 were waited for; matrix products, arithmetic and copies ran while one was open for 0% of the time, Pallas kernels for 47%

profile of v3, /device:TPU:9, one launch (start us, length us, event | category | flops | bytes accessed | tf_op | source)
XLA Modules:
  0.0 40.5 jit_solution(8669090348466200167)
XLA Ops:
  0.6 0.1 pad_add_fusion.where_ref
  0.7 0.0 copy-start
  0.7 0.0 copy-start.1
  0.7 0.0 copy-start.2
  0.7 0.0 copy-start.3
  0.7 0.0 copy-start.4
  0.7 1.7 %corner.1 = f32[2,2560]{1,0:T(2,128)S(1)} custom-call(s32[2]{0:T(128)S(1)} %pad_add_fusion.where_ref, f32[1,32,8192]{2,1,0:T(8,128)} %st.5, f32[1,3,32,8192]{3,2,1,0:T(8,128)} %cp.5, s32[1,32,8192]{2,1,0:T(8,128)} %fa.5, s32[1,32,8192]{2,1,0:T(8,128)} %ij.5, s32[1,32,8192]{2,1,0:T(8,128)} %pr.5), custom_call_target="tpu_custom_call" | custom-call | flops 1150000000 | bytes 3600000 | tf_op jit(solution)/shard_map/corner/pallas_call | solution.py:998
  2.5 1.3 %collective-permute-start = (f32[2,2560]{1,0:T(2,128)S(1)}, f32[2,2560]{1,0:T(2,128)S(1)}, u32[]{:S(2)}, u32[]{:S(2)}) collective-permute-start(f32[2,2560]{1,0:T(2,128)S(1)} %corner.1), channel_id=1, source_target_pairs={{0,1},{1,0},{2,3},{3,2},{4,5},{5,4},{6,7},{7,6},{8,9},{9,8},{10,11... | collective-permute-start | bytes 61448 | tf_op jit(solution)/shard_map/ppermute | solution.py:1013
  3.8 0.0 copy-done
  3.8 0.0 copy-done.1
  3.8 0.0 copy-done.2
  3.8 0.0 copy-done.3
  3.8 0.1 copy-done.4
  3.9 0.8 %edges.1 = (f32[32,1792]{1,0:T(8,128)S(1)}, f32[32,1792]{1,0:T(8,128)S(1)}, f32[2,40960]{1,0:T(2,128)S(1)}) custom-call(s32[2]{0:T(128)S(1)} %pad_add_fusion.where_ref, f32[1,32,8192]{2,1,0:T(8,128)S(1)} %copy-done.1, f32[1,3,32,8192]{3,2,1,0:T(8,128)S(1)} %copy-done, s32[1,32,8192]{2,1,0:T(8,128)S(1)} %copy-done.2, s32[1,32,8192]{2,1,0:T(8,128)S(1)} %copy-done.3, ...), custom_call_target="tpu_custom_call" | custom-call | flops 2300000000 | bytes 7200000 | tf_op jit(solution)/shard_map/edges/pallas_call | solution.py:1014
  4.7 0.5 %collective-permute-done.corners = f32[2,2560]{1,0:T(2,128)S(1)} collective-permute-done((f32[2,2560]{1,0:T(2,128)S(1)}, f32[2,2560]{1,0:T(2,128)S(1)}, u32[]{:S(2)}, u32[]{:S(2)}) %collective-permute-start) | collective-permute-done | bytes 20512 | tf_op jit(solution)/shard_map/ppermute | solution.py:1013
  5.2 0.0 copy-start.5
  5.2 0.0 copy-start.6
  5.2 0.1 pack.1
  5.2 1.3 %collective-permute-start.3 = (f32[2,40960]{1,0:T(2,128)S(1)}, f32[2,40960]{1,0:T(2,128)S(1)}, u32[]{:S(2)}, u32[]{:S(2)}) collective-permute-start(f32[2,40960]{1,0:T(2,128)S(1)} %get-tuple-element.48.corners), channel_id=1, source_target_pairs={{0,1},{1,0},{2,3},{3,2},{4,5},{5,4},{6,7},{7,6},{8,9},{9,8},{10,11... | collective-permute-start | bytes 983048 | tf_op jit(solution)/shard_map/ppermute | solution.py:1042
  6.5 3.1 %collective-permute-start.1 = (f32[32,1920]{1,0:T(8,128)S(1)}, f32[32,1920]{1,0:T(8,128)S(1)}, u32[]{:S(2)}, u32[]{:S(2)}) collective-permute-start(f32[32,1920]{1,0:T(8,128)S(1)} %get-tuple-element.46), channel_id=1, source_target_pairs={{0,2},{2,4},{4,6},{6,8},{8,10},{10,12},{12,14},{1,3},{3,5},{5,7},{... | collective-permute-start | bytes 737288 | tf_op jit(solution)/shard_map/ppermute | solution.py:1040
  9.7 3.0 %collective-permute-start.2 = (f32[32,1920]{1,0:T(8,128)S(1)}, f32[32,1920]{1,0:T(8,128)S(1)}, u32[]{:S(2)}, u32[]{:S(2)}) collective-permute-start(f32[32,1920]{1,0:T(8,128)S(1)} %get-tuple-element.47), channel_id=1, source_target_pairs={{2,0},{4,2},{6,4},{8,6},{10,8},{12,10},{14,12},{3,1},{5,3},{7,5},{... | collective-permute-start | bytes 737288 | tf_op jit(solution)/shard_map/ppermute | solution.py:1041
  12.7 0.0 copy-done.5
  12.7 0.0 copy-done.6
  12.7 2.6 %turn.1 = (f32[32,4096]{1,0:T(8,128)S(1)}, f32[32,4224]{1,0:T(8,128)S(1)}, f32[32,256]{1,0:T(8,128)S(1)}, f32[70,40,128]{2,1,0:T(8,128)S(1)}, f32[70,40,128]{2,1...) custom-call(s32[2]{0:T(128)S(1)} %pad_add_fusion.where_ref, ...), custom_call_target="tpu_custom_call" | custom-call | flops 1150000000 | bytes 3600000 | tf_op jit(solution)/shard_map/turn/pallas_call | solution.py:1045
  15.3 2.7 %collective-permute-start.4 = (f32[32,4096]{1,0:T(8,128)S(1)}, f32[32,4096]{1,0:T(8,128)S(1)}, u32[]{:S(2)}, u32[]{:S(2)}) collective-permute-start(f32[32,4096]{1,0:T(8,128)S(1)} %get-tuple-element.72), channel_id=1, source_target_pairs={{0,16},{16,0},{1,17},{17,1},{2,18},{18,2},{3,19},{19,3},{4,20},{20... | collective-permute-start | bytes 1572872 | tf_op jit(solution)/shard_map/ppermute | solution.py:1062
  18.0 0.2 collective-permute-start.5
  18.2 0.0 collective-permute-done.3.across
  18.2 6.8 %inner.1 = (f32[6,70,40,128]{3,2,1,0:T(8,128)S(1)}, f32[70,40,128]{2,1,0:T(8,128)S(1)}, f32[70,40,128]{2,1,0:T(8,128)S(1)}, f32[70,40,128]{2,1,0:T(8,128)S(1)}, ...) custom-call(s32[2]{0:T(128)S(1)} %pad_add_fusion.where_ref, ...), custom_call_target="tpu_custom_call", output_to_operand_aliasing={{3}: (4, {}), {4}: (5, {}), {5}: (6, {}), {6}: (7, {}), {7}... | custom-call | flops 11500000256 | bytes 36000000 | tf_op jit(solution)/shard_map/inner/pallas_call | solution.py:1063
  25.1 0.0 collective-permute-done.1.from_left.rest_0_
  25.1 0.0 collective-permute-done.2.from_right
  25.1 0.6 %plane.1 = f32[32,256]{1,0:T(8,128)S(1)} custom-call(s32[2]{0:T(128)S(1)} %pad_add_fusion.where_ref, f32[32,1920]{1,0:T(8,128)S(1)} %collective-permute-done.2.from_right, f32[32,256]{1,0:T(8,128)S(1)} %get-tuple-element.74.own_in, f32[32,1920]{1,0:T(8,128)S(1)} %collective-permute-done.1.from_left.rest_0_, ...), custom_call_target="tpu_custom_call", output_to_operand_aliasing={{}: (2, {})} | custom-call | flops 1150000000 | bytes 3600000 | tf_op jit(solution)/shard_map/plane/pallas_call | solution.py:1073
  25.7 0.1 collective-permute-start.6
  25.8 3.9 %main.1 = (f32[70,40,128]{2,1,0:T(8,128)S(1)}, f32[70,40,128]{2,1,0:T(8,128)S(1)}, f32[6,70,40,128]{3,2,1,0:T(8,128)S(1)}, f32[70,40,128]{2,1,0:T(8,128)S(1)}, f...) custom-call(s32[2]{0:T(128)S(1)} %pad_add_fusion.where_ref, ...), custom_call_target="tpu_custom_call", output_to_operand_aliasing={{2}: (5, {}), {3}: (6, {}), {4}: (7, {}), {5}: (8, {}), {6}... | custom-call | flops 11500000256 | bytes 36000000 | tf_op jit(solution)/shard_map/main/pallas_call | solution.py:1085
  29.8 0.0 collective-permute-done.6.own_rim.own.rim
  29.8 0.6 %send.1 = f32[2,10752]{1,0:T(2,128)S(1)} custom-call(s32[2]{0:T(128)S(1)} %pad_add_fusion.where_ref, f32[70,40,128]{2,1,0:T(8,128)S(1)} %get-tuple-element.71.v2.v2_in, f32[32,256]{1,0:T(8,128)S(1)} %collective-permute-done.6.own_rim.own.rim), custom_call_target="tpu_custom_call" | custom-call | flops 1150000000 | bytes 3600000 | tf_op jit(solution)/shard_map/send/pallas_call | solution.py:1100
  30.4 1.3 %collective-permute-start.7 = (f32[2,10752]{1,0:T(2,128)S(1)}, f32[2,10752]{1,0:T(2,128)S(1)}, u32[]{:S(2)}, u32[]{:S(2)}) collective-permute-start(f32[2,10752]{1,0:T(2,128)S(1)} %send.1), channel_id=1, source_target_pairs={{0,1},{1,0},{2,3},{3,2},{4,5},{5,4},{6,7},{7,6},{8,9},{9,8},{10,11... | collective-permute-start | bytes 258056 | tf_op jit(solution)/shard_map/ppermute | solution.py:1109
  31.7 0.0 collective-permute-done.4.own
  31.7 0.3 collective-permute-done.5.other
  32.0 4.1 %faces.1 = (f32[1,3,32,8192]{3,2,1,0:T(8,128)}, f32[2,32,128]{2,1,0:T(8,128)S(1)}) custom-call(s32[2]{0:T(128)S(1)} %pad_add_fusion.where_ref, f32[32,4096]{1,0:T(8,128)S(1)} %collective-permute-done.4.own, f32[32,4224]{1,0:T(8,128)S(1)} %collective-permute-done.5.other, f32[32,256]{1,0:T(8,128)S(1)} %collective-permute-done.6.own_rim.own.rim, ...), custom_call_target="tpu_custom_call" | custom-call | flops 6899999744 | bytes 21600000 | tf_op jit(solution)/shard_map/faces/pallas_call | solution.py:1110
  36.1 0.0 collective-permute-done.7.boundary
  36.1 4.2 %finish.1 = (f32[1,32,8192]{2,1,0:T(8,128)}, f32[70,40,128]{2,1,0:T(8,128)S(1)}, f32[1,3,32,8192]{3,2,1,0:T(8,128)}) custom-call(s32[2]{0:T(128)S(1)} %pad_add_fusion.where_ref, f32[70,40,128]{2,1,0:T(8,128)S(1)} %get-tuple-element.70.v1, f32[70,40,128]{2,1,0:T(8,128)S(1)} %get-tuple-element.71.v2.v2_in, ...), custom_call_target="tpu_custom_call", output_to_operand_aliasing={{1}: (2, {}), {2}: (3, {})} | custom-call | flops 6899999744 | bytes 21600000 | tf_op jit(solution)/shard_map/finish/pallas_call | solution.py:1126
Async XLA Ops:
  0.7 3.0 %copy-start = (f32[1,3,32,8192]{3,2,1,0:T(8,128)S(1)}, f32[1,3,32,8192]{3,2,1,0:T(8,128)}, u32[]{:S(2)}) copy-start(f32[1,3,32,8192]{3,2,1,0:T(8,128)} %cp.5) | copy-start | bytes 9437188
  0.7 3.0 %copy-start.1 = (f32[1,32,8192]{2,1,0:T(8,128)S(1)}, f32[1,32,8192]{2,1,0:T(8,128)}, u32[]{:S(2)}) copy-start(f32[1,32,8192]{2,1,0:T(8,128)} %st.5) | copy-start | bytes 3145732
  0.7 3.0 %copy-start.2 = (s32[1,32,8192]{2,1,0:T(8,128)S(1)}, s32[1,32,8192]{2,1,0:T(8,128)}, u32[]{:S(2)}) copy-start(s32[1,32,8192]{2,1,0:T(8,128)} %fa.5) | copy-start | bytes 3145732
  0.7 3.0 %copy-start.3 = (s32[1,32,8192]{2,1,0:T(8,128)S(1)}, s32[1,32,8192]{2,1,0:T(8,128)}, u32[]{:S(2)}) copy-start(s32[1,32,8192]{2,1,0:T(8,128)} %ij.5) | copy-start | bytes 3145732
  0.7 3.2 %copy-start.4 = (s32[1,32,8192]{2,1,0:T(8,128)S(1)}, s32[1,32,8192]{2,1,0:T(8,128)}, u32[]{:S(2)}) copy-start(s32[1,32,8192]{2,1,0:T(8,128)} %pr.5) | copy-start | bytes 3145732
  2.5 2.7 %collective-permute-start = (f32[2,2560]{1,0:T(2,128)S(1)}, f32[2,2560]{1,0:T(2,128)S(1)}, u32[]{:S(2)}, u32[]{:S(2)}) collective-permute-start(f32[2,2560]{1,0:T(2,128)S(1)} %corner.1), channel_id=1, source_target_pairs={{0,1},{1,0},{2,3},{3,2},{4,5},{5,4},{6,7},{7,6},{8,9},{9,8},{10,11... | collective-permute-start | bytes 61448 | tf_op jit(solution)/shard_map/ppermute | solution.py:1013
  5.2 7.5 %copy-start.5 = (f32[6]{0:T(128)S(1)}, f32[6]{0:T(128)}, u32[]{:S(2)}) copy-start(f32[6]{0:T(128)} %perm_ref.5) | copy-start | bytes 76
  5.2 7.5 %copy-start.6 = (f32[6]{0:T(128)S(1)}, f32[6]{0:T(128)}, u32[]{:S(2)}) copy-start(f32[6]{0:T(128)} %cond_ref.5) | copy-start | bytes 76
  5.2 13.0 %collective-permute-start.3 = (f32[2,40960]{1,0:T(2,128)S(1)}, f32[2,40960]{1,0:T(2,128)S(1)}, u32[]{:S(2)}, u32[]{:S(2)}) collective-permute-start(f32[2,40960]{1,0:T(2,128)S(1)} %get-tuple-element.48.corners), channel_id=1, source_target_pairs={{0,1},{1,0},{2,3},{3,2},{4,5},{5,4},{6,7},{7,6},{8,9},{9,8},{10,11... | collective-permute-start | bytes 983048 | tf_op jit(solution)/shard_map/ppermute | solution.py:1042
  6.5 18.6 %collective-permute-start.1 = (f32[32,1920]{1,0:T(8,128)S(1)}, f32[32,1920]{1,0:T(8,128)S(1)}, u32[]{:S(2)}, u32[]{:S(2)}) collective-permute-start(f32[32,1920]{1,0:T(8,128)S(1)} %get-tuple-element.46), channel_id=1, source_target_pairs={{0,2},{2,4},{4,6},{6,8},{8,10},{10,12},{12,14},{1,3},{3,5},{5,7},{... | collective-permute-start | bytes 737288 | tf_op jit(solution)/shard_map/ppermute | solution.py:1040
  9.7 15.4 %collective-permute-start.2 = (f32[32,1920]{1,0:T(8,128)S(1)}, f32[32,1920]{1,0:T(8,128)S(1)}, u32[]{:S(2)}, u32[]{:S(2)}) collective-permute-start(f32[32,1920]{1,0:T(8,128)S(1)} %get-tuple-element.47), channel_id=1, source_target_pairs={{2,0},{4,2},{6,4},{8,6},{10,8},{12,10},{14,12},{3,1},{5,3},{7,5},{... | collective-permute-start | bytes 737288 | tf_op jit(solution)/shard_map/ppermute | solution.py:1041
  15.3 16.4 %collective-permute-start.4 = (f32[32,4096]{1,0:T(8,128)S(1)}, f32[32,4096]{1,0:T(8,128)S(1)}, u32[]{:S(2)}, u32[]{:S(2)}) collective-permute-start(f32[32,4096]{1,0:T(8,128)S(1)} %get-tuple-element.72), channel_id=1, source_target_pairs={{0,16},{16,0},{1,17},{17,1},{2,18},{18,2},{3,19},{19,3},{4,20},{20... | collective-permute-start | bytes 1572872 | tf_op jit(solution)/shard_map/ppermute | solution.py:1062
  18.0 14.0 %collective-permute-start.5 = (f32[32,4224]{1,0:T(8,128)S(1)}, f32[32,4224]{1,0:T(8,128)S(1)}, u32[]{:S(2)}, u32[]{:S(2)}) collective-permute-start(f32[32,4224]{1,0:T(8,128)S(1)} %get-tuple-element.73), channel_id=1, source_target_pairs={{0,17},{1,16},{16,1},{17,0},{2,19},{3,18},{18,3},{19,2},{4,21},{5,... | collective-permute-start | bytes 1622024 | tf_op jit(solution)/shard_map/ppermute | solution.py:1061
  25.7 4.0 %collective-permute-start.6 = (f32[32,256]{1,0:T(8,128)S(1)}, f32[32,256]{1,0:T(8,128)S(1)}, u32[]{:S(2)}, u32[]{:S(2)}) collective-permute-start(f32[32,256]{1,0:T(8,128)S(1)} %plane.1), channel_id=1, source_target_pairs={{0,16},{16,0},{1,17},{17,1},{2,18},{18,2},{3,19},{19,3},{4,20},{20... | collective-permute-start | bytes 98312 | tf_op jit(solution)/shard_map/ppermute | solution.py:1083
  30.4 5.7 %collective-permute-start.7 = (f32[2,10752]{1,0:T(2,128)S(1)}, f32[2,10752]{1,0:T(2,128)S(1)}, u32[]{:S(2)}, u32[]{:S(2)}) collective-permute-start(f32[2,10752]{1,0:T(2,128)S(1)} %send.1), channel_id=1, source_target_pairs={{0,1},{1,0},{2,3},{3,2},{4,5},{5,4},{6,7},{7,6},{8,9},{9,8},{10,11... | collective-permute-start | bytes 258056 | tf_op jit(solution)/shard_map/ppermute | solution.py:1109

commit v4 on v3

--- a/solution.py
+++ b/solution.py
@@ -414,8 +414,7 @@
         across[:, index * cols : (index + 1) * cols] = slot
 
 
-def pack_kernel(right_in, left_in, across_in, corners, to_right, to_left, across):
-    across[...] = across_in[...]
+def pack_kernel(right_in, left_in, corners, to_right, to_left):
     wide = XH * W
     for side, (source, target) in enumerate(((left_in, to_left), (right_in, to_right))):
         target[:, : 7 * wide] = source[...]
@@ -435,18 +434,39 @@
     state, codes, f0, f1, f2, inject, produce = cells
     v0[e + 1, rows, :] = state
     prop[e + 1, rows, :] = look_up(tables[0], codes)
-    rock[e + 1, rows, :] = look_up(tables[1], codes)
+    if is_press is not True:
+        rock[e + 1, rows, :] = look_up(tables[1], codes)
     c0[e + 1, rows, :] = f0
     c1[e + 1, rows, :] = f1
     c2[e + 1, rows, :] = f2
-    src[e + 1, rows, :] = jnp.where(is_press, 2.0 * inject - produce, 0.1 * inject)
-    snk[e + 1, rows, :] = jnp.where(is_press, produce, produce + inject)
+    if is_press is True:
+        src[e + 1, rows, :], snk[e + 1, rows, :] = 2.0 * inject - produce, produce
+    elif is_press is False:
+        src[e + 1, rows, :], snk[e + 1, rows, :] = 0.1 * inject, produce + inject
+    else:
+        src[e + 1, rows, :] = jnp.where(is_press, 2.0 * inject - produce, 0.1 * inject)
+        snk[e + 1, rows, :] = jnp.where(is_press, produce, produce + inject)
 
 
 def class_tables(is_press, perm_ref, cond_ref):
     perm = [perm_ref[index_c] for index_c in range(NF)]
     own = [jnp.where(is_press, perm[index_c], cond_ref[index_c]) for index_c in range(NF)]
     return own, perm
+
+
+def fill_own(refs, is_press, tables, own_rows, raw):
+    st, cp, fa, ij, pr = raw
+
+    def fill(t, carry):
+        at = lanes_at(t)
+        cells = (
+            st[0, :, at], fa[0, :, at] + 1, cp[0, 0, :, at], cp[0, 1, :, at], cp[0, 2, :, at],
+            ij[0, :, at].astype(jnp.float32), pr[0, :, at].astype(jnp.float32),
+        )
+        put_cells(refs, is_press, tables, t + XH // 2, own_rows, cells)
+        return carry
+
+    lax.fori_loop(0, st.shape[2] // LANES, fill, 0, unroll=8)
 
 
 def turn_kernel(
@@ -484,20 +504,11 @@
     rim[:, :LANES] = jnp.where(is_low, rims, 0.0)
     other[:, extra : extra + LANES] = jnp.where(is_low, 0.0, rims)
     refs = (v0, prop, rock, c0, c1, c2, src, snk)
-    is_press = where_ref[0] == 0
-    tables = class_tables(is_press, perm_ref, cond_ref)
-    tiles = st.shape[2] // LANES
-
-    def fill(t, carry):
-        at = lanes_at(t)
-        cells = (
-            st[0, :, at], fa[0, :, at] + 1, cp[0, 0, :, at], cp[0, 1, :, at], cp[0, 2, :, at],
-            ij[0, :, at].astype(jnp.float32), pr[0, :, at].astype(jnp.float32),
-        )
-        put_cells(refs, is_press, tables, t + XH // 2, own_rows, cells)
-        return carry
-
-    lax.fori_loop(0, tiles, fill, 0, unroll=8)
+    tables = class_tables(jnp.logical_not(is_heat), perm_ref, cond_ref)
+
+    @pl.when(is_heat)
+    def _():
+        fill_own(refs, False, tables, own_rows, (st, cp, fa, ij, pr))
 
 
 def plane_kernel(where_ref, from_right, own_in, *rest):
@@ -515,49 +526,43 @@
     own[:, own.shape[1] - LANES :] = jnp.where(keep == is_low, low, high)
 
 
-def send_kernel(where_ref, v2, own, boundary):
-    is_low = where_ref[1] == 0
-    ext = v2.shape[0] - 2
-
-    def send(e, carry):
-        value = v2[e + 1]
-        boundary[:, lanes_at(e)] = jnp.where(is_low, value[30:32], value[8:10])
-        return carry
-
-    lax.fori_loop(0, ext, send, 0, unroll=17)
+def send_kernel(boundary_in, rim, boundary):
+    del boundary_in
+    first = boundary.shape[1] - 16 * LANES
     for index in range(16):
-        start = (ext + index) * LANES
-        boundary[:, start : start + LANES] = own[
-            2 * index : 2 * index + 2, own.shape[1] - LANES :
-        ]
-
-
-def sweep(tiles, coeffs, force, diag, now, last, target, weight, pull):
+        start = first + index * LANES
+        boundary[:, start : start + LANES] = rim[2 * index : 2 * index + 2, LANES:]
+
+
+def sweep(tiles, coeffs, force, diag, now, last, target, weight, pull, rows=slice(None)):
     first, stop = tiles
-    low_lanes = lane_index((now.shape[1], LANES)) < HALF
+    shape = now[0, rows].shape
+    low_lanes = lane_index(shape) < HALF
 
     def step(e, carry):
         before, here = carry
-        value = now[e + 1]
-        after = half_turn(now[e + 2])
-        total = force[e + 1]
-        total += coeffs[0, e + 1] * next_row(value)
-        total += coeffs[1, e + 1] * prev_row(value)
-        total += coeffs[2, e + 1] * jnp.where(low_lanes, here, after)
-        total += coeffs[3, e + 1] * jnp.where(low_lanes, before, here)
-        total += coeffs[4, e + 1] * next_lane(value)
-        total += coeffs[5, e + 1] * prev_lane(value)
+        tall = now[e + 1]
+        value = tall[rows]
+        after = half_turn(now[e + 2, rows])
+        total = force[e + 1, rows]
+        total += coeffs[0, e + 1, rows] * next_row(tall)[rows]
+        total += coeffs[1, e + 1, rows] * prev_row(tall)[rows]
+        total += coeffs[2, e + 1, rows] * jnp.where(low_lanes, here, after)
+        total += coeffs[3, e + 1, rows] * jnp.where(low_lanes, before, here)
+        total += coeffs[4, e + 1, rows] * next_lane(value)
+        total += coeffs[5, e + 1, rows] * prev_lane(value)
         if diag is None:
             result = (1.0 + pull - weight) * value + weight * total
         else:
-            result = (1.0 + pull) * value + weight * (total - diag[e + 1] * value)
+            result = (1.0 + pull) * value + weight * (total - diag[e + 1, rows] * value)
         if pull != 0.0:
-            result -= pull * last[e + 1]
+            result -= pull * last[e + 1, rows]
         target(e, result)
         return here, after
 
     lax.fori_loop(
-        first, stop, step, (half_turn(now[first]), half_turn(now[first + 1])),
+        first, stop, step,
+        (half_turn(now[first, rows]), half_turn(now[first + 1, rows])),
         unroll=stop - first,
     )
 
@@ -595,6 +600,27 @@
     for ref in refs:
         for e in places:
             ref[e] = jnp.zeros(ref.shape[1:], jnp.float32)
+
+
+def flow_pair(mean, flow, field):
+    speed = flow * field
+    gain = mean + jnp.maximum(speed, 0.0)
+    return gain, gain - speed
+
+
+def heat_b_terms(cells, made, e):
+    v0, prop, rock, c0, c1, c2, src, snk = cells
+    coeffs, force, diag, fluid = made
+    value, level = prop[e + 1], fluid[e + 1]
+    not_last = lane_index(value.shape) % W != W - 1
+    gain, loss = flow_pair(
+        face_mean(value, jnp.where(not_last, next_lane(value), 0.0)),
+        face_mean(level, jnp.where(not_last, next_lane(level), 0.0)),
+        c2[e + 1],
+    )
+    coeffs[4, e + 1] = loss
+    coeffs[5, e + 1] = prev_lane(gain)
+    diag[e + 1] = snk[e + 1] + gain + prev_lane(loss)
 
 
 def face_terms(cells, made, is_press, ranges):
@@ -660,68 +686,58 @@
 
     def heat_range(first, stop):
         def turns(e):
-            value, level = prop[e + 1], fluid[e + 1]
-            return half_turn(value), next_lane(value), half_turn(level), next_lane(level)
-
-        def pair_of(mean, flow, field):
-            speed = flow * field
-            gain = mean + jnp.maximum(speed, 0.0)
-            return gain, gain - speed
+            return half_turn(prop[e + 1]), half_turn(fluid[e + 1])
 
         def along(e, now, after):
             value, level = prop[e + 1], fluid[e + 1]
-            x_value, b_value = beside(value, now[:2], after[:2])
-            x_level, b_level = beside(level, now[2:], after[2:])
-            return (
-                pair_of(face_mean(value, x_value), face_mean(level, x_level), c1[e + 1]),
-                pair_of(face_mean(value, b_value), face_mean(level, b_level), c2[e + 1]),
+            return flow_pair(
+                face_mean(value, jnp.where(low_lanes, now[0], after[0])),
+                face_mean(level, jnp.where(low_lanes, now[1], after[1])),
+                c1[e + 1],
             )
 
-        def turned_pairs(x_pair, b_pair):
-            return (
-                half_turn(x_pair[0]), half_turn(x_pair[1]),
-                prev_lane(b_pair[0]), prev_lane(b_pair[1]),
-            )
-
-        def open_cell(e, x_pair, b_pair):
-            coeffs[2, e + 1] = x_pair[1]
-            coeffs[4, e + 1] = b_pair[1]
-            return snk[e + 1] + x_pair[0] + b_pair[0]
-
-        def close(e, before, turned, total):
-            coeffs[3, e + 1] = jnp.where(low_lanes, before[0], turned[0])
-            coeffs[5, e + 1] = turned[2]
-            diag[e + 1] = total + turned[3] + jnp.where(low_lanes, before[1], turned[1])
-
-        def step(e, carry):
-            before, turned, total, now, after = carry
-            close(e - 1, before, turned, total)
-            later = turns(e + 2)
-            x_pair, b_pair = along(e, now, after)
-            total = open_cell(e, x_pair, b_pair)
-            return turned[:2], turned_pairs(x_pair, b_pair), total, after, later
-
-        def row_step(e, carry):
+        def close(e, before, turned):
             value, level = prop[e + 1], fluid[e + 1]
-            gain, loss = pair_of(
+            gain, loss = flow_pair(
                 face_mean(value, next_row(value)), face_mean(level, next_row(level)), c0[e + 1]
             )
             coeffs[0, e + 1] = loss
             coeffs[1, e + 1] = prev_row(gain)
-            diag[e + 1] += gain + prev_row(loss)
-            return carry
-
+            coeffs[3, e + 1] = jnp.where(low_lanes, before[0], turned[0])
+            total = diag[e + 1] + gain + prev_row(loss)
+            diag[e + 1] = total + turned[2] + jnp.where(low_lanes, before[1], turned[1])
+
+        def opened(e, now, after):
+            gain, loss = along(e, now, after)
+            coeffs[2, e + 1] = loss
+            return half_turn(gain), half_turn(loss), gain
+
+        def step(e, carry):
+            before, turned, now, after = carry
+            close(e - 1, before, turned)
+            later = turns(e + 2)
+            return turned[:2], opened(e, now, after), after, later
+
+        def b_steps(first, stop):
+            def b_step(e, carry):
+                heat_b_terms(cells, made, e)
+                return carry
+
+            if stop - first > 8:
+                lax.fori_loop(first, stop, b_step, 0, unroll=8)
+            else:
+                for e in range(first, stop):
+                    b_step(e, 0)
+
+        b_steps(first, stop)
         now, after = turns(first), turns(first + 1)
         before = (blank, blank)
         if first > 0:
-            gain, loss = along(first - 1, turns(first - 1), now)[0]
+            gain, loss = along(first - 1, turns(first - 1), now)
             before = half_turn(gain), half_turn(loss)
-        x_pair, b_pair = along(first, now, after)
-        total = open_cell(first, x_pair, b_pair)
-        carry = (before, turned_pairs(x_pair, b_pair), total, after, turns(first + 2))
-        before, turned, total, _, _ = run(step, first + 1, stop, carry)
-        close(stop - 1, before, turned, total)
-        run(row_step, first, stop, 0)
+        carry = (before, opened(first, now, after), after, turns(first + 2))
+        before, turned, _, _ = run(step, first + 1, stop, carry)
+        close(stop - 1, before, turned)
 
     @pl.when(is_press)
     def _():
@@ -734,7 +750,7 @@
             heat_range(first, stop)
 
 
-def inner_kernel(where_ref, perm_ref, cond_ref, across, *refs):
+def inner_kernel(where_ref, perm_ref, cond_ref, across, st, cp, fa, ij, pr, *refs):
     coeffs, force, diag, fluid = refs[-12:-8]
     cells = refs[-8:]
     is_press = where_ref[0] == 0
@@ -747,6 +763,11 @@
     tables = class_tables(is_press, perm_ref, cond_ref)
     clear(tuple(cells[:3]) + (fluid,), (0, 1, 2, ext - 1, ext, ext + 1))
 
+    @pl.when(is_press)
+    def _():
+        own_rows = pl.ds(pl.multiple_of(jnp.where(is_low, 0, 8), 8), 32)
+        fill_own(cells, True, tables, own_rows, (st, cp, fa, ij, pr))
+
     def fill(t, carry):
         read = lambda index, row: across[row : row + 1, lanes_at(t, index * cols)]
         put_cells(cells, is_press, tables, t + side, rows, rim_cells(is_low, read))
@@ -759,9 +780,9 @@
 
 
 def main_kernel(where_ref, perm_ref, cond_ref, from_left, from_right, *refs):
-    v1, v2 = refs[12:14]
-    coeffs, force, diag, fluid = refs[14:18]
-    cells = refs[18:]
+    v1, v2, boundary = refs[12:15]
+    coeffs, force, diag, fluid = refs[15:19]
+    cells = refs[19:]
     v0 = cells[0]
     is_press = where_ref[0] == 0
     is_low = where_ref[1] == 0
@@ -784,10 +805,16 @@
         put_cells(cells, is_press, tables, e, rim_rows(is_low), rim_cells(is_low, read))
         put_level(fluid, cells, e, slice(None))
     clear((v1, v2), (0, ext + 1))
+    clear((v2,), (1, ext))
+    for e in (0, ext - 1):
+        boundary[:, e * LANES : (e + 1) * LANES] = jnp.zeros((2, LANES), jnp.float32)
     made = (coeffs, force, diag, fluid)
     face_terms(cells, made, is_press, [(0, side + 1), (ext - side - 1, ext)])
     chebyshev, explicit = sweep_weights()
     src = cells[6]
+
+    is_high = jnp.logical_not(is_low)
+
     for chosen, weights, centre, drive in (
         (is_press, chebyshev, None, force),
         (jnp.logical_not(is_press), explicit, diag, src),
@@ -797,7 +824,17 @@
         def _(weights=weights, centre=centre, force=drive):
             (w0, u0), (w1, u1) = weights[:2]
             sweep((0, ext), coeffs, force, centre, v0, v0, store_in(v1), w0, u0)
-            sweep((0, ext), coeffs, force, centre, v1, v0, store_in(v2), w1, u1)
+            for placed, rows, edge in (
+                (is_low, slice(0, 32), slice(30, 32)), (is_high, slice(8, 40), slice(0, 2))
+            ):
+
+                @pl.when(placed)
+                def _(rows=rows, edge=edge):
+                    def put(e, value):
+                        v2[e + 1, rows] = value
+                        boundary[:, lanes_at(e)] = value[edge]
+
+                    sweep((1, ext - 1), coeffs, force, centre, v1, v0, put, w1, u1, rows)
 
 
 def finish_kernel(
@@ -839,8 +876,9 @@
     chebyshev, explicit = sweep_weights()
 
     def put_out(e, value):
-        out[:, lanes_at(e - side)] = jnp.where(is_low, value[0:32], value[8:40])
-
+        out[:, lanes_at(e - side)] = value
+
+    is_high = jnp.logical_not(is_low)
     for chosen, weights, centre, drive in (
         (is_press, chebyshev, None, force),
         (jnp.logical_not(is_press), explicit, diag, src),
@@ -849,20 +887,28 @@
         @pl.when(chosen)
         def _(weights=weights, centre=centre, force=drive):
             (w2, u2), (w3, u3) = weights[2:]
-            sweep((0, ext), coeffs, force, centre, now, v1, store_in(later), w2, u2)
-            part = tiles // PARTS
-            copies = []
-            for index in range(PARTS):
-                first = side + index * part
-                sweep((first, first + part), coeffs, force, centre, later, now, put_out, w3, u3)
-                at = pl.ds(index * part * LANES, part * LANES)
-                copy = pltpu.make_async_copy(
-                    out.at[:, at], out_ref.at[0, :, at], sems.at[index]
-                )
-                copy.start()
-                copies.append(copy)
-            for copy in copies:
-                copy.wait()
+            sweep((1, ext - 1), coeffs, force, centre, now, v1, store_in(later), w2, u2)
+            for placed, rows in ((is_low, slice(0, 32)), (is_high, slice(8, 40))):
+
+                @pl.when(placed)
+                def _(rows=rows):
+                    part = tiles // PARTS
+                    copies = []
+                    for index in range(PARTS):
+                        first = side + index * part
+                        sweep(
+                            (first, first + part), coeffs, force, centre, later, now, put_out,
+                            w3, u3, rows,
+                        )
+                        at = pl.ds(index * part * LANES, part * LANES)
+                        copy = pltpu.make_async_copy(
+                            out.at[:, at], out_ref.at[0, :, at], sems.at[index]
+                        )
+                        copy.start()
+                        copies.append(copy)
+                    for copy in copies:
+                        copy.wait()
+
     tile_copy.wait()
 
 
@@ -1024,22 +1070,18 @@
         cost_estimate=cost(2),
         name="edges",
     )(place, *loaded)
-    to_right, to_left, across = pl.pallas_call(
+    from_across = held(lax.ppermute(across, "ba", swap))
+    to_right, to_left = pl.pallas_call(
         pack_kernel,
-        out_shape=[
-            in_vmem((rows, 7 * wide + LANES)),
-            in_vmem((rows, 7 * wide + LANES)),
-            in_vmem(across.shape),
-        ],
-        in_specs=[VM] * 4,
-        out_specs=[VM] * 3,
+        out_shape=[in_vmem((rows, 7 * wide + LANES))] * 2,
+        in_specs=[VM] * 3,
+        out_specs=[VM] * 2,
         compiler_params=LEAN,
         cost_estimate=cost(1),
         name="pack",
-    )(to_right, to_left, across, corners)
+    )(to_right, to_left, corners)
     from_left = held(lax.ppermute(to_right, "aa", up))
     from_right = held(lax.ppermute(to_left, "aa", down))
-    from_across = held(lax.ppermute(across, "ba", swap))
 
     field = (ext + 2, rows + 8, LANES)
     turned_own, turned_other, rim, fluid, *cells = pl.pallas_call(
@@ -1053,23 +1095,23 @@
         in_specs=[SM] * 3 + [VM] * 6,
         out_specs=[VM] * 12,
         compiler_params=params(2),
-        cost_estimate=cost(1),
+        cost_estimate=cost(2.5),
         name="turn",
     )(
-        place, perm_table, cond_table, *loaded, across,
+        place, perm_table, cond_table, *loaded, to_left,
     )
     other = held(lax.ppermute(turned_other, ("code", "ba"), opposite))
     own = held(lax.ppermute(turned_own, "code", swap))
     coeffs, force, diag, fluid, *cells = pl.pallas_call(
         inner_kernel,
         out_shape=[in_vmem((6,) + field)] + [in_vmem(field)] * 11,
-        in_specs=[SM] * 3 + [VM] * 10,
+        in_specs=[SM] * 3 + [VM] * 15,
         out_specs=[VM] * 12,
-        input_output_aliases={4 + index: 3 + index for index in range(9)},
+        input_output_aliases={9 + index: 3 + index for index in range(9)},
         compiler_params=params(2),
         cost_estimate=cost(10),
         name="inner",
-    )(place, perm_table, cond_table, from_across, fluid, *cells)
+    )(place, perm_table, cond_table, from_across, *loaded, fluid, *cells)
     rim = pl.pallas_call(
         plane_kernel,
         out_shape=in_vmem(rim.shape),
@@ -1082,14 +1124,14 @@
     )(place, from_right, rim, from_left, force)
     rim = held(lax.ppermute(rim, "code", swap))
 
-    v1, v2, coeffs, force, diag, fluid, *cells = pl.pallas_call(
+    v1, v2, boundary, coeffs, force, diag, fluid, *cells = pl.pallas_call(
         main_kernel,
-        out_shape=[in_vmem(field), in_vmem(field)]
+        out_shape=[in_vmem(field), in_vmem(field), in_vmem((2, (ext + 16) * LANES))]
         + [in_vmem((6,) + field)]
         + [in_vmem(field)] * 11,
         in_specs=[SM] * 3 + [VM] * 14,
-        out_specs=[VM] * 14,
-        input_output_aliases={5 + index: 2 + index for index in range(12)},
+        out_specs=[VM] * 15,
+        input_output_aliases={5 + index: 3 + index for index in range(12)},
         compiler_params=params(2),
         cost_estimate=cost(10),
         name="main",
@@ -1099,13 +1141,14 @@
     )
     boundary = pl.pallas_call(
         send_kernel,
-        out_shape=in_vmem((2, (ext + 16) * LANES)),
-        in_specs=[SM] + [VM] * 2,
+        out_shape=in_vmem(boundary.shape),
+        in_specs=[VM] * 2,
         out_specs=VM,
+        input_output_aliases={0: 0},
         compiler_params=LEAN,
         cost_estimate=cost(1),
         name="send",
-    )(place, v2, rim)
+    )(boundary, rim)
     boundary = held(lax.ppermute(boundary, "ba", swap))
     received, edge = pl.pallas_call(
         faces_kernel,

time: 40.7 us -> 37.7 us (0.926)
  starting transfers between devices: 13 us -> 10.8 us
  Pallas kernels: 25.6 us -> 24.9 us
    ppermute x1, starting transfers between devices: 2.73 us -> 0.33 us  [paired_body(): own = held(lax.ppermute(turned_own, 'code', swap))]
    ppermute x1, starting transfers between devices: 0.22 us -> 1.17 us  [paired_body(): other = held(lax.ppermute(turned_other, ('code', 'ba'), opposite))]
    ppermute x1, starting transfers between devices: 1.28 us -> 0.52 us  [paired_body(): boundary = held(lax.ppermute(boundary, 'ba', swap))]
    pallas_call x3, Pallas kernels: 4.65 us -> 4.02 us  [the longest x1 3.97 us: paired_body(): pl.pallas_call(main_kernel, out_shape=[in_vmem(field), in_vmem(field), in...]
    ppermute x1, waiting for transfers between devices: 0.45 us -> 0.01 us  [paired_body(): corners = held(lax.ppermute(corners, 'ba', swap))]
  transfers between devices with their start and end apart: 8 -> 8, of which waited for: 2 -> 1; matrix products, arithmetic and copies ran while one was open for 0% -> 0% of each run, Pallas kernels for 47% -> 51%
where the time goes in v4:
time: 37.7 us; the launch traced here: 37.5 us
  Pallas kernels  24.9 us (66%)
  starting transfers between devices  10.8 us (29%)
  between operations  0.95 us (3%)
  waiting for transfers between devices  0.54 us (1%)
    pallas_call x1, Pallas kernels, paired_body(): pl.pallas_call(inner_kernel, out_shape=[in_vmem((6,) + field)] + [in_vmem...  7.17 us
    pallas_call x1, Pallas kernels, paired_body(): pl.pallas_call(faces_kernel, out_shape=[jax.ShapeDtypeStruct(coupled.shap...  4.23 us
    pallas_call x1, Pallas kernels, paired_body(): pl.pallas_call(main_kernel, out_shape=[in_vmem(field), in_vmem(field), in...  3.97 us
    pallas_call x1, Pallas kernels, paired_body(): pl.pallas_call(finish_kernel, out_shape=[jax.ShapeDtypeStruct(states.shap...  3.9 us
    ppermute x1, starting transfers between devices, paired_body(): from_left = held(lax.ppermute(to_right, 'aa', up))  3.15 us
    ppermute x1, starting transfers between devices, paired_body(): from_right = held(lax.ppermute(to_left, 'aa', down))  3.03 us
    pallas_call x1, Pallas kernels, paired_body(): pl.pallas_call(turn_kernel, out_shape=[in_vmem((32, 2 * groups * LANES)),...  2.41 us
    pallas_call x1, Pallas kernels, paired_body(): pl.pallas_call(corner_kernel, out_shape=in_vmem((2, 10 * wide)), in_specs...  1.73 us
  transfers between devices with their start and end apart: 8, of which 1 were waited for; matrix products, arithmetic and copies ran while one was open for 0% of the time, Pallas kernels for 51%

profile of v4, /device:TPU:9, one launch (start us, length us, event | category | flops | bytes accessed | tf_op | source)
XLA Modules:
  0.0 37.5 jit_solution(8501580952597738882)
XLA Ops:
  0.6 0.1 pad_add_fusion.where_ref
  0.7 0.0 copy-start
  0.7 0.0 copy-start.1
  0.7 0.0 copy-start.2
  0.7 0.0 copy-start.3
  0.7 0.0 copy-start.4
  0.7 1.7 %corner.1 = f32[2,2560]{1,0:T(2,128)S(1)} custom-call(s32[2]{0:T(128)S(1)} %pad_add_fusion.where_ref, f32[1,32,8192]{2,1,0:T(8,128)} %st.7, f32[1,3,32,8192]{3,2,1,0:T(8,128)} %cp.7, s32[1,32,8192]{2,1,0:T(8,128)} %fa.7, s32[1,32,8192]{2,1,0:T(8,128)} %ij.7, s32[1,32,8192]{2,1,0:T(8,128)} %pr.7), custom_call_target="tpu_custom_call" | custom-call | flops 1150000000 | bytes 3600000 | tf_op jit(solution)/shard_map/corner/pallas_call | solution.py:1044
  2.5 1.3 %collective-permute-start = (f32[2,2560]{1,0:T(2,128)S(1)}, f32[2,2560]{1,0:T(2,128)S(1)}, u32[]{:S(2)}, u32[]{:S(2)}) collective-permute-start(f32[2,2560]{1,0:T(2,128)S(1)} %corner.1), channel_id=1, source_target_pairs={{0,1},{1,0},{2,3},{3,2},{4,5},{5,4},{6,7},{7,6},{8,9},{9,8},{10,11... | collective-permute-start | bytes 61448 | tf_op jit(solution)/shard_map/ppermute | solution.py:1059
  3.8 0.0 copy-done
  3.8 0.0 copy-done.1
  3.8 0.0 copy-done.2
  3.8 0.0 copy-done.3
  3.8 0.1 copy-done.4
  3.9 0.8 %edges.1 = (f32[32,1792]{1,0:T(8,128)S(1)}, f32[32,1792]{1,0:T(8,128)S(1)}, f32[2,40960]{1,0:T(2,128)S(1)}) custom-call(s32[2]{0:T(128)S(1)} %pad_add_fusion.where_ref, f32[1,32,8192]{2,1,0:T(8,128)S(1)} %copy-done.1, f32[1,3,32,8192]{3,2,1,0:T(8,128)S(1)} %copy-done, s32[1,32,8192]{2,1,0:T(8,128)S(1)} %copy-done.2, s32[1,32,8192]{2,1,0:T(8,128)S(1)} %copy-done.3, ...), custom_call_target="tpu_custom_call" | custom-call | flops 2300000000 | bytes 7200000 | tf_op jit(solution)/shard_map/edges/pallas_call | solution.py:1060
  4.7 1.3 %collective-permute-start.3 = (f32[2,40960]{1,0:T(2,128)S(1)}, f32[2,40960]{1,0:T(2,128)S(1)}, u32[]{:S(2)}, u32[]{:S(2)}) collective-permute-start(f32[2,40960]{1,0:T(2,128)S(1)} %get-tuple-element.47), channel_id=1, source_target_pairs={{0,1},{1,0},{2,3},{3,2},{4,5},{5,4},{6,7},{7,6},{8,9},{9,8},{10,11... | collective-permute-start | bytes 983048 | tf_op jit(solution)/shard_map/ppermute | solution.py:1073
  6.0 0.0 collective-permute-done.corners
  6.0 0.0 copy-start.5
  6.0 0.0 copy-start.6
  6.1 3.1 %collective-permute-start.1 = (f32[32,1920]{1,0:T(8,128)S(1)}, f32[32,1920]{1,0:T(8,128)S(1)}, u32[]{:S(2)}, u32[]{:S(2)}) collective-permute-start(f32[32,1920]{1,0:T(8,128)S(1)} %get-tuple-element.45), channel_id=1, source_target_pairs={{0,2},{2,4},{4,6},{6,8},{8,10},{10,12},{12,14},{1,3},{3,5},{5,7},{... | collective-permute-start | bytes 737288 | tf_op jit(solution)/shard_map/ppermute | solution.py:1083
  9.2 3.0 %collective-permute-start.2 = (f32[32,1920]{1,0:T(8,128)S(1)}, f32[32,1920]{1,0:T(8,128)S(1)}, u32[]{:S(2)}, u32[]{:S(2)}) collective-permute-start(f32[32,1920]{1,0:T(8,128)S(1)} %get-tuple-element.46.corners), channel_id=1, source_target_pairs={{2,0},{4,2},{6,4},{8,6},{10,8},{12,10},{14,12},{3,1},{5,3},{7,5},{... | collective-permute-start | bytes 737288 | tf_op jit(solution)/shard_map/ppermute | solution.py:1084
  12.3 0.0 copy-done.5
  12.3 0.0 copy-done.6
  12.3 2.4 %turn.1 = (f32[32,4096]{1,0:T(8,128)S(1)}, f32[32,4224]{1,0:T(8,128)S(1)}, f32[32,256]{1,0:T(8,128)S(1)}, f32[70,40,128]{2,1,0:T(8,128)S(1)}, f32[70,40,128]{2,1...) custom-call(s32[2]{0:T(128)S(1)} %pad_add_fusion.where_ref, ...), custom_call_target="tpu_custom_call" | custom-call | flops 2875000064 | bytes 9000000 | tf_op jit(solution)/shard_map/turn/pallas_call | solution.py:1087
  14.7 0.3 collective-permute-start.4
  15.0 1.2 %collective-permute-start.5 = (f32[32,4224]{1,0:T(8,128)S(1)}, f32[32,4224]{1,0:T(8,128)S(1)}, u32[]{:S(2)}, u32[]{:S(2)}) collective-permute-start(f32[32,4224]{1,0:T(8,128)S(1)} %get-tuple-element.72), channel_id=1, source_target_pairs={{0,17},{1,16},{16,1},{17,0},{2,19},{3,18},{18,3},{19,2},{4,21},{5,... | collective-permute-start | bytes 1622024 | tf_op jit(solution)/shard_map/ppermute | solution.py:1103
  16.2 0.0 collective-permute-done.3.across
  16.2 7.2 %inner.1 = (f32[6,70,40,128]{3,2,1,0:T(8,128)S(1)}, f32[70,40,128]{2,1,0:T(8,128)S(1)}, f32[70,40,128]{2,1,0:T(8,128)S(1)}, f32[70,40,128]{2,1,0:T(8,128)S(1)}, ...) custom-call(s32[2]{0:T(128)S(1)} %pad_add_fusion.where_ref, ...), custom_call_target="tpu_custom_call", output_to_operand_aliasing={{3}: (9, {}), {4}: (10, {}), {5}: (11, {}), {6}: (12, {}), ... | custom-call | flops 11500000256 | bytes 36000000 | tf_op jit(solution)/shard_map/inner/pallas_call | solution.py:1105
  23.4 0.0 collective-permute-done.1.from_left.rest_0_
  23.4 0.0 collective-permute-done.2.from_right
  23.4 0.6 %plane.1 = f32[32,256]{1,0:T(8,128)S(1)} custom-call(s32[2]{0:T(128)S(1)} %pad_add_fusion.where_ref, f32[32,1920]{1,0:T(8,128)S(1)} %collective-permute-done.2.from_right, f32[32,256]{1,0:T(8,128)S(1)} %get-tuple-element.73.own_in, f32[32,1920]{1,0:T(8,128)S(1)} %collective-permute-done.1.from_left.rest_0_, ...), custom_call_target="tpu_custom_call", output_to_operand_aliasing={{}: (2, {})} | custom-call | flops 1150000000 | bytes 3600000 | tf_op jit(solution)/shard_map/plane/pallas_call | solution.py:1115
  24.0 0.1 collective-permute-start.6
  24.1 4.0 %main.1 = (f32[70,40,128]{2,1,0:T(8,128)S(1)}, f32[70,40,128]{2,1,0:T(8,128)S(1)}, f32[2,10752]{1,0:T(2,128)S(1)}, f32[6,70,40,128]{3,2,1,0:T(8,128)S(1)}, f32[7...) custom-call(s32[2]{0:T(128)S(1)} %pad_add_fusion.where_ref, ...), custom_call_target="tpu_custom_call", output_to_operand_aliasing={{3}: (5, {}), {4}: (6, {}), {5}: (7, {}), {6}: (8, {}), {7}... | custom-call | flops 11500000256 | bytes 36000000 | tf_op jit(solution)/shard_map/main/pallas_call | solution.py:1127
  28.1 0.0 collective-permute-done.6.own_rim.rim
  28.1 0.5 %collective-permute-start.7 = (f32[2,10752]{1,0:T(2,128)S(1)}, f32[2,10752]{1,0:T(2,128)S(1)}, u32[]{:S(2)}, u32[]{:S(2)}) collective-permute-start(f32[2,10752]{1,0:T(2,128)S(1)} %send.1), channel_id=1, source_target_pairs={{0,1},{1,0},{2,3},{3,2},{4,5},{5,4},{6,7},{7,6},{8,9},{9,8},{10,11... | collective-permute-start | bytes 258056 | tf_op jit(solution)/shard_map/ppermute | solution.py:1152
  28.6 0.0 collective-permute-done.4.own
  28.6 0.5 %collective-permute-done.5.other = f32[32,4224]{1,0:T(8,128)S(1)} collective-permute-done((f32[32,4224]{1,0:T(8,128)S(1)}, f32[32,4224]{1,0:T(8,128)S(1)}, u32[]{:S(2)}, u32[]{:S(2)}) %collective-permute-start.5) | collective-permute-done | bytes 540704 | tf_op jit(solution)/shard_map/ppermute | solution.py:1103
  29.1 4.2 %faces.1 = (f32[1,3,32,8192]{3,2,1,0:T(8,128)}, f32[2,32,128]{2,1,0:T(8,128)S(1)}) custom-call(s32[2]{0:T(128)S(1)} %pad_add_fusion.where_ref, f32[32,4096]{1,0:T(8,128)S(1)} %collective-permute-done.4.own, f32[32,4224]{1,0:T(8,128)S(1)} %collective-permute-done.5.other, f32[32,256]{1,0:T(8,128)S(1)} %collective-permute-done.6.own_rim.rim, ...), custom_call_target="tpu_custom_call" | custom-call | flops 6899999744 | bytes 21600000 | tf_op jit(solution)/shard_map/faces/pallas_call | solution.py:1153
  33.4 0.0 collective-permute-done.7.boundary
  33.4 3.9 %finish.1 = (f32[1,32,8192]{2,1,0:T(8,128)}, f32[70,40,128]{2,1,0:T(8,128)S(1)}, f32[1,3,32,8192]{3,2,1,0:T(8,128)}) custom-call(s32[2]{0:T(128)S(1)} %pad_add_fusion.where_ref, f32[70,40,128]{2,1,0:T(8,128)S(1)} %get-tuple-element.69.v1, f32[70,40,128]{2,1,0:T(8,128)S(1)} %get-tuple-element.70.v2_in, ...), custom_call_target="tpu_custom_call", output_to_operand_aliasing={{1}: (2, {}), {2}: (3, {})} | custom-call | flops 6899999744 | bytes 21600000 | tf_op jit(solution)/shard_map/finish/pallas_call | solution.py:1169
  (2 shorter events, 0.1 us)
Async XLA Ops:
  0.7 3.0 %copy-start = (f32[1,3,32,8192]{3,2,1,0:T(8,128)S(1)}, f32[1,3,32,8192]{3,2,1,0:T(8,128)}, u32[]{:S(2)}) copy-start(f32[1,3,32,8192]{3,2,1,0:T(8,128)} %cp.7) | copy-start | bytes 9437188
  0.7 3.0 %copy-start.1 = (f32[1,32,8192]{2,1,0:T(8,128)S(1)}, f32[1,32,8192]{2,1,0:T(8,128)}, u32[]{:S(2)}) copy-start(f32[1,32,8192]{2,1,0:T(8,128)} %st.7) | copy-start | bytes 3145732
  0.7 3.0 %copy-start.2 = (s32[1,32,8192]{2,1,0:T(8,128)S(1)}, s32[1,32,8192]{2,1,0:T(8,128)}, u32[]{:S(2)}) copy-start(s32[1,32,8192]{2,1,0:T(8,128)} %fa.7) | copy-start | bytes 3145732
  0.7 3.0 %copy-start.3 = (s32[1,32,8192]{2,1,0:T(8,128)S(1)}, s32[1,32,8192]{2,1,0:T(8,128)}, u32[]{:S(2)}) copy-start(s32[1,32,8192]{2,1,0:T(8,128)} %ij.7) | copy-start | bytes 3145732
  0.7 3.2 %copy-start.4 = (s32[1,32,8192]{2,1,0:T(8,128)S(1)}, s32[1,32,8192]{2,1,0:T(8,128)}, u32[]{:S(2)}) copy-start(s32[1,32,8192]{2,1,0:T(8,128)} %pr.7) | copy-start | bytes 3145732
  2.5 3.5 %collective-permute-start = (f32[2,2560]{1,0:T(2,128)S(1)}, f32[2,2560]{1,0:T(2,128)S(1)}, u32[]{:S(2)}, u32[]{:S(2)}) collective-permute-start(f32[2,2560]{1,0:T(2,128)S(1)} %corner.1), channel_id=1, source_target_pairs={{0,1},{1,0},{2,3},{3,2},{4,5},{5,4},{6,7},{7,6},{8,9},{9,8},{10,11... | collective-permute-start | bytes 61448 | tf_op jit(solution)/shard_map/ppermute | solution.py:1059
  4.7 11.5 %collective-permute-start.3 = (f32[2,40960]{1,0:T(2,128)S(1)}, f32[2,40960]{1,0:T(2,128)S(1)}, u32[]{:S(2)}, u32[]{:S(2)}) collective-permute-start(f32[2,40960]{1,0:T(2,128)S(1)} %get-tuple-element.47), channel_id=1, source_target_pairs={{0,1},{1,0},{2,3},{3,2},{4,5},{5,4},{6,7},{7,6},{8,9},{9,8},{10,11... | collective-permute-start | bytes 983048 | tf_op jit(solution)/shard_map/ppermute | solution.py:1073
  6.0 6.3 %copy-start.5 = (f32[6]{0:T(128)S(1)}, f32[6]{0:T(128)}, u32[]{:S(2)}) copy-start(f32[6]{0:T(128)} %perm_ref.5) | copy-start | bytes 76
  6.0 6.3 %copy-start.6 = (f32[6]{0:T(128)S(1)}, f32[6]{0:T(128)}, u32[]{:S(2)}) copy-start(f32[6]{0:T(128)} %cond_ref.5) | copy-start | bytes 76
  6.1 17.3 %collective-permute-start.1 = (f32[32,1920]{1,0:T(8,128)S(1)}, f32[32,1920]{1,0:T(8,128)S(1)}, u32[]{:S(2)}, u32[]{:S(2)}) collective-permute-start(f32[32,1920]{1,0:T(8,128)S(1)} %get-tuple-element.45), channel_id=1, source_target_pairs={{0,2},{2,4},{4,6},{6,8},{8,10},{10,12},{12,14},{1,3},{3,5},{5,7},{... | collective-permute-start | bytes 737288 | tf_op jit(solution)/shard_map/ppermute | solution.py:1083
  9.2 14.2 %collective-permute-start.2 = (f32[32,1920]{1,0:T(8,128)S(1)}, f32[32,1920]{1,0:T(8,128)S(1)}, u32[]{:S(2)}, u32[]{:S(2)}) collective-permute-start(f32[32,1920]{1,0:T(8,128)S(1)} %get-tuple-element.46.corners), channel_id=1, source_target_pairs={{2,0},{4,2},{6,4},{8,6},{10,8},{12,10},{14,12},{3,1},{5,3},{7,5},{... | collective-permute-start | bytes 737288 | tf_op jit(solution)/shard_map/ppermute | solution.py:1084
  14.7 13.9 %collective-permute-start.4 = (f32[32,4096]{1,0:T(8,128)S(1)}, f32[32,4096]{1,0:T(8,128)S(1)}, u32[]{:S(2)}, u32[]{:S(2)}) collective-permute-start(f32[32,4096]{1,0:T(8,128)S(1)} %get-tuple-element.71), channel_id=1, source_target_pairs={{0,16},{16,0},{1,17},{17,1},{2,18},{18,2},{3,19},{19,3},{4,20},{20... | collective-permute-start | bytes 1572872 | tf_op jit(solution)/shard_map/ppermute | solution.py:1104
  15.0 14.1 %collective-permute-start.5 = (f32[32,4224]{1,0:T(8,128)S(1)}, f32[32,4224]{1,0:T(8,128)S(1)}, u32[]{:S(2)}, u32[]{:S(2)}) collective-permute-start(f32[32,4224]{1,0:T(8,128)S(1)} %get-tuple-element.72), channel_id=1, source_target_pairs={{0,17},{1,16},{16,1},{17,0},{2,19},{3,18},{18,3},{19,2},{4,21},{5,... | collective-permute-start | bytes 1622024 | tf_op jit(solution)/shard_map/ppermute | solution.py:1103
  24.0 4.1 %collective-permute-start.6 = (f32[32,256]{1,0:T(8,128)S(1)}, f32[32,256]{1,0:T(8,128)S(1)}, u32[]{:S(2)}, u32[]{:S(2)}) collective-permute-start(f32[32,256]{1,0:T(8,128)S(1)} %plane.1), channel_id=1, source_target_pairs={{0,16},{16,0},{1,17},{17,1},{2,18},{18,2},{3,19},{19,3},{4,20},{20... | collective-permute-start | bytes 98312 | tf_op jit(solution)/shard_map/ppermute | solution.py:1125
  28.1 5.3 %collective-permute-start.7 = (f32[2,10752]{1,0:T(2,128)S(1)}, f32[2,10752]{1,0:T(2,128)S(1)}, u32[]{:S(2)}, u32[]{:S(2)}) collective-permute-start(f32[2,10752]{1,0:T(2,128)S(1)} %send.1), channel_id=1, source_target_pairs={{0,1},{1,0},{2,3},{3,2},{4,5},{5,4},{6,7},{7,6},{8,9},{9,8},{10,11... | collective-permute-start | bytes 258056 | tf_op jit(solution)/shard_map/ppermute | solution.py:1152

commit v5 on v4

--- a/solution.py
+++ b/solution.py
@@ -632,6 +632,11 @@
     not_last = lane % W != W - 1
     blank = jnp.zeros(shape, jnp.float32)
 
+    last_tile = v0.shape[0] - 3
+
+    def inside(e):
+        return min(e, last_tile) if isinstance(e, int) else e
+
     def run(step, first, stop, start):
         if stop - first > 8:
             unroll = max(n for n in range(1, 10) if (stop - first) % n == 0)
@@ -669,7 +674,7 @@
         def step(e, carry):
             before, plus, turned, now, after = carry
             close(e - 1, before, plus, turned)
-            later = turns(e + 2)
+            later = turns(inside(e + 2))
             fresh = along(e, now, after)
             return turned[0], fresh, (half_turn(fresh[0]), prev_lane(fresh[1])), after, later
 
@@ -715,7 +720,7 @@
         def step(e, carry):
             before, turned, now, after = carry
             close(e - 1, before, turned)
-            later = turns(e + 2)
+            later = turns(inside(e + 2))
             return turned[:2], opened(e, now, after), after, later
 
         def b_steps(first, stop):

time: 37.7 us -> 37.7 us (level)
  no operation moved by 1% of the time
where the time goes in v5:
time: 37.7 us; the launch traced here: 37.5 us
  Pallas kernels  24.9 us (66%)
  starting transfers between devices  10.8 us (29%)
  between operations  0.95 us (3%)
  waiting for transfers between devices  0.54 us (1%)
    pallas_call x1, Pallas kernels, paired_body(): pl.pallas_call(inner_kernel, out_shape=[in_vmem((6,) + field)] + [in_vmem...  7.17 us
    pallas_call x1, Pallas kernels, paired_body(): pl.pallas_call(faces_kernel, out_shape=[jax.ShapeDtypeStruct(coupled.shap...  4.23 us
    pallas_call x1, Pallas kernels, paired_body(): pl.pallas_call(main_kernel, out_shape=[in_vmem(field), in_vmem(field), in...  3.97 us
    pallas_call x1, Pallas kernels, paired_body(): pl.pallas_call(finish_kernel, out_shape=[jax.ShapeDtypeStruct(states.shap...  3.9 us
    ppermute x1, starting transfers between devices, paired_body(): from_left = held(lax.ppermute(to_right, 'aa', up))  3.15 us
    ppermute x1, starting transfers between devices, paired_body(): from_right = held(lax.ppermute(to_left, 'aa', down))  3.03 us
    pallas_call x1, Pallas kernels, paired_body(): pl.pallas_call(turn_kernel, out_shape=[in_vmem((32, 2 * groups * LANES)),...  2.41 us
    pallas_call x1, Pallas kernels, paired_body(): pl.pallas_call(corner_kernel, out_shape=in_vmem((2, 10 * wide)), in_specs...  1.73 us
  transfers between devices with their start and end apart: 8, of which 1 were waited for; matrix products, arithmetic and copies ran while one was open for 0% of the time, Pallas kernels for 51%

profile of v5, /device:TPU:9, one launch (start us, length us, event | category | flops | bytes accessed | tf_op | source)
XLA Modules:
  0.0 37.5 jit_solution(801905510626000533)
XLA Ops:
  0.6 0.1 pad_add_fusion.where_ref
  0.7 0.0 copy-start
  0.7 0.0 copy-start.1
  0.7 0.0 copy-start.2
  0.7 0.0 copy-start.3
  0.7 0.0 copy-start.4
  0.7 1.7 %corner.1 = f32[2,2560]{1,0:T(2,128)S(1)} custom-call(s32[2]{0:T(128)S(1)} %pad_add_fusion.where_ref, f32[1,32,8192]{2,1,0:T(8,128)} %st.7, f32[1,3,32,8192]{3,2,1,0:T(8,128)} %cp.7, s32[1,32,8192]{2,1,0:T(8,128)} %fa.7, s32[1,32,8192]{2,1,0:T(8,128)} %ij.7, s32[1,32,8192]{2,1,0:T(8,128)} %pr.7), custom_call_target="tpu_custom_call" | custom-call | flops 1150000000 | bytes 3600000 | tf_op jit(solution)/shard_map/corner/pallas_call | solution.py:1049
  2.5 1.3 %collective-permute-start = (f32[2,2560]{1,0:T(2,128)S(1)}, f32[2,2560]{1,0:T(2,128)S(1)}, u32[]{:S(2)}, u32[]{:S(2)}) collective-permute-start(f32[2,2560]{1,0:T(2,128)S(1)} %corner.1), channel_id=1, source_target_pairs={{0,1},{1,0},{2,3},{3,2},{4,5},{5,4},{6,7},{7,6},{8,9},{9,8},{10,11... | collective-permute-start | bytes 61448 | tf_op jit(solution)/shard_map/ppermute | solution.py:1064
  3.8 0.0 copy-done
  3.8 0.0 copy-done.1
  3.8 0.0 copy-done.2
  3.8 0.0 copy-done.3
  3.8 0.1 copy-done.4
  3.9 0.8 %edges.1 = (f32[32,1792]{1,0:T(8,128)S(1)}, f32[32,1792]{1,0:T(8,128)S(1)}, f32[2,40960]{1,0:T(2,128)S(1)}) custom-call(s32[2]{0:T(128)S(1)} %pad_add_fusion.where_ref, f32[1,32,8192]{2,1,0:T(8,128)S(1)} %copy-done.1, f32[1,3,32,8192]{3,2,1,0:T(8,128)S(1)} %copy-done, s32[1,32,8192]{2,1,0:T(8,128)S(1)} %copy-done.2, s32[1,32,8192]{2,1,0:T(8,128)S(1)} %copy-done.3, ...), custom_call_target="tpu_custom_call" | custom-call | flops 2300000000 | bytes 7200000 | tf_op jit(solution)/shard_map/edges/pallas_call | solution.py:1065
  4.7 1.3 %collective-permute-start.3 = (f32[2,40960]{1,0:T(2,128)S(1)}, f32[2,40960]{1,0:T(2,128)S(1)}, u32[]{:S(2)}, u32[]{:S(2)}) collective-permute-start(f32[2,40960]{1,0:T(2,128)S(1)} %get-tuple-element.47), channel_id=1, source_target_pairs={{0,1},{1,0},{2,3},{3,2},{4,5},{5,4},{6,7},{7,6},{8,9},{9,8},{10,11... | collective-permute-start | bytes 983048 | tf_op jit(solution)/shard_map/ppermute | solution.py:1078
  6.0 0.0 collective-permute-done.corners
  6.0 0.0 copy-start.5
  6.0 0.0 copy-start.6
  6.1 3.1 %collective-permute-start.1 = (f32[32,1920]{1,0:T(8,128)S(1)}, f32[32,1920]{1,0:T(8,128)S(1)}, u32[]{:S(2)}, u32[]{:S(2)}) collective-permute-start(f32[32,1920]{1,0:T(8,128)S(1)} %get-tuple-element.45), channel_id=1, source_target_pairs={{0,2},{2,4},{4,6},{6,8},{8,10},{10,12},{12,14},{1,3},{3,5},{5,7},{... | collective-permute-start | bytes 737288 | tf_op jit(solution)/shard_map/ppermute | solution.py:1088
  9.2 3.0 %collective-permute-start.2 = (f32[32,1920]{1,0:T(8,128)S(1)}, f32[32,1920]{1,0:T(8,128)S(1)}, u32[]{:S(2)}, u32[]{:S(2)}) collective-permute-start(f32[32,1920]{1,0:T(8,128)S(1)} %get-tuple-element.46.corners), channel_id=1, source_target_pairs={{2,0},{4,2},{6,4},{8,6},{10,8},{12,10},{14,12},{3,1},{5,3},{7,5},{... | collective-permute-start | bytes 737288 | tf_op jit(solution)/shard_map/ppermute | solution.py:1089
  12.3 0.0 copy-done.5
  12.3 0.0 copy-done.6
  12.3 2.4 %turn.1 = (f32[32,4096]{1,0:T(8,128)S(1)}, f32[32,4224]{1,0:T(8,128)S(1)}, f32[32,256]{1,0:T(8,128)S(1)}, f32[70,40,128]{2,1,0:T(8,128)S(1)}, f32[70,40,128]{2,1...) custom-call(s32[2]{0:T(128)S(1)} %pad_add_fusion.where_ref, ...), custom_call_target="tpu_custom_call" | custom-call | flops 2875000064 | bytes 9000000 | tf_op jit(solution)/shard_map/turn/pallas_call | solution.py:1092
  14.7 0.3 collective-permute-start.4
  15.0 1.2 %collective-permute-start.5 = (f32[32,4224]{1,0:T(8,128)S(1)}, f32[32,4224]{1,0:T(8,128)S(1)}, u32[]{:S(2)}, u32[]{:S(2)}) collective-permute-start(f32[32,4224]{1,0:T(8,128)S(1)} %get-tuple-element.72), channel_id=1, source_target_pairs={{0,17},{1,16},{16,1},{17,0},{2,19},{3,18},{18,3},{19,2},{4,21},{5,... | collective-permute-start | bytes 1622024 | tf_op jit(solution)/shard_map/ppermute | solution.py:1108
  16.2 0.0 collective-permute-done.3.across
  16.2 7.2 %inner.1 = (f32[6,70,40,128]{3,2,1,0:T(8,128)S(1)}, f32[70,40,128]{2,1,0:T(8,128)S(1)}, f32[70,40,128]{2,1,0:T(8,128)S(1)}, f32[70,40,128]{2,1,0:T(8,128)S(1)}, ...) custom-call(s32[2]{0:T(128)S(1)} %pad_add_fusion.where_ref, ...), custom_call_target="tpu_custom_call", output_to_operand_aliasing={{3}: (9, {}), {4}: (10, {}), {5}: (11, {}), {6}: (12, {}), ... | custom-call | flops 11500000256 | bytes 36000000 | tf_op jit(solution)/shard_map/inner/pallas_call | solution.py:1110
  23.4 0.0 collective-permute-done.1.from_left.rest_0_
  23.4 0.0 collective-permute-done.2.from_right
  23.4 0.6 %plane.1 = f32[32,256]{1,0:T(8,128)S(1)} custom-call(s32[2]{0:T(128)S(1)} %pad_add_fusion.where_ref, f32[32,1920]{1,0:T(8,128)S(1)} %collective-permute-done.2.from_right, f32[32,256]{1,0:T(8,128)S(1)} %get-tuple-element.73.own_in, f32[32,1920]{1,0:T(8,128)S(1)} %collective-permute-done.1.from_left.rest_0_, ...), custom_call_target="tpu_custom_call", output_to_operand_aliasing={{}: (2, {})} | custom-call | flops 1150000000 | bytes 3600000 | tf_op jit(solution)/shard_map/plane/pallas_call | solution.py:1120
  24.0 0.1 collective-permute-start.6
  24.1 4.0 %main.1 = (f32[70,40,128]{2,1,0:T(8,128)S(1)}, f32[70,40,128]{2,1,0:T(8,128)S(1)}, f32[2,10752]{1,0:T(2,128)S(1)}, f32[6,70,40,128]{3,2,1,0:T(8,128)S(1)}, f32[7...) custom-call(s32[2]{0:T(128)S(1)} %pad_add_fusion.where_ref, ...), custom_call_target="tpu_custom_call", output_to_operand_aliasing={{3}: (5, {}), {4}: (6, {}), {5}: (7, {}), {6}: (8, {}), {7}... | custom-call | flops 11500000256 | bytes 36000000 | tf_op jit(solution)/shard_map/main/pallas_call | solution.py:1132
  28.1 0.0 collective-permute-done.6.own_rim.rim
  28.1 0.5 %collective-permute-start.7 = (f32[2,10752]{1,0:T(2,128)S(1)}, f32[2,10752]{1,0:T(2,128)S(1)}, u32[]{:S(2)}, u32[]{:S(2)}) collective-permute-start(f32[2,10752]{1,0:T(2,128)S(1)} %send.1), channel_id=1, source_target_pairs={{0,1},{1,0},{2,3},{3,2},{4,5},{5,4},{6,7},{7,6},{8,9},{9,8},{10,11... | collective-permute-start | bytes 258056 | tf_op jit(solution)/shard_map/ppermute | solution.py:1157
  28.6 0.0 collective-permute-done.4.own
  28.6 0.5 %collective-permute-done.5.other = f32[32,4224]{1,0:T(8,128)S(1)} collective-permute-done((f32[32,4224]{1,0:T(8,128)S(1)}, f32[32,4224]{1,0:T(8,128)S(1)}, u32[]{:S(2)}, u32[]{:S(2)}) %collective-permute-start.5) | collective-permute-done | bytes 540704 | tf_op jit(solution)/shard_map/ppermute | solution.py:1108
  29.1 4.2 %faces.1 = (f32[1,3,32,8192]{3,2,1,0:T(8,128)}, f32[2,32,128]{2,1,0:T(8,128)S(1)}) custom-call(s32[2]{0:T(128)S(1)} %pad_add_fusion.where_ref, f32[32,4096]{1,0:T(8,128)S(1)} %collective-permute-done.4.own, f32[32,4224]{1,0:T(8,128)S(1)} %collective-permute-done.5.other, f32[32,256]{1,0:T(8,128)S(1)} %collective-permute-done.6.own_rim.rim, ...), custom_call_target="tpu_custom_call" | custom-call | flops 6899999744 | bytes 21600000 | tf_op jit(solution)/shard_map/faces/pallas_call | solution.py:1158
  33.4 0.0 collective-permute-done.7.boundary
  33.4 3.9 %finish.1 = (f32[1,32,8192]{2,1,0:T(8,128)}, f32[70,40,128]{2,1,0:T(8,128)S(1)}, f32[1,3,32,8192]{3,2,1,0:T(8,128)}) custom-call(s32[2]{0:T(128)S(1)} %pad_add_fusion.where_ref, f32[70,40,128]{2,1,0:T(8,128)S(1)} %get-tuple-element.69.v1, f32[70,40,128]{2,1,0:T(8,128)S(1)} %get-tuple-element.70.v2_in, ...), custom_call_target="tpu_custom_call", output_to_operand_aliasing={{1}: (2, {}), {2}: (3, {})} | custom-call | flops 6899999744 | bytes 21600000 | tf_op jit(solution)/shard_map/finish/pallas_call | solution.py:1174
  (2 shorter events, 0.1 us)
Async XLA Ops:
  0.7 3.0 %copy-start = (f32[1,3,32,8192]{3,2,1,0:T(8,128)S(1)}, f32[1,3,32,8192]{3,2,1,0:T(8,128)}, u32[]{:S(2)}) copy-start(f32[1,3,32,8192]{3,2,1,0:T(8,128)} %cp.7) | copy-start | bytes 9437188
  0.7 3.0 %copy-start.1 = (f32[1,32,8192]{2,1,0:T(8,128)S(1)}, f32[1,32,8192]{2,1,0:T(8,128)}, u32[]{:S(2)}) copy-start(f32[1,32,8192]{2,1,0:T(8,128)} %st.7) | copy-start | bytes 3145732
  0.7 3.0 %copy-start.2 = (s32[1,32,8192]{2,1,0:T(8,128)S(1)}, s32[1,32,8192]{2,1,0:T(8,128)}, u32[]{:S(2)}) copy-start(s32[1,32,8192]{2,1,0:T(8,128)} %fa.7) | copy-start | bytes 3145732
  0.7 3.0 %copy-start.3 = (s32[1,32,8192]{2,1,0:T(8,128)S(1)}, s32[1,32,8192]{2,1,0:T(8,128)}, u32[]{:S(2)}) copy-start(s32[1,32,8192]{2,1,0:T(8,128)} %ij.7) | copy-start | bytes 3145732
  0.7 3.2 %copy-start.4 = (s32[1,32,8192]{2,1,0:T(8,128)S(1)}, s32[1,32,8192]{2,1,0:T(8,128)}, u32[]{:S(2)}) copy-start(s32[1,32,8192]{2,1,0:T(8,128)} %pr.7) | copy-start | bytes 3145732
  2.5 3.5 %collective-permute-start = (f32[2,2560]{1,0:T(2,128)S(1)}, f32[2,2560]{1,0:T(2,128)S(1)}, u32[]{:S(2)}, u32[]{:S(2)}) collective-permute-start(f32[2,2560]{1,0:T(2,128)S(1)} %corner.1), channel_id=1, source_target_pairs={{0,1},{1,0},{2,3},{3,2},{4,5},{5,4},{6,7},{7,6},{8,9},{9,8},{10,11... | collective-permute-start | bytes 61448 | tf_op jit(solution)/shard_map/ppermute | solution.py:1064
  4.7 11.5 %collective-permute-start.3 = (f32[2,40960]{1,0:T(2,128)S(1)}, f32[2,40960]{1,0:T(2,128)S(1)}, u32[]{:S(2)}, u32[]{:S(2)}) collective-permute-start(f32[2,40960]{1,0:T(2,128)S(1)} %get-tuple-element.47), channel_id=1, source_target_pairs={{0,1},{1,0},{2,3},{3,2},{4,5},{5,4},{6,7},{7,6},{8,9},{9,8},{10,11... | collective-permute-start | bytes 983048 | tf_op jit(solution)/shard_map/ppermute | solution.py:1078
  6.0 6.3 %copy-start.5 = (f32[6]{0:T(128)S(1)}, f32[6]{0:T(128)}, u32[]{:S(2)}) copy-start(f32[6]{0:T(128)} %perm_ref.5) | copy-start | bytes 76
  6.0 6.3 %copy-start.6 = (f32[6]{0:T(128)S(1)}, f32[6]{0:T(128)}, u32[]{:S(2)}) copy-start(f32[6]{0:T(128)} %cond_ref.5) | copy-start | bytes 76
  6.1 17.3 %collective-permute-start.1 = (f32[32,1920]{1,0:T(8,128)S(1)}, f32[32,1920]{1,0:T(8,128)S(1)}, u32[]{:S(2)}, u32[]{:S(2)}) collective-permute-start(f32[32,1920]{1,0:T(8,128)S(1)} %get-tuple-element.45), channel_id=1, source_target_pairs={{0,2},{2,4},{4,6},{6,8},{8,10},{10,12},{12,14},{1,3},{3,5},{5,7},{... | collective-permute-start | bytes 737288 | tf_op jit(solution)/shard_map/ppermute | solution.py:1088
  9.2 14.2 %collective-permute-start.2 = (f32[32,1920]{1,0:T(8,128)S(1)}, f32[32,1920]{1,0:T(8,128)S(1)}, u32[]{:S(2)}, u32[]{:S(2)}) collective-permute-start(f32[32,1920]{1,0:T(8,128)S(1)} %get-tuple-element.46.corners), channel_id=1, source_target_pairs={{2,0},{4,2},{6,4},{8,6},{10,8},{12,10},{14,12},{3,1},{5,3},{7,5},{... | collective-permute-start | bytes 737288 | tf_op jit(solution)/shard_map/ppermute | solution.py:1089
  14.7 13.9 %collective-permute-start.4 = (f32[32,4096]{1,0:T(8,128)S(1)}, f32[32,4096]{1,0:T(8,128)S(1)}, u32[]{:S(2)}, u32[]{:S(2)}) collective-permute-start(f32[32,4096]{1,0:T(8,128)S(1)} %get-tuple-element.71), channel_id=1, source_target_pairs={{0,16},{16,0},{1,17},{17,1},{2,18},{18,2},{3,19},{19,3},{4,20},{20... | collective-permute-start | bytes 1572872 | tf_op jit(solution)/shard_map/ppermute | solution.py:1109
  15.0 14.1 %collective-permute-start.5 = (f32[32,4224]{1,0:T(8,128)S(1)}, f32[32,4224]{1,0:T(8,128)S(1)}, u32[]{:S(2)}, u32[]{:S(2)}) collective-permute-start(f32[32,4224]{1,0:T(8,128)S(1)} %get-tuple-element.72), channel_id=1, source_target_pairs={{0,17},{1,16},{16,1},{17,0},{2,19},{3,18},{18,3},{19,2},{4,21},{5,... | collective-permute-start | bytes 1622024 | tf_op jit(solution)/shard_map/ppermute | solution.py:1108
  24.0 4.1 %collective-permute-start.6 = (f32[32,256]{1,0:T(8,128)S(1)}, f32[32,256]{1,0:T(8,128)S(1)}, u32[]{:S(2)}, u32[]{:S(2)}) collective-permute-start(f32[32,256]{1,0:T(8,128)S(1)} %plane.1), channel_id=1, source_target_pairs={{0,16},{16,0},{1,17},{17,1},{2,18},{18,2},{3,19},{19,3},{4,20},{20... | collective-permute-start | bytes 98312 | tf_op jit(solution)/shard_map/ppermute | solution.py:1130
  28.1 5.3 %collective-permute-start.7 = (f32[2,10752]{1,0:T(2,128)S(1)}, f32[2,10752]{1,0:T(2,128)S(1)}, u32[]{:S(2)}, u32[]{:S(2)}) collective-permute-start(f32[2,10752]{1,0:T(2,128)S(1)} %send.1), channel_id=1, source_target_pairs={{0,1},{1,0},{2,3},{3,2},{4,5},{5,4},{6,7},{7,6},{8,9},{9,8},{10,11... | collective-permute-start | bytes 258056 | tf_op jit(solution)/shard_map/ppermute | solution.py:1157

commit v6 on v5

--- a/solution.py
+++ b/solution.py
@@ -779,7 +779,7 @@
         put_level(fluid, cells, t + side, rows)
         return carry
 
-    lax.fori_loop(0, tiles, fill, 0, unroll=8)
+    lax.fori_loop(0, tiles, fill, 0, unroll=16)
     made = (coeffs, force, diag, fluid)
     face_terms(cells, made, is_press, [(side, ext - side)])
 
@@ -843,16 +843,26 @@
 
 
 def finish_kernel(
-    where_ref, v1, v2_in, received_in, coeffs, force, src, diag, boundary, edge, rim,
+    where_ref, v1, v2_in, fresh, coeffs, force, src, diag, boundary, edge, rim,
     out_ref, now, received, later, out, tile, sems,
 ):
-    del v2_in, received_in
+    del v2_in
     is_press = where_ref[0] == 0
     is_low = where_ref[1] == 0
     ext = now.shape[0] - 2
     side = XH // 2
     tiles = ext - XH
     rows = rim_rows(is_low)
+    most = pl.ds(0, (tiles - 1) * LANES)
+    face_copies = [
+        pltpu.make_async_copy(fresh.at[0], received.at[0, 0], sems.at[PARTS + 1]),
+        pltpu.make_async_copy(
+            fresh.at[1, :, most], received.at[0, 1, :, most], sems.at[PARTS + 2]
+        ),
+        pltpu.make_async_copy(fresh.at[2], received.at[0, 2], sems.at[PARTS + 3]),
+    ]
+    for copy in face_copies:
+        copy.start()
     clear((later,), (0, ext + 1))
     lane = lane_index((32, LANES))
     mine = rim[:, LANES:]
@@ -914,6 +924,8 @@
                     for copy in copies:
                         copy.wait()
 
+    for copy in face_copies:
+        copy.wait()
     tile_copy.wait()
 
 
@@ -932,7 +944,7 @@
 
 
 def faces_kernel(
-    where_ref, own, other, own_rim, rock, out_ref, edge, field, rim, out, sems
+    where_ref, own, other, own_rim, rock, out, edge, field, rim
 ):
     is_press = where_ref[0] == 0
     is_low = where_ref[1] == 0
@@ -965,7 +977,7 @@
             field[4 * group + q, 32:33, :] = rim[q, pl.ds(group, 1), :]
         return carry
 
-    lax.fori_loop(0, groups, gather, 0, unroll=8)
+    lax.fori_loop(0, groups, gather, 0, unroll=16)
     low_lanes = lane < HALF
     not_last = lane % W != W - 1
 
@@ -1000,31 +1012,19 @@
 
     own_rows = pl.ds(pl.multiple_of(jnp.where(is_low, 0, 8), 8), 32)
     last_row = lax.broadcasted_iota(jnp.int32, (32, LANES), 0) == 31
-    part = tiles // PARTS
-    copies = []
     edge[0] = field[tiles - 1, 0:32, :]
     stone = rock[tiles - 1 + side + 1, own_rows, :]
     stone_after = half_turn(rock[tiles + side + 1, own_rows, :])
     edge[1] = face_mean(stone, jnp.where(low_lanes, half_turn(stone), stone_after))
-    for index in range(PARTS):
-        first = index * part
-
-        @pl.when(is_press)
-        def _(first=first):
-            start = half_turn(field[first, 0:32, :])
-            lax.fori_loop(first, first + part, press, start, unroll=16)
-
-        @pl.when(jnp.logical_not(is_press))
-        def _(first=first):
-            start = half_turn(field[first, 0:32, :]), half_turn(rock[first + side + 1, own_rows, :])
-            lax.fori_loop(first, first + part, heat, start, unroll=16)
-
-        at = pl.ds(first * LANES, part * LANES)
-        copy = pltpu.make_async_copy(out.at[:, :, at], out_ref.at[0, :, :, at], sems.at[index])
-        copy.start()
-        copies.append(copy)
-    for copy in copies:
-        copy.wait()
+
+    @pl.when(is_press)
+    def _():
+        lax.fori_loop(0, tiles, press, half_turn(field[0, 0:32, :]), unroll=16)
+
+    @pl.when(jnp.logical_not(is_press))
+    def _():
+        start = half_turn(field[0, 0:32, :]), half_turn(rock[side + 1, own_rows, :])
+        lax.fori_loop(0, tiles, heat, start, unroll=16)
 
 
 def paired_body(states, coupled, facies, injectors, producers, perm_table, cond_table):
@@ -1155,22 +1155,19 @@
         name="send",
     )(boundary, rim)
     boundary = held(lax.ppermute(boundary, "ba", swap))
-    received, edge = pl.pallas_call(
+    fresh, edge = pl.pallas_call(
         faces_kernel,
-        out_shape=[jax.ShapeDtypeStruct(coupled.shape, f32), in_vmem((2, 32, LANES))],
+        out_shape=[in_vmem(coupled.shape[1:]), in_vmem((2, 32, LANES))],
         in_specs=[SM] + [VM] * 4,
-        out_specs=[HB, VM],
+        out_specs=[VM] * 2,
         scratch_shapes=[
             pltpu.VMEM((tiles + 1, rows + 8, LANES), f32),
             pltpu.VMEM((4, groups, LANES), f32),
-            pltpu.VMEM(coupled.shape[1:], f32),
-            pltpu.SemaphoreType.DMA((PARTS,)),
         ],
-        compiler_params=params(8),
+        compiler_params=params(5),
         cost_estimate=cost(6),
         name="faces",
     )(place, own, other, rim, cells[2])
-    received = pltpu.with_memory_space_constraint(received, pltpu.HBM)
     stepped, _, received = pl.pallas_call(
         finish_kernel,
         out_shape=[
@@ -1178,19 +1175,19 @@
             in_vmem(field),
             jax.ShapeDtypeStruct(coupled.shape, f32),
         ],
-        in_specs=[SM] + [VM] * 2 + [HB] + [VM] * 7,
+        in_specs=[SM] + [VM] * 10,
         out_specs=[HB, VM, HB],
         scratch_shapes=[
             pltpu.VMEM(field, f32),
             pltpu.VMEM(states.shape[1:], f32),
             pltpu.VMEM((32, LANES), f32),
-            pltpu.SemaphoreType.DMA((PARTS + 1,)),
+            pltpu.SemaphoreType.DMA((PARTS + 4,)),
         ],
-        input_output_aliases={2: 1, 3: 2},
+        input_output_aliases={2: 1},
         compiler_params=params(5),
         cost_estimate=cost(6),
         name="finish",
-    )(place, v1, v2, received, coeffs, force, cells[6], diag, boundary, edge, rim)
+    )(place, v1, v2, fresh, coeffs, force, cells[6], diag, boundary, edge, rim)
     return (stepped, received)
 
 

time: 37.7 us -> 36.6 us (0.971)
  Pallas kernels: 24.9 us -> 23.8 us
    pallas_call x1, Pallas kernels: 4.23 us -> 3.14 us  [paired_body(): pl.pallas_call(faces_kernel, out_shape=[in_vmem(coupled.shape[1:]), in_vm...]
  transfers between devices with their start and end apart: 8 -> 8, of which waited for: 1 -> 1; matrix products, arithmetic and copies ran while one was open for 0% -> 0% of each run, Pallas kernels for 51% -> 50%
where the time goes in v6:
time: 36.6 us; the launch traced here: 36.4 us
  Pallas kernels  23.8 us (65%)
  starting transfers between devices  10.8 us (30%)
  between operations  0.95 us (3%)
  waiting for transfers between devices  0.62 us (2%)
    pallas_call x1, Pallas kernels, paired_body(): pl.pallas_call(inner_kernel, out_shape=[in_vmem((6,) + field)] + [in_vmem...  7.08 us
    pallas_call x1, Pallas kernels, paired_body(): pl.pallas_call(main_kernel, out_shape=[in_vmem(field), in_vmem(field), in...  3.97 us
    pallas_call x1, Pallas kernels, paired_body(): pl.pallas_call(finish_kernel, out_shape=[jax.ShapeDtypeStruct(states.shap...  3.92 us
    ppermute x1, starting transfers between devices, paired_body(): from_left = held(lax.ppermute(to_right, 'aa', up))  3.15 us
    pallas_call x1, Pallas kernels, paired_body(): pl.pallas_call(faces_kernel, out_shape=[in_vmem(coupled.shape[1:]), in_vm...  3.14 us
    ppermute x1, starting transfers between devices, paired_body(): from_right = held(lax.ppermute(to_left, 'aa', down))  3.03 us
    pallas_call x1, Pallas kernels, paired_body(): pl.pallas_call(turn_kernel, out_shape=[in_vmem((32, 2 * groups * LANES)),...  2.41 us
    pallas_call x1, Pallas kernels, paired_body(): pl.pallas_call(corner_kernel, out_shape=in_vmem((2, 10 * wide)), in_specs...  1.73 us
  transfers between devices with their start and end apart: 8, of which 1 were waited for; matrix products, arithmetic and copies ran while one was open for 0% of the time, Pallas kernels for 50%

profile of v6, /device:TPU:9, one launch (start us, length us, event | category | flops | bytes accessed | tf_op | source)
XLA Modules:
  0.0 36.4 jit_solution(17587201752785537897)
XLA Ops:
  0.6 0.1 pad_add_fusion.where_ref
  0.7 0.0 copy-start
  0.7 0.0 copy-start.1
  0.7 0.0 copy-start.2
  0.7 0.0 copy-start.3
  0.7 0.0 copy-start.4
  0.7 1.7 %corner.1 = f32[2,2560]{1,0:T(2,128)S(1)} custom-call(s32[2]{0:T(128)S(1)} %pad_add_fusion.where_ref, f32[1,32,8192]{2,1,0:T(8,128)} %st.7, f32[1,3,32,8192]{3,2,1,0:T(8,128)} %cp.7, s32[1,32,8192]{2,1,0:T(8,128)} %fa.7, s32[1,32,8192]{2,1,0:T(8,128)} %ij.7, s32[1,32,8192]{2,1,0:T(8,128)} %pr.7), custom_call_target="tpu_custom_call" | custom-call | flops 1150000000 | bytes 3600000 | tf_op jit(solution)/shard_map/corner/pallas_call | solution.py:1049
  2.5 1.3 %collective-permute-start = (f32[2,2560]{1,0:T(2,128)S(1)}, f32[2,2560]{1,0:T(2,128)S(1)}, u32[]{:S(2)}, u32[]{:S(2)}) collective-permute-start(f32[2,2560]{1,0:T(2,128)S(1)} %corner.1), channel_id=1, source_target_pairs={{0,1},{1,0},{2,3},{3,2},{4,5},{5,4},{6,7},{7,6},{8,9},{9,8},{10,11... | collective-permute-start | bytes 61448 | tf_op jit(solution)/shard_map/ppermute | solution.py:1064
  3.8 0.0 copy-done
  3.8 0.0 copy-done.1
  3.8 0.0 copy-done.2
  3.8 0.0 copy-done.3
  3.8 0.1 copy-done.4
  3.9 0.8 %edges.1 = (f32[32,1792]{1,0:T(8,128)S(1)}, f32[32,1792]{1,0:T(8,128)S(1)}, f32[2,40960]{1,0:T(2,128)S(1)}) custom-call(s32[2]{0:T(128)S(1)} %pad_add_fusion.where_ref, f32[1,32,8192]{2,1,0:T(8,128)S(1)} %copy-done.1, f32[1,3,32,8192]{3,2,1,0:T(8,128)S(1)} %copy-done, s32[1,32,8192]{2,1,0:T(8,128)S(1)} %copy-done.2, s32[1,32,8192]{2,1,0:T(8,128)S(1)} %copy-done.3, ...), custom_call_target="tpu_custom_call" | custom-call | flops 2300000000 | bytes 7200000 | tf_op jit(solution)/shard_map/edges/pallas_call | solution.py:1065
  4.7 1.3 %collective-permute-start.3 = (f32[2,40960]{1,0:T(2,128)S(1)}, f32[2,40960]{1,0:T(2,128)S(1)}, u32[]{:S(2)}, u32[]{:S(2)}) collective-permute-start(f32[2,40960]{1,0:T(2,128)S(1)} %get-tuple-element.47), channel_id=1, source_target_pairs={{0,1},{1,0},{2,3},{3,2},{4,5},{5,4},{6,7},{7,6},{8,9},{9,8},{10,11... | collective-permute-start | bytes 983048 | tf_op jit(solution)/shard_map/ppermute | solution.py:1078
  6.0 0.0 collective-permute-done.corners
  6.0 0.0 copy-start.5
  6.0 0.0 copy-start.6
  6.1 3.1 %collective-permute-start.1 = (f32[32,1920]{1,0:T(8,128)S(1)}, f32[32,1920]{1,0:T(8,128)S(1)}, u32[]{:S(2)}, u32[]{:S(2)}) collective-permute-start(f32[32,1920]{1,0:T(8,128)S(1)} %get-tuple-element.45), channel_id=1, source_target_pairs={{0,2},{2,4},{4,6},{6,8},{8,10},{10,12},{12,14},{1,3},{3,5},{5,7},{... | collective-permute-start | bytes 737288 | tf_op jit(solution)/shard_map/ppermute | solution.py:1088
  9.2 3.0 %collective-permute-start.2 = (f32[32,1920]{1,0:T(8,128)S(1)}, f32[32,1920]{1,0:T(8,128)S(1)}, u32[]{:S(2)}, u32[]{:S(2)}) collective-permute-start(f32[32,1920]{1,0:T(8,128)S(1)} %get-tuple-element.46.corners), channel_id=1, source_target_pairs={{2,0},{4,2},{6,4},{8,6},{10,8},{12,10},{14,12},{3,1},{5,3},{7,5},{... | collective-permute-start | bytes 737288 | tf_op jit(solution)/shard_map/ppermute | solution.py:1089
  12.3 0.0 copy-done.5
  12.3 0.0 copy-done.6
  12.3 2.4 %turn.1 = (f32[32,4096]{1,0:T(8,128)S(1)}, f32[32,4224]{1,0:T(8,128)S(1)}, f32[32,256]{1,0:T(8,128)S(1)}, f32[70,40,128]{2,1,0:T(8,128)S(1)}, f32[70,40,128]{2,1...) custom-call(s32[2]{0:T(128)S(1)} %pad_add_fusion.where_ref, ...), custom_call_target="tpu_custom_call" | custom-call | flops 2875000064 | bytes 9000000 | tf_op jit(solution)/shard_map/turn/pallas_call | solution.py:1092
  14.7 0.3 collective-permute-start.4
  15.0 1.2 %collective-permute-start.5 = (f32[32,4224]{1,0:T(8,128)S(1)}, f32[32,4224]{1,0:T(8,128)S(1)}, u32[]{:S(2)}, u32[]{:S(2)}) collective-permute-start(f32[32,4224]{1,0:T(8,128)S(1)} %get-tuple-element.72), channel_id=1, source_target_pairs={{0,17},{1,16},{16,1},{17,0},{2,19},{3,18},{18,3},{19,2},{4,21},{5,... | collective-permute-start | bytes 1622024 | tf_op jit(solution)/shard_map/ppermute | solution.py:1108
  16.2 0.0 collective-permute-done.3.across
  16.2 7.1 %inner.1 = (f32[6,70,40,128]{3,2,1,0:T(8,128)S(1)}, f32[70,40,128]{2,1,0:T(8,128)S(1)}, f32[70,40,128]{2,1,0:T(8,128)S(1)}, f32[70,40,128]{2,1,0:T(8,128)S(1)}, ...) custom-call(s32[2]{0:T(128)S(1)} %pad_add_fusion.where_ref, ...), custom_call_target="tpu_custom_call", output_to_operand_aliasing={{3}: (9, {}), {4}: (10, {}), {5}: (11, {}), {6}: (12, {}), ... | custom-call | flops 11500000256 | bytes 36000000 | tf_op jit(solution)/shard_map/inner/pallas_call | solution.py:1110
  23.3 0.0 collective-permute-done.1.from_left.rest_0_
  23.3 0.0 collective-permute-done.2.from_right
  23.3 0.6 %plane.1 = f32[32,256]{1,0:T(8,128)S(1)} custom-call(s32[2]{0:T(128)S(1)} %pad_add_fusion.where_ref, f32[32,1920]{1,0:T(8,128)S(1)} %collective-permute-done.2.from_right, f32[32,256]{1,0:T(8,128)S(1)} %get-tuple-element.73.own_in, f32[32,1920]{1,0:T(8,128)S(1)} %collective-permute-done.1.from_left.rest_0_, ...), custom_call_target="tpu_custom_call", output_to_operand_aliasing={{}: (2, {})} | custom-call | flops 1150000000 | bytes 3600000 | tf_op jit(solution)/shard_map/plane/pallas_call | solution.py:1120
  23.9 0.1 collective-permute-start.6
  24.0 4.0 %main.1 = (f32[70,40,128]{2,1,0:T(8,128)S(1)}, f32[70,40,128]{2,1,0:T(8,128)S(1)}, f32[2,10752]{1,0:T(2,128)S(1)}, f32[6,70,40,128]{3,2,1,0:T(8,128)S(1)}, f32[7...) custom-call(s32[2]{0:T(128)S(1)} %pad_add_fusion.where_ref, ...), custom_call_target="tpu_custom_call", output_to_operand_aliasing={{3}: (5, {}), {4}: (6, {}), {5}: (7, {}), {6}: (8, {}), {7}... | custom-call | flops 11500000256 | bytes 36000000 | tf_op jit(solution)/shard_map/main/pallas_call | solution.py:1132
  28.0 0.0 collective-permute-done.6.own_rim.rim
  28.0 0.5 %collective-permute-start.7 = (f32[2,10752]{1,0:T(2,128)S(1)}, f32[2,10752]{1,0:T(2,128)S(1)}, u32[]{:S(2)}, u32[]{:S(2)}) collective-permute-start(f32[2,10752]{1,0:T(2,128)S(1)} %send.1), channel_id=1, source_target_pairs={{0,1},{1,0},{2,3},{3,2},{4,5},{5,4},{6,7},{7,6},{8,9},{9,8},{10,11... | collective-permute-start | bytes 258056 | tf_op jit(solution)/shard_map/ppermute | solution.py:1157
  28.5 0.0 collective-permute-done.4.own
  28.6 0.6 %collective-permute-done.5.other = f32[32,4224]{1,0:T(8,128)S(1)} collective-permute-done((f32[32,4224]{1,0:T(8,128)S(1)}, f32[32,4224]{1,0:T(8,128)S(1)}, u32[]{:S(2)}, u32[]{:S(2)}) %collective-permute-start.5) | collective-permute-done | bytes 540704 | tf_op jit(solution)/shard_map/ppermute | solution.py:1108
  29.1 3.1 %faces.1 = (f32[3,32,8192]{2,1,0:T(8,128)S(1)}, f32[2,32,128]{2,1,0:T(8,128)S(1)}) custom-call(s32[2]{0:T(128)S(1)} %pad_add_fusion.where_ref, f32[32,4096]{1,0:T(8,128)S(1)} %collective-permute-done.4.own, f32[32,4224]{1,0:T(8,128)S(1)} %collective-permute-done.5.other, f32[32,256]{1,0:T(8,128)S(1)} %collective-permute-done.6.own_rim.rim, ...), custom_call_target="tpu_custom_call" | custom-call | flops 6899999744 | bytes 21600000 | tf_op jit(solution)/shard_map/faces/pallas_call | solution.py:1158
  32.3 0.0 collective-permute-done.7.boundary
  32.3 3.9 %finish.1 = (f32[1,32,8192]{2,1,0:T(8,128)}, f32[70,40,128]{2,1,0:T(8,128)S(1)}, f32[1,3,32,8192]{3,2,1,0:T(8,128)}) custom-call(s32[2]{0:T(128)S(1)} %pad_add_fusion.where_ref, f32[70,40,128]{2,1,0:T(8,128)S(1)} %get-tuple-element.69.v1, f32[70,40,128]{2,1,0:T(8,128)S(1)} %get-tuple-element.70.v2_in, ...), custom_call_target="tpu_custom_call", output_to_operand_aliasing={{1}: (2, {})} | custom-call | flops 6899999744 | bytes 21600000 | tf_op jit(solution)/shard_map/finish/pallas_call | solution.py:1171
  (2 shorter events, 0.1 us)
Async XLA Ops:
  0.7 3.0 %copy-start = (f32[1,3,32,8192]{3,2,1,0:T(8,128)S(1)}, f32[1,3,32,8192]{3,2,1,0:T(8,128)}, u32[]{:S(2)}) copy-start(f32[1,3,32,8192]{3,2,1,0:T(8,128)} %cp.7) | copy-start | bytes 9437188
  0.7 3.0 %copy-start.1 = (f32[1,32,8192]{2,1,0:T(8,128)S(1)}, f32[1,32,8192]{2,1,0:T(8,128)}, u32[]{:S(2)}) copy-start(f32[1,32,8192]{2,1,0:T(8,128)} %st.7) | copy-start | bytes 3145732
  0.7 3.0 %copy-start.2 = (s32[1,32,8192]{2,1,0:T(8,128)S(1)}, s32[1,32,8192]{2,1,0:T(8,128)}, u32[]{:S(2)}) copy-start(s32[1,32,8192]{2,1,0:T(8,128)} %fa.7) | copy-start | bytes 3145732
  0.7 3.0 %copy-start.3 = (s32[1,32,8192]{2,1,0:T(8,128)S(1)}, s32[1,32,8192]{2,1,0:T(8,128)}, u32[]{:S(2)}) copy-start(s32[1,32,8192]{2,1,0:T(8,128)} %ij.7) | copy-start | bytes 3145732
  0.7 3.2 %copy-start.4 = (s32[1,32,8192]{2,1,0:T(8,128)S(1)}, s32[1,32,8192]{2,1,0:T(8,128)}, u32[]{:S(2)}) copy-start(s32[1,32,8192]{2,1,0:T(8,128)} %pr.7) | copy-start | bytes 3145732
  2.5 3.5 %collective-permute-start = (f32[2,2560]{1,0:T(2,128)S(1)}, f32[2,2560]{1,0:T(2,128)S(1)}, u32[]{:S(2)}, u32[]{:S(2)}) collective-permute-start(f32[2,2560]{1,0:T(2,128)S(1)} %corner.1), channel_id=1, source_target_pairs={{0,1},{1,0},{2,3},{3,2},{4,5},{5,4},{6,7},{7,6},{8,9},{9,8},{10,11... | collective-permute-start | bytes 61448 | tf_op jit(solution)/shard_map/ppermute | solution.py:1064
  4.7 11.5 %collective-permute-start.3 = (f32[2,40960]{1,0:T(2,128)S(1)}, f32[2,40960]{1,0:T(2,128)S(1)}, u32[]{:S(2)}, u32[]{:S(2)}) collective-permute-start(f32[2,40960]{1,0:T(2,128)S(1)} %get-tuple-element.47), channel_id=1, source_target_pairs={{0,1},{1,0},{2,3},{3,2},{4,5},{5,4},{6,7},{7,6},{8,9},{9,8},{10,11... | collective-permute-start | bytes 983048 | tf_op jit(solution)/shard_map/ppermute | solution.py:1078
  6.0 6.3 %copy-start.5 = (f32[6]{0:T(128)S(1)}, f32[6]{0:T(128)}, u32[]{:S(2)}) copy-start(f32[6]{0:T(128)} %perm_ref.5) | copy-start | bytes 76
  6.0 6.3 %copy-start.6 = (f32[6]{0:T(128)S(1)}, f32[6]{0:T(128)}, u32[]{:S(2)}) copy-start(f32[6]{0:T(128)} %cond_ref.5) | copy-start | bytes 76
  6.1 17.2 %collective-permute-start.1 = (f32[32,1920]{1,0:T(8,128)S(1)}, f32[32,1920]{1,0:T(8,128)S(1)}, u32[]{:S(2)}, u32[]{:S(2)}) collective-permute-start(f32[32,1920]{1,0:T(8,128)S(1)} %get-tuple-element.45), channel_id=1, source_target_pairs={{0,2},{2,4},{4,6},{6,8},{8,10},{10,12},{12,14},{1,3},{3,5},{5,7},{... | collective-permute-start | bytes 737288 | tf_op jit(solution)/shard_map/ppermute | solution.py:1088
  9.2 14.1 %collective-permute-start.2 = (f32[32,1920]{1,0:T(8,128)S(1)}, f32[32,1920]{1,0:T(8,128)S(1)}, u32[]{:S(2)}, u32[]{:S(2)}) collective-permute-start(f32[32,1920]{1,0:T(8,128)S(1)} %get-tuple-element.46.corners), channel_id=1, source_target_pairs={{2,0},{4,2},{6,4},{8,6},{10,8},{12,10},{14,12},{3,1},{5,3},{7,5},{... | collective-permute-start | bytes 737288 | tf_op jit(solution)/shard_map/ppermute | solution.py:1089
  14.7 13.9 %collective-permute-start.4 = (f32[32,4096]{1,0:T(8,128)S(1)}, f32[32,4096]{1,0:T(8,128)S(1)}, u32[]{:S(2)}, u32[]{:S(2)}) collective-permute-start(f32[32,4096]{1,0:T(8,128)S(1)} %get-tuple-element.71), channel_id=1, source_target_pairs={{0,16},{16,0},{1,17},{17,1},{2,18},{18,2},{3,19},{19,3},{4,20},{20... | collective-permute-start | bytes 1572872 | tf_op jit(solution)/shard_map/ppermute | solution.py:1109
  15.0 14.1 %collective-permute-start.5 = (f32[32,4224]{1,0:T(8,128)S(1)}, f32[32,4224]{1,0:T(8,128)S(1)}, u32[]{:S(2)}, u32[]{:S(2)}) collective-permute-start(f32[32,4224]{1,0:T(8,128)S(1)} %get-tuple-element.72), channel_id=1, source_target_pairs={{0,17},{1,16},{16,1},{17,0},{2,19},{3,18},{18,3},{19,2},{4,21},{5,... | collective-permute-start | bytes 1622024 | tf_op jit(solution)/shard_map/ppermute | solution.py:1108
  23.9 4.1 %collective-permute-start.6 = (f32[32,256]{1,0:T(8,128)S(1)}, f32[32,256]{1,0:T(8,128)S(1)}, u32[]{:S(2)}, u32[]{:S(2)}) collective-permute-start(f32[32,256]{1,0:T(8,128)S(1)} %plane.1), channel_id=1, source_target_pairs={{0,16},{16,0},{1,17},{17,1},{2,18},{18,2},{3,19},{19,3},{4,20},{20... | collective-permute-start | bytes 98312 | tf_op jit(solution)/shard_map/ppermute | solution.py:1130
  28.0 4.3 %collective-permute-start.7 = (f32[2,10752]{1,0:T(2,128)S(1)}, f32[2,10752]{1,0:T(2,128)S(1)}, u32[]{:S(2)}, u32[]{:S(2)}) collective-permute-start(f32[2,10752]{1,0:T(2,128)S(1)} %send.1), channel_id=1, source_target_pairs={{0,1},{1,0},{2,3},{3,2},{4,5},{5,4},{6,7},{7,6},{8,9},{9,8},{10,11... | collective-permute-start | bytes 258056 | tf_op jit(solution)/shard_map/ppermute | solution.py:1157
